TPU v7x, 32 devices: a whole 2x2x4 slice. The times are simulated.
32 devices in a mesh: dp: 32 (over z, y, x, core).
Axes of the slice: x: 2, y: 2, z: 4, core: 2. Of those that a mesh axis runs over, the one named last changes fastest.
Arguments:
- tokens: bfloat16 [32768, 768], P('dp'), may hold values from -6 to 6
- lengths: int32 [64, 5], P('dp'), may hold values from 0 to 509, as said below
- norm_gain: bfloat16 [768], P('dp'), may hold values from 0.5 to 1.5
- w_query: bfloat16 [768, 768], P('dp'), may hold values from -0.109375 to 0.109375
- w_key: bfloat16 [768, 768], P('dp'), may hold values from -0.109375 to 0.109375
- w_value: bfloat16 [768, 768], P('dp'), may hold values from -0.21875 to 0.21875
- w_out: bfloat16 [768, 768], P('dp'), may hold values from -0.625 to 0.625
- bias_table: bfloat16 [32, 12], replicated, may hold values from -4 to 4
- ffn_gain: bfloat16 [768], P('dp'), may hold values from 0.5 to 1.5
- w_in: bfloat16 [768, 3072], P('dp'), may hold values from -0.21875 to 0.21875
- w_ffn_out: bfloat16 [3072, 768], P('dp'), may hold values from -0.15625 to 0.15625
- cotangent: bfloat16 [32768, 768], P('dp'), may hold values from -6 to 6
Outputs:
- output: bfloat16 [32768, 768], P('dp')
- grad_tokens: float32 [32768, 768], P('dp')
- grad_norm_gain: float32 [768], P('dp')
- grad_query: float32 [768, 768], P('dp')
- grad_key: float32 [768, 768], P('dp')
- grad_value: float32 [768, 768], P('dp')
- grad_out: float32 [768, 768], P('dp')
- grad_bias_table: float32 [32, 12], replicated
- grad_ffn_gain: float32 [768], P('dp')
- grad_in: float32 [768, 3072], P('dp')
- grad_ffn_out: float32 [3072, 768], P('dp')
Inputs may be any that keep to these rules, and one draw needn't show every extreme that they name: Column 0 of a row is its count of padding positions, which stand at the row's end; columns 1 to 4 are the lengths of its pairs in order, each 1 or more; a row's entries sum to 512. Some row has 24 padding positions and some row none; some row has a pair of 509 positions.
All inputs are finite; a program needn't handle non-finite values.
Results may differ from a plain program's by a relative error of at most 0.013.
The roundings to bfloat16 on the way count: a program that leaves them out, or rounds other values in their place, can miss the bound.
Values may be sent and summed in bfloat16 or wider, within the bound.
A program may use at most 192 MiB of HBM per device.

v0:
```python
from functools import partial

import jax
import jax.numpy as jnp
from jax import lax
from jax.sharding import PartitionSpec as P

D = 768
H = 12
DH = 64
NB = 32
SEQ = 512


EPSILON = 1e-06
CUTOFFS = (12, 16, 23, 32, 46, 64, 91)


def bucket_index(length):
    positions = jnp.arange(length, dtype=jnp.int32)
    offsets = positions[None, :] - positions[:, None]
    distance = jnp.abs(offsets)
    coarse = jnp.full_like(distance, 8)
    for cutoff in CUTOFFS:
        coarse = coarse + (distance >= cutoff).astype(jnp.int32)
    return jnp.where(distance < 8, distance, coarse) + jnp.where(offsets > 0, 16, 0)


def segment_ids(lengths, length):
    seg_ends = jnp.cumsum(lengths[:, 1:], axis=1)
    positions = jnp.arange(length, dtype=jnp.int32)
    return jnp.sum((positions[None, :, None] >= seg_ends[:, None, :]).astype(jnp.int32), axis=2)


def rms_norm(values, gains):
    inv_rms = lax.rsqrt(jnp.mean(values * values, axis=-1, keepdims=True) + EPSILON)
    return values * inv_rms * gains


def project(left, right):
    return jnp.dot(left, right, preferred_element_type=jnp.float32)


def project_back(left, right):
    return jnp.einsum("te,de->td", left, right, preferred_element_type=jnp.float32)


def weight_grad(left, right):
    return jnp.einsum("te,td->ed", left, right, preferred_element_type=jnp.float32)


def per_device(
    tokens,
    lengths,
    norm_gain,
    w_query,
    w_key,
    w_value,
    w_out,
    bias_table,
    ffn_gain,
    w_in,
    w_ffn_out,
    cotangent,
):
    row_count = tokens.shape[0] // SEQ
    gain_one, full_query, full_key, full_value, full_out = (
        lax.all_gather(norm_gain, "dp", axis=0, tiled=True),
        lax.all_gather(w_query, "dp", axis=0, tiled=True),
        lax.all_gather(w_key, "dp", axis=0, tiled=True),
        lax.all_gather(w_value, "dp", axis=0, tiled=True),
        lax.all_gather(w_out, "dp", axis=0, tiled=True),
    )
    bucket = bucket_index(SEQ).reshape(1, SEQ * SEQ)
    onehot_flat = (bucket == jnp.arange(NB, dtype=jnp.int32)[:, None]).astype(jnp.bfloat16)
    rel_bias = jnp.dot(
        jnp.transpose(bias_table), onehot_flat, preferred_element_type=jnp.float32
    ).reshape(H, SEQ, SEQ)
    onehot = onehot_flat.reshape(NB, SEQ, SEQ)
    seg_all = segment_ids(lengths, SEQ)
    inputs = tokens.astype(jnp.float32)
    normed_one = rms_norm(inputs, gain_one.astype(jnp.float32)).astype(jnp.bfloat16)
    query_proj = project(normed_one, full_query).astype(jnp.bfloat16).reshape(row_count, SEQ, H, DH)
    key_proj = project(normed_one, full_key).astype(jnp.bfloat16).reshape(row_count, SEQ, H, DH)
    value_proj = project(normed_one, full_value).astype(jnp.bfloat16).reshape(row_count, SEQ, H, DH)

    def scores_of(query_row, key_row, seg_row):
        raw_scores = (
            jnp.einsum("ihd,jhd->hij", query_row, key_row, preferred_element_type=jnp.float32)
            + rel_bias
        )
        same_seg = seg_row[:, None] == seg_row[None, :]
        return jnp.where(same_seg[None], raw_scores, -1e30)

    def attend(row_items):
        query_row, key_row, value_row, seg_row = row_items
        scores = scores_of(query_row, key_row, seg_row)
        row_peak = jnp.max(scores, axis=2, keepdims=True)
        log_total = row_peak + jnp.log(jnp.sum(jnp.exp(scores - row_peak), axis=2, keepdims=True))
        probs_low = jnp.exp(scores - log_total).astype(jnp.bfloat16)
        attn_row = jnp.einsum(
            "hij,jhd->ihd", probs_low, value_row, preferred_element_type=jnp.float32
        )
        return (attn_row.astype(jnp.bfloat16), log_total)

    attn_mix, log_totals = lax.map(attend, (query_proj, key_proj, value_proj, seg_all))
    attn_mix = attn_mix.reshape(-1, D)
    residual = inputs + project(attn_mix, full_out)
    gain_two, full_in, full_ffn = (
        lax.all_gather(ffn_gain, "dp", axis=0, tiled=True),
        lax.all_gather(w_in, "dp", axis=0, tiled=True),
        lax.all_gather(w_ffn_out, "dp", axis=0, tiled=True),
    )
    normed_two = rms_norm(residual, gain_two.astype(jnp.float32)).astype(jnp.bfloat16)
    ffn_inner = project(normed_two, full_in)
    ffn_act = jax.nn.gelu(ffn_inner, approximate=False).astype(jnp.bfloat16)
    output = (residual + project(ffn_act, full_ffn)).astype(jnp.bfloat16)
    grad_output = cotangent.astype(jnp.float32)
    grad_ffn = weight_grad(ffn_act, cotangent)
    grad_act = project_back(cotangent, full_ffn)
    gelu_value, gelu_pull = jax.vjp(partial(jax.nn.gelu, approximate=False), ffn_inner)
    grad_inner = gelu_pull(grad_act)[0].astype(jnp.bfloat16)
    grad_wide = weight_grad(normed_two, grad_inner)
    grad_normed_two = project_back(grad_inner, full_in)
    norm_value, norm_pull = jax.vjp(rms_norm, residual, gain_two.astype(jnp.float32))
    grad_res_norm, grad_gain_two = norm_pull(grad_normed_two)
    grad_residual = grad_output + grad_res_norm
    ffn_sums = (
        lax.psum_scatter(grad_gain_two, "dp", scatter_dimension=0, tiled=True),
        lax.psum_scatter(grad_wide, "dp", scatter_dimension=0, tiled=True),
        lax.psum_scatter(grad_ffn, "dp", scatter_dimension=0, tiled=True),
    )
    grad_attn = grad_residual.astype(jnp.bfloat16)
    grad_proj_out = weight_grad(attn_mix, grad_attn)
    grad_mix = project_back(grad_attn, full_out).astype(jnp.bfloat16).reshape(row_count, SEQ, H, DH)

    def attend_back(table_sum, row_items):
        query_row, key_row, value_row, seg_row, log_total, grad_row = row_items
        scores = scores_of(query_row, key_row, seg_row)
        probabilities = jnp.exp(scores - log_total)
        grad_values = jnp.einsum(
            "hij,ihd->jhd",
            probabilities.astype(jnp.bfloat16),
            grad_row,
            preferred_element_type=jnp.float32,
        )
        grad_probs = jnp.einsum(
            "ihd,jhd->hij", grad_row, value_row, preferred_element_type=jnp.float32
        )
        inner_sum = jnp.sum(probabilities * grad_probs, axis=2, keepdims=True)
        grad_scores = (probabilities * (grad_probs - inner_sum)).astype(jnp.bfloat16)
        grad_queries = jnp.einsum(
            "hij,jhd->ihd", grad_scores, key_row, preferred_element_type=jnp.float32
        )
        grad_keys = jnp.einsum(
            "hij,ihd->jhd", grad_scores, query_row, preferred_element_type=jnp.float32
        )
        table_sum = table_sum + jnp.einsum(
            "hij,bij->bh", grad_scores, onehot, preferred_element_type=jnp.float32
        )
        return (
            table_sum,
            (
                grad_queries.astype(jnp.bfloat16),
                grad_keys.astype(jnp.bfloat16),
                grad_values.astype(jnp.bfloat16),
            ),
        )

    table_start = jnp.zeros((NB, H), jnp.float32)
    table_sum, grad_heads = lax.scan(
        attend_back, table_start, (query_proj, key_proj, value_proj, seg_all, log_totals, grad_mix)
    )
    grad_queries = grad_heads[0].reshape(-1, D)
    grad_keys = grad_heads[1].reshape(-1, D)
    grad_values = grad_heads[2].reshape(-1, D)
    grad_proj_query = weight_grad(normed_one, grad_queries)
    grad_proj_key = weight_grad(normed_one, grad_keys)
    grad_proj_value = weight_grad(normed_one, grad_values)
    grad_normed_one = (
        project_back(grad_queries, full_query)
        + project_back(grad_keys, full_key)
        + project_back(grad_values, full_value)
    )
    first_value, first_pull = jax.vjp(rms_norm, inputs, gain_one.astype(jnp.float32))
    grad_in_norm, grad_gain_one = first_pull(grad_normed_one)
    grad_tokens = grad_residual + grad_in_norm
    attn_sums = (
        lax.psum_scatter(grad_gain_one, "dp", scatter_dimension=0, tiled=True),
        lax.psum_scatter(grad_proj_query, "dp", scatter_dimension=0, tiled=True),
        lax.psum_scatter(grad_proj_key, "dp", scatter_dimension=0, tiled=True),
        lax.psum_scatter(grad_proj_value, "dp", scatter_dimension=0, tiled=True),
        lax.psum_scatter(grad_proj_out, "dp", scatter_dimension=0, tiled=True),
    )
    table_total = lax.psum(table_sum, "dp")
    return (
        output,
        grad_tokens,
        attn_sums[0],
        attn_sums[1],
        attn_sums[2],
        attn_sums[3],
        attn_sums[4],
        table_total,
        ffn_sums[0],
        ffn_sums[1],
        ffn_sums[2],
    )


def solution(mesh):
    return jax.shard_map(
        per_device,
        mesh=mesh,
        in_specs=(
            P("dp", None),
            P("dp", None),
            P("dp"),
            P("dp", None),
            P("dp", None),
            P("dp", None),
            P("dp", None),
            P(),
            P("dp"),
            P("dp", None),
            P("dp", None),
            P("dp", None),
        ),
        out_specs=(
            P("dp", None),
            P("dp", None),
            P("dp"),
            P("dp", None),
            P("dp", None),
            P("dp", None),
            P("dp", None),
            P(),
            P("dp"),
            P("dp", None),
            P("dp", None),
        ),
        check_vma=False,
    )
```

profile of v0, /device:TPU:0, one launch (start us, length us, event | category | flops | bytes accessed | tf_op | source)
XLA Modules:
  0.0 1156.0 jit_solution(4505106061038808593)
XLA Ops:
  16.5 42.2 %all-reduce.5 = (bf16[768]{0:T(1024)(128)(2,1)S(1)}, bf16[768]{0:T(1024)(128)(2,1)}) all-reduce(bf16[768]{0:T(1024)(128)(2,1)S(1)} %dynamic-update-slice, bf16[768]{0:T(1024)(128)(2,1)S(1)} %dynamic-update-slice.1), channel_id=1, replica_groups=mesh['dp'=32] {'dp'}, use_global_device_ids=true, to_apply=%add | all-reduce | flops 1536 | bytes 6144
  66.5 19.1 %copy.154 = f32[2,8,512,512]{3,2,1,0:T(8,128)} copy(f32[2,8,512,512]{3,1,2,0:T(8,128)S(1)} %bitcast.187) | data formatting | bytes 33554432
  85.6 10.7 slice.4
  96.3 12.8 %copy.123 = f32[12,512,512]{1,2,0:T(8,128)} copy(f32[12,512,512]{2,1,0:T(8,128)} %slice.4) | data formatting | bytes 25165824 | tf_op jit(solution)/shard_map/while | solution.py:106
  133.4 46.1 %all-gather.11.cloned.1.call-done = bf16[768,768]{1,0:T(8,128)(2,1)} async-done(((bf16[24,768]{1,0:T(8,128)(2,1)}), bf16[768,768]{1,0:T(8,128)(2,1)}) %all-gather.11.cloned.1.call-update) | async-done | bytes 1179664 | tf_op jit(solution)/shard_map/all_gather | solution.py:70
  190.6 23.8 %while.29 = (s32[]{:T(128)}, bf16[2,512,12,64]{1,3,2,0:T(8,128)(2,1)}, f32[2,12,512,1]{2,1,3,0:T(8,128)}, bf16[2,512,12,64]{1,3,2,0:T(8,128)(2,1)}, s32[2,512]{1...) while((s32[]{:T(128)}, ...), condition=%wide.region_6.7_spmd, body=%wide.region_3.6_spmd.sunk | while | flops 827975680 | bytes 60514940 | solution.py:106
  203.0 6.1 fusion.157
  219.1 16.2 %all-gather.13.cloned.1.call-done = bf16[768,768]{1,0:T(8,128)(2,1)} async-done(((bf16[24,768]{1,0:T(8,128)(2,1)}), bf16[768,768]{1,0:T(8,128)(2,1)}) %all-gather.13.cloned.1.call-update) | async-done | bytes 1179664 | tf_op jit(solution)/shard_map/all_gather | solution.py:72
  240.8 59.8 %all-gather.15.cloned.1.call-done = bf16[768,3072]{1,0:T(8,128)(2,1)} async-done(((bf16[24,3072]{1,0:T(8,128)(2,1)}), bf16[768,3072]{1,0:T(8,128)(2,1)}) %all-gather.15.cloned.1.call-update) | async-done | bytes 4718608 | tf_op jit(solution)/shard_map/all_gather | solution.py:111
  300.6 37.4 %multiply_convert_fusion.1 = (bf16[1024,3072]{1,0:T(8,128)(2,1)}, f32[1024,3072]{1,0:T(8,128)}, f32[1024,3072]{1,0:T(8,128)}) fusion(bf16[768,3072]{1,0:T(8,128)(2,1)} %all-gather.15.cloned.1.call-done, f32[1024,768]{0,1:T(8,128)} %get-tuple-element.363, f32[768]{0:T(1024)S(1)} %convert_element_type.168, f32[1024]{0:T(1024)S(1)} %fusion.91), kind=kOutput, calls=%fused_computation.70 | convolution fusion | flops 5038669824 | bytes 39328768 | tf_op jit(solution)/shard_map/dot_general | solution.py:41
  338.1 27.8 %all-gather.17.cloned.1.call-done = bf16[3072,768]{1,0:T(8,128)(2,1)} async-done(((bf16[96,768]{1,0:T(8,128)(2,1)}), bf16[3072,768]{1,0:T(8,128)(2,1)}) %all-gather.17.cloned.1.call-update) | async-done | bytes 4718608 | tf_op jit(solution)/shard_map/all_gather | solution.py:112
  365.9 17.5 %add_convert_fusion = bf16[1024,3072]{1,0:T(8,128)(2,1)} fusion(f32[1024,3072]{1,0:T(8,128)} %get-tuple-element.357, f32[1024,3072]{1,0:T(8,128)} %get-tuple-element.364, bf16[1024,768]{1,0:T(8,128)(2,1)} %param.27, bf16[3072,768]{1,0:T(8,128)(2,1)} %all-gather.17.cloned.1.call-done), kind=kOutput, calls=%fused_computation.69 | convolution fusion | flops 4875878400 | bytes 37748736 | tf_op jit(solution)/shard_map/te,de->td/dot_general | solution.py:45
  383.4 10.1 multiply_reduce_fusion.1
  417.1 134.4 %while.30 = (s32[]{:T(128)}, f32[32,12]{0,1:T(8,128)S(1)}, bf16[2,512,12,64]{1,3,2,0:T(8,128)(2,1)}, bf16[2,512,12,64]{1,3,2,0:T(8,128)(2,1)}, bf16[2,512,12,64]...) while((s32[]{:T(128)}, f32[32,12]{0,1:T(8,128)S(1)}, ...), condition=%wide.region_11.12_spmd.clone, body=%wide.region_9.11_spmd.clone.sunk | while | flops 2261117696 | bytes 303413984 | solution.py:171
  417.1 9.0 fusion.169
  426.4 11.1 multiply_reduce_fusion.5
  442.0 9.6 multiply_convert_fusion.6
  451.6 14.6 %copy.160 = bf16[12,512,512]{2,0,1:T(8,128)(2,1)} copy(bf16[12,512,512]{1,2,0:T(8,128)(2,1)} %multiply_convert_fusion.6) | data formatting | bytes 12582912 | tf_op jit(solution)/shard_map/while/body/eval_jaxpr/convert_element_type | solution.py:151
  466.2 7.0 fusion.170
  484.4 9.0 fusion.169
  493.7 10.8 multiply_reduce_fusion.5
  509.0 9.6 multiply_convert_fusion.6
  518.6 14.6 %copy.160 = bf16[12,512,512]{2,0,1:T(8,128)(2,1)} copy(bf16[12,512,512]{1,2,0:T(8,128)(2,1)} %multiply_convert_fusion.6) | data formatting | bytes 12582912 | tf_op jit(solution)/shard_map/while/body/eval_jaxpr/convert_element_type | solution.py:151
  533.2 7.0 fusion.170
  574.3 10.5 fusion.92
  586.2 10.5 fusion.105
  606.5 40.1 %all-reduce.4 = (f32[768]{0:T(1024)S(1)}, f32[32,12]{0,1:T(8,128)}, f32[768]{0:T(1024)S(1)}) all-reduce(f32[768]{0:T(1024)S(1)} %get-tuple-element.305, f32[32,12]{0,1:T(8,128)S(1)} %get-tuple-element.129, f32[768]{0:T(1024)S(1)} %copy-done.47), channel_id=2, replica_groups=mesh['dp'=32] {'dp'}, use_global_device_ids=true, to_apply=%region_14.15.clone | all-reduce | flops 1920 | bytes 15360
  656.8 9.6 add_convert_fusion.1
  668.9 92.3 %reduce-scatter.7.cloned.1.call-done = f32[24,768]{1,0:T(8,128)} async-done(((f32[768,768]{1,0:T(8,128)}), f32[24,768]{1,0:T(8,128)}) %reduce-scatter.7.cloned.1.call-update) | async-done | bytes 73744 | tf_op jit(solution)/shard_map/reduce_scatter | solution.py:190
  761.3 104.6 %reduce-scatter.9.cloned.1.call-done = f32[24,768]{1,0:T(8,128)} async-done(((f32[768,768]{1,0:T(8,128)}), f32[24,768]{1,0:T(8,128)}) %reduce-scatter.9.cloned.1.call-update) | async-done | bytes 73744 | tf_op jit(solution)/shard_map/reduce_scatter | solution.py:191
  865.9 141.0 %reduce-scatter.15.cloned.1.call-done = f32[24,3072]{1,0:T(8,128)} async-done(((f32[768,3072]{1,0:T(8,128)}), f32[24,3072]{1,0:T(8,128)}) %reduce-scatter.15.cloned.1.call-update) | async-done | bytes 294928 | tf_op jit(solution)/shard_map/reduce_scatter | solution.py:130
  1006.9 141.9 %reduce-scatter.17.cloned.1.call-done = f32[96,768]{1,0:T(8,128)} async-done(((f32[3072,768]{1,0:T(8,128)}), f32[96,768]{1,0:T(8,128)}) %reduce-scatter.17.cloned.1.call-update) | async-done | bytes 294928 | tf_op jit(solution)/shard_map/reduce_scatter | solution.py:131
  (278 shorter events, 181.3 us)
Async XLA Ops:
  7.2 54.2 %copy-start = (bf16[32,12]{0,1:T(8,128)(2,1)S(1)}, bf16[32,12]{0,1:T(8,128)(2,1)}, u32[]{:S(2)}) copy-start(bf16[32,12]{0,1:T(8,128)(2,1)} %param.23) | copy-start | bytes 2308
  7.2 104.1 %all-gather.7.cloned.1.call-start = ((), (), s32[]{:S(2)}) async-start(), calls=%async_computation.6 | async-start | bytes 1216512 | tf_op jit(solution)/shard_map/all_gather | solution.py:71
  7.9 115.7 %all-gather.9.cloned.1.call-start = ((), (), s32[]{:S(2)}) async-start(), calls=%async_computation.7 | async-start | bytes 1216512 | tf_op jit(solution)/shard_map/all_gather | solution.py:69
  8.7 170.8 %all-gather.11.cloned.1.call-start = ((), (), s32[]{:S(2)}) async-start(), calls=%async_computation.8 | async-start | bytes 1216512 | tf_op jit(solution)/shard_map/all_gather | solution.py:70
  9.4 225.9 %all-gather.13.cloned.1.call-start = ((), (), s32[]{:S(2)}) async-start(), calls=%async_computation.9 | async-start | bytes 1216512 | tf_op jit(solution)/shard_map/all_gather | solution.py:72
  10.0 290.7 %all-gather.15.cloned.1.call-start = ((), (), s32[]{:S(2)}) async-start(), calls=%async_computation.10 | async-start | bytes 4866048 | tf_op jit(solution)/shard_map/all_gather | solution.py:111
  10.6 355.3 %all-gather.17.cloned.1.call-start = ((), (), s32[]{:S(2)}) async-start(), calls=%async_computation.11 | async-start | bytes 4866048 | tf_op jit(solution)/shard_map/all_gather | solution.py:112
  11.2 657.8 %reduce-scatter.13.cloned.1.call-start = ((), (), s32[]{:S(2)}) async-start(), calls=%async_computation.15 | async-start | bytes 2433024 | tf_op jit(solution)/shard_map/reduce_scatter | solution.py:193
  15.6 44.9 %copy-start.9 = (bf16[1024,768]{0,1:T(8,128)(2,1)}, bf16[1024,768]{0,1:T(8,128)(2,1)S(1)}, u32[]{:S(2)}) copy-start(bf16[1024,768]{0,1:T(8,128)(2,1)S(1)} %copy.116) | copy-start | bytes 4718596
  16.0 44.6 %copy-start.40 = (f32[1024]{0:T(1024)}, f32[1024]{0:T(1024)S(1)}, u32[]{:S(2)}) copy-start(f32[1024]{0:T(1024)S(1)} %fusion.74) | copy-start | bytes 12292
  16.0 163.5 %copy-start.36 = (f32[1024]{0:T(1024)}, f32[1024]{0:T(1024)S(1)}, u32[]{:S(2)}) copy-start(f32[1024]{0:T(1024)S(1)} %fusion.90) | copy-start | bytes 12292
  58.7 120.8 %copy-start.38 = (f32[768]{0:T(1024)}, f32[768]{0:T(1024)S(1)}, u32[]{:S(2)}) copy-start(f32[768]{0:T(1024)S(1)} %convert_element_type.155) | copy-start | bytes 9220
  96.3 13.2 %copy-start.48 = (bf16[768]{0:T(1024)(128)(2,1)S(1)}, bf16[768]{0:T(1024)(128)(2,1)}, u32[]{:S(2)}) copy-start(bf16[768]{0:T(1024)(128)(2,1)} %get-tuple-element.353) | copy-start | bytes 4612
  96.3 13.2 %copy-start.24 = (bf16[1024,768]{1,0:T(8,128)(2,1)S(1)}, bf16[1024,768]{1,0:T(8,128)(2,1)}, u32[]{:S(2)}) copy-start(bf16[1024,768]{1,0:T(8,128)(2,1)} %param.27) | copy-start | bytes 4718596
  109.5 284.0 %copy-start.42 = (f32[768]{0:T(1024)}, f32[768]{0:T(1024)S(1)}, u32[]{:S(2)}) copy-start(f32[768]{0:T(1024)S(1)} %convert_element_type.168) | copy-start | bytes 9220
  240.8 152.7 %copy-start.44 = (f32[1024]{0:T(1024)}, f32[1024]{0:T(1024)S(1)}, u32[]{:S(2)}) copy-start(f32[1024]{0:T(1024)S(1)} %fusion.91) | copy-start | bytes 12292
  365.9 17.5 %copy-start.22 = (f32[1024,768]{0,1:T(8,128)S(1)}, f32[1024,768]{0,1:T(8,128)}, u32[]{:S(2)}) copy-start(f32[1024,768]{0,1:T(8,128)} %get-tuple-element.363) | copy-start | bytes 9437188
  398.8 270.1 %reduce-scatter.11.cloned.1.call-start = ((), (), s32[]{:S(2)}) async-start(), calls=%async_computation.14 | async-start | bytes 2433024 | tf_op jit(solution)/shard_map/reduce_scatter | solution.py:192
  451.6 14.6 %copy-start.32 = (s32[512,512]{1,0:T(8,128)S(1)}, s32[512,512]{1,0:T(8,128)}, u32[]{:S(2)}) copy-start(s32[512,512]{1,0:T(8,128)} %get-tuple-element.576) | copy-start | bytes 3145732 | tf_op jit(solution)/shard_map/while
  451.6 21.7 %slice-start = ((s8[6291456]{0:T(1024)(128)(4,1)}), s8[2097152]{0:T(1024)(128)(4,1)S(1)}, s32[]{:S(2)}) async-start(s8[6291456]{0:T(1024)(128)(4,1)} %bitcast.183), calls=%async_computation.18 | async-start | bytes 4194304 | tf_op jit(solution)/shard_map/while
  466.2 15.2 %slice-start.2 = ((s8[12582912]{0:T(1024)(128)(4,1)}), s8[4194304]{0:T(1024)(128)(4,1)S(1)}, s32[]{:S(2)}) async-start(s8[12582912]{0:T(1024)(128)(4,1)} %bitcast.185), calls=%async_computation.20 | async-start | bytes 8388608 | tf_op jit(solution)/shard_map/while
  466.2 15.2 %slice-start.3 = ((s8[12582912]{0:T(1024)(128)(4,1)}), s8[4194304]{0:T(1024)(128)(4,1)S(1)}, s32[]{:S(2)}) async-start(s8[12582912]{0:T(1024)(128)(4,1)} %bitcast.185), calls=%async_computation.21 | async-start | bytes 8388608 | tf_op jit(solution)/shard_map/while
  518.6 14.6 %copy-start.32 = (s32[512,512]{1,0:T(8,128)S(1)}, s32[512,512]{1,0:T(8,128)}, u32[]{:S(2)}) copy-start(s32[512,512]{1,0:T(8,128)} %get-tuple-element.576) | copy-start | bytes 3145732 | tf_op jit(solution)/shard_map/while
  518.6 21.6 %slice-start = ((s8[6291456]{0:T(1024)(128)(4,1)}), s8[2097152]{0:T(1024)(128)(4,1)S(1)}, s32[]{:S(2)}) async-start(s8[6291456]{0:T(1024)(128)(4,1)} %bitcast.183), calls=%async_computation.18 | async-start | bytes 4194304 | tf_op jit(solution)/shard_map/while
  533.2 15.2 %slice-start.2 = ((s8[12582912]{0:T(1024)(128)(4,1)}), s8[4194304]{0:T(1024)(128)(4,1)S(1)}, s32[]{:S(2)}) async-start(s8[12582912]{0:T(1024)(128)(4,1)} %bitcast.185), calls=%async_computation.20 | async-start | bytes 8388608 | tf_op jit(solution)/shard_map/while
  533.2 15.2 %slice-start.3 = ((s8[12582912]{0:T(1024)(128)(4,1)}), s8[4194304]{0:T(1024)(128)(4,1)S(1)}, s32[]{:S(2)}) async-start(s8[12582912]{0:T(1024)(128)(4,1)} %bitcast.185), calls=%async_computation.21 | async-start | bytes 8388608 | tf_op jit(solution)/shard_map/while
  559.2 202.1 %reduce-scatter.7.cloned.1.call-start = ((), (), s32[]{:S(2)}) async-start(), calls=%async_computation.12 | async-start | bytes 2433024 | tf_op jit(solution)/shard_map/reduce_scatter | solution.py:190
  566.6 299.3 %reduce-scatter.9.cloned.1.call-start = ((), (), s32[]{:S(2)}) async-start(), calls=%async_computation.13 | async-start | bytes 2433024 | tf_op jit(solution)/shard_map/reduce_scatter | solution.py:191
  574.2 432.8 %reduce-scatter.15.cloned.1.call-start = ((), (), s32[]{:S(2)}) async-start(), calls=%async_computation.16 | async-start | bytes 9732096 | tf_op jit(solution)/shard_map/reduce_scatter | solution.py:130
  584.8 564.1 %reduce-scatter.17.cloned.1.call-start = ((), (), s32[]{:S(2)}) async-start(), calls=%async_computation.17 | async-start | bytes 9732096 | tf_op jit(solution)/shard_map/reduce_scatter | solution.py:131
  602.7 45.0 %copy-start.41 = (f32[1024]{0:T(1024)S(1)}, f32[1024]{0:T(1024)}, u32[]{:S(2)}) copy-start(f32[1024]{0:T(1024)} %copy-done.40) | copy-start | bytes 12292
  656.8 492.1 %copy-start.1 = (bf16[32,12]{0,1:T(8,128)(2,1)S(1)}, bf16[32,12]{0,1:T(8,128)(2,1)}, u32[]{:S(2)}) copy-start(bf16[32,12]{0,1:T(8,128)(2,1)} %param.23) | copy-start | bytes 2308
  (58 other events, 256.8 us)
Sparse Core Ops, SparseCore 0:
  10.9 56.7 all-gather.6
  70.7 52.8 all-gather.8
  126.5 52.9 all-gather.10
  182.3 52.9 all-gather.12
  238.0 62.5 all-gather.14
  303.4 62.4 all-gather.16
  399.0 97.8 reduce-scatter.12
  559.3 98.0 reduce-scatter.10
  663.2 97.9 reduce-scatter.6
  767.8 98.0 reduce-scatter.8
  872.4 134.5 reduce-scatter.14
  1014.3 134.5 reduce-scatter.16
where the time goes:
time: 1160 us
  waiting for transfers between devices  635 us (55%)
  matrix products  232 us (20%)
  local copies, waits for them, and re-layouts  155 us (13%)
  blocking collectives  82.3 us (7%)
  other arithmetic  35.1 us (3%)
  between operations  14.9 us (1%)
    reduce_scatter x1, waiting for transfers between devices, per_device(): lax.psum_scatter(grad_ffn, 'dp', scatter_dimension=0, tiled=True)  142 us
    reduce_scatter x1, waiting for transfers between devices, per_device(): lax.psum_scatter(grad_wide, 'dp', scatter_dimension=0, tiled=True)  141 us
    reduce_scatter x1, waiting for transfers between devices, per_device(): lax.psum_scatter(grad_proj_key, 'dp', scatter_dimension=0, tiled=True)  105 us
    reduce_scatter x1, waiting for transfers between devices, per_device(): lax.psum_scatter(grad_proj_query, 'dp', scatter_dimension=0, tiled=True)  92.3 us
    unnamed x2, blocking collectives  82.3 us
    dot_general x6, matrix products, project(): return jnp.dot(left, right, preferred_element_type=jnp.float32)  64.5 us
    all_gather x1, waiting for transfers between devices, per_device(): lax.all_gather(w_in, 'dp', axis=0, tiled=True)  59.8 us
    unnamed x94, local copies, waits for them, and re-layouts  49.1 us
  transfers between devices with their start and end apart: 12, of which 9 were waited for; matrix products, arithmetic and copies ran while one was open for 32% of the time, Pallas kernels for 0%

commit v1 on v0

--- a/solution.py
+++ b/solution.py
@@ -4,6 +4,9 @@
 import jax.numpy as jnp
 from jax import lax
 from jax.sharding import PartitionSpec as P
+
+from jax.experimental import pallas as pl
+from jax.experimental.pallas import tpu as pltpu
 
 D = 768
 H = 12
@@ -47,6 +50,364 @@
 
 def weight_grad(left, right):
     return jnp.einsum("te,td->ed", left, right, preferred_element_type=jnp.float32)
+
+
+MESH_ID = pl.DeviceIdType.MESH
+RANKS = 32
+
+
+def place():
+    me = lax.axis_index("dp")
+    group = lax.axis_size("dp") // RANKS
+    rank, low = me // group, me % group
+    digits = dict(z=rank // 8, y=(rank // 4) % 2, x=(rank // 2) % 2, c=rank % 2)
+
+    def device(**changed):
+        d = {**digits, **changed}
+        return ((((d["z"] * 2 + d["y"]) * 2 + d["x"]) * 2 + d["c"]) * group + low,)
+
+    return digits, device
+
+
+def greet(digits, device):
+    barrier = pltpu.get_barrier_semaphore()
+    others = [device(z=(digits["z"] + step) % 4) for step in (1, 2, 3)]
+    others += [device(**{axis: 1 - digits[axis]}) for axis in "yxc"]
+    for other in others:
+        pl.semaphore_signal(barrier, inc=1, device_id=other, device_id_type=MESH_ID)
+    pl.semaphore_wait(barrier, len(others))
+
+
+def send(source, target, send_sem, recv_sem, device_id):
+    return pltpu.make_async_remote_copy(
+        src_ref=source,
+        dst_ref=target,
+        send_sem=send_sem,
+        recv_sem=recv_sem,
+        device_id=device_id,
+        device_id_type=MESH_ID,
+    )
+
+
+class Gather:
+    COPIES = 10
+
+    def __init__(self, block, full, own_sem, send_sems, recv_sems, order):
+        self.block, self.full, self.own_sem = block, full, own_sem
+        self.send_sems, self.recv_sems = send_sems, recv_sems
+        self.first, self.second = order
+        self.digits, self.device = place()
+        self.started = []
+
+    def part(self, **changed):
+        d = {**self.digits, **changed}
+        return self.full.at[:, d["y"], d["x"], d["c"]]
+
+    def one(self, z, **changed):
+        d = {**self.digits, **changed}
+        return self.full.at[z, d["y"], d["x"], d["c"]]
+
+    def go(self, slot, source, target, device_id):
+        copy = send(source, target, self.send_sems.at[slot], self.recv_sems.at[slot], device_id)
+        copy.start()
+        self.started.append(copy)
+
+    def arrived(self, slot, landing):
+        send(landing, landing, self.send_sems.at[slot], self.recv_sems.at[slot], self.device(c=1 - self.digits["c"])).wait_recv()
+
+    def start(self):
+        z = self.digits["z"]
+        own = pltpu.make_async_copy(self.block, self.one(z), self.own_sem)
+        own.start()
+        for step in (1, 2, 3):
+            self.go(step - 1, self.block, self.one(z), self.device(z=(z + step) % 4))
+        self.own = own
+
+    def spread_line(self):
+        z = self.digits["z"]
+        self.own.wait()
+        for step in (1, 2, 3):
+            self.arrived(step - 1, self.one((z - step + 4) % 4))
+        line = self.part()
+        self.go(3, line, line, self.device(**{self.first: 1 - self.digits[self.first]}))
+        self.go(4, line, line, self.device(**{self.second: 1 - self.digits[self.second]}))
+        self.go(5, line, line, self.device(c=1 - self.digits["c"]))
+
+    def spread_first(self):
+        line = self.part(**{self.first: 1 - self.digits[self.first]})
+        self.arrived(3, line)
+        self.go(6, line, line, self.device(**{self.second: 1 - self.digits[self.second]}))
+        self.go(7, line, line, self.device(c=1 - self.digits["c"]))
+
+    def spread_second(self):
+        other = {self.second: 1 - self.digits[self.second]}
+        for slot, line in ((4, self.part(**other)), (6, self.part(**other, **{self.first: 1 - self.digits[self.first]}))):
+            self.arrived(slot, line)
+            self.go(slot + 4 - (slot == 6), line, line, self.device(c=1 - self.digits["c"]))
+
+    def finish(self):
+        c = 1 - self.digits["c"]
+        a = {self.first: 1 - self.digits[self.first]}
+        b = {self.second: 1 - self.digits[self.second]}
+        for slot, line in ((5, self.part(c=c)), (7, self.part(c=c, **a)), (8, self.part(c=c, **b)), (9, self.part(c=c, **a, **b))):
+            self.arrived(slot, line)
+        for copy in self.started:
+            copy.wait_send()
+
+
+class Reduce:
+    COPIES = 8
+
+    def __init__(self, parts, from_core, from_first, from_second, from_line, send_sems, recv_sems, order):
+        self.parts = parts
+        self.from_core, self.from_first, self.from_second, self.from_line = from_core, from_first, from_second, from_line
+        self.send_sems, self.recv_sems = send_sems, recv_sems
+        self.first, self.second = order
+        self.digits, self.device = place()
+        self.started = []
+
+    def at(self, z, first, second, c):
+        d = {self.first: first, self.second: second}
+        return (z, d["y"], d["x"], c)
+
+    def go(self, slot, source, target, device_id):
+        copy = send(source, target, self.send_sems.at[slot], self.recv_sems.at[slot], device_id)
+        copy.start()
+        self.started.append(copy)
+
+    def arrived(self, slot, landing):
+        send(landing, landing, self.send_sems.at[slot], self.recv_sems.at[slot], self.device(c=1 - self.digits["c"])).wait_recv()
+
+    def add(self, place_of, received, count):
+        def body(i, carry):
+            index = place_of(i)
+            total = self.parts[index].astype(jnp.float32) + received(i).astype(jnp.float32)
+            self.parts[index] = total.astype(jnp.bfloat16)
+            return carry
+
+        lax.fori_loop(0, count, body, 0)
+
+    def half(self, first, c):
+        if self.first == "y":
+            return self.parts.at[:, first, :, c]
+        return self.parts.at[:, :, first, c]
+
+    def start(self):
+        d = self.digits
+        c = 1 - d["c"]
+        sibling = self.device(c=c)
+        self.go(0, self.half(1 - d[self.first], c), self.from_core.at[0], sibling)
+        self.go(1, self.half(d[self.first], c), self.from_core.at[1], sibling)
+
+    def core_far(self):
+        d = self.digits
+        self.arrived(0, self.from_core.at[0])
+        self.add(
+            lambda i: self.at(i // 2, 1 - d[self.first], i % 2, d["c"]), lambda i: self.from_core[0, i // 2, i % 2], 8
+        )
+        self.go(2, self.half(1 - d[self.first], d["c"]), self.from_first, self.device(**{self.first: 1 - d[self.first]}))
+
+    def core_near(self):
+        d = self.digits
+        self.arrived(1, self.from_core.at[1])
+        self.add(lambda i: self.at(i // 2, d[self.first], i % 2, d["c"]), lambda i: self.from_core[1, i // 2, i % 2], 8)
+
+    def first_axis(self):
+        d = self.digits
+        self.arrived(2, self.from_first)
+        far = 1 - d[self.second]
+        self.add(lambda i: self.at(i, d[self.first], far, d["c"]), lambda i: self.from_first[i, far], 4)
+        q = {self.first: d[self.first], self.second: far}
+        self.go(3, self.parts.at[:, q["y"], q["x"], d["c"]], self.from_second, self.device(**{self.second: far}))
+        near = d[self.second]
+        self.add(lambda i: self.at(i, d[self.first], near, d["c"]), lambda i: self.from_first[i, near], 4)
+
+    def second_axis(self):
+        d = self.digits
+        self.arrived(3, self.from_second)
+        self.add(lambda i: self.at(i, d[self.first], d[self.second], d["c"]), lambda i: self.from_second[i], 4)
+        for step in (1, 2, 3):
+            z = (d["z"] + step) % 4
+            source = self.parts.at[z, d["y"], d["x"], d["c"]]
+            self.go(3 + step, source, self.from_line.at[step - 1], self.device(z=z))
+
+    def finish(self, out_ref):
+        d = self.digits
+        total = self.parts[d["z"], d["y"], d["x"], d["c"]].astype(jnp.float32)
+        for step in (1, 2, 3):
+            self.arrived(3 + step, self.from_line.at[step - 1])
+            total = total + self.from_line[step - 1].astype(jnp.float32)
+        out_ref[...] = total
+        for copy in self.started:
+            copy.wait_send()
+
+
+ORDERS = ("xy", "yx")
+ANY = pl.BlockSpec(memory_space=pl.ANY)
+VMEM = pl.BlockSpec(memory_space=pltpu.VMEM)
+FULL = (4, 2, 2, 2)
+
+
+def halves(width):
+    return ((0, width // 2), (width // 2, width))
+
+
+def gather_kernel(count, *refs):
+    blocks, fulls = refs[:count], refs[count : 2 * count]
+    own_sems, send_sems, recv_sems = refs[2 * count :]
+    digits, device = place()
+    greet(digits, device)
+    pieces = [
+        Gather(blocks[i], fulls[i], own_sems.at[i], send_sems.at[i], recv_sems.at[i], ORDERS[i % 2]) for i in range(count)
+    ]
+    for stage in ("start", "spread_line", "spread_first", "spread_second", "finish"):
+        for piece in pieces:
+            getattr(piece, stage)()
+
+
+def inner_groups():
+    total = lax.axis_size("dp")
+    group = total // RANKS
+    return group, [list(range(i * group, (i + 1) * group)) for i in range(RANKS)]
+
+
+def widen(block):
+    group, groups = inner_groups()
+    if group == 1:
+        return block
+    return lax.all_gather(block, "dp", axis=0, tiled=True, axis_index_groups=groups)
+
+
+def narrow(block):
+    group, groups = inner_groups()
+    if group == 1:
+        return block
+    return lax.psum_scatter(block, "dp", scatter_dimension=0, tiled=True, axis_index_groups=groups)
+
+
+def gather_weights(norm_gain, ffn_gain, attn_weights, w_in, w_ffn_out):
+    gains = widen(jnp.stack([norm_gain, ffn_gain], axis=1))
+    gain_rows = jnp.zeros((16, 128), jnp.bfloat16).at[: 2, : gains.shape[0]].set(gains.T)
+    attn = widen(jnp.concatenate(attn_weights, axis=1))
+    wide = widen(w_in)
+    ffn = widen(w_ffn_out)
+    blocks = [gain_rows, gain_rows]
+    for block in (attn, wide, ffn):
+        blocks += [block[:, lo:hi] for lo, hi in halves(block.shape[1])]
+    blocks = blocks[1:]
+    count = len(blocks)
+    fulls = pl.pallas_call(
+        partial(gather_kernel, count),
+        out_shape=[jax.ShapeDtypeStruct(FULL + block.shape, block.dtype) for block in blocks],
+        in_specs=[ANY] * count,
+        out_specs=[ANY] * count,
+        scratch_shapes=[
+            pltpu.SemaphoreType.DMA((count,)),
+            pltpu.SemaphoreType.DMA((count, Gather.COPIES)),
+            pltpu.SemaphoreType.DMA((count, Gather.COPIES)),
+        ],
+        compiler_params=pltpu.CompilerParams(collective_id=1, has_side_effects=True),
+    )(*blocks)
+    gain_full = fulls[0].reshape(RANKS, 16, 128)[:, :2, : gains.shape[0]]
+    gain_one, gain_two = gain_full[:, 0].reshape(-1), gain_full[:, 1].reshape(-1)
+    whole = [jnp.concatenate([a.reshape(-1, a.shape[-1]), b.reshape(-1, b.shape[-1])], axis=1) for a, b in zip(fulls[1::2], fulls[2::2])]
+    return gain_one, gain_two, *whole
+
+
+def reduce_kernel(count, *refs):
+    parts, small, outs, small_out = refs[:count], refs[count], refs[count + 1 : 2 * count + 1], refs[2 * count + 1]
+    buffers = refs[2 * count + 2 : 6 * count + 2]
+    small_buffer, send_sems, recv_sems, small_send, small_recv = refs[6 * count + 2 :]
+    digits, device = place()
+    greet(digits, device)
+    pieces = [
+        Reduce(parts[i], *buffers[4 * i : 4 * i + 4], send_sems.at[i], recv_sems.at[i], ORDERS[i % 2]) for i in range(count)
+    ]
+    for stage in ("start", "core_far", "core_near", "first_axis", "second_axis"):
+        for piece in pieces:
+            getattr(piece, stage)()
+    small_sum(small, small_buffer, small_out, small_send, small_recv, digits, device)
+    for piece, out in zip(pieces, outs):
+        piece.finish(out)
+
+
+def small_sum(values, buffer, out, send_sems, recv_sems, digits, device):
+    out[...] = values[...]
+    copies = []
+    for slot, axis in enumerate("cxy"):
+        buffer[2 * slot] = out[...]
+        copy = send(
+            buffer.at[2 * slot],
+            buffer.at[2 * slot + 1],
+            send_sems.at[slot],
+            recv_sems.at[slot],
+            device(**{axis: 1 - digits[axis]}),
+        )
+        copy.start()
+        copies.append(copy)
+        copy.wait_recv()
+        out[...] = out[...] + buffer[2 * slot + 1]
+    z = digits["z"]
+    buffer[6 + z] = out[...]
+    line = []
+    for step in (1, 2, 3):
+        mine = buffer.at[6 + z]
+        copy = send(mine, mine, send_sems.at[2 + step], recv_sems.at[2 + step], device(z=(z + step) % 4))
+        copy.start()
+        line.append(copy)
+    for step in (1, 2, 3):
+        theirs = buffer.at[6 + (z - step + 4) % 4]
+        send(theirs, theirs, send_sems.at[2 + step], recv_sems.at[2 + step], device(z=(z + step) % 4)).wait_recv()
+    out[...] = (buffer[6] + buffer[7]) + (buffer[8] + buffer[9])
+    for copy in copies + line:
+        copy.wait_send()
+
+
+def reduce_grads(attn, wide, ffn, gain_one, gain_two, table_sum):
+    blocks = []
+    for block in (attn, wide, ffn):
+        blocks += [
+            block[:, lo:hi].astype(jnp.bfloat16).reshape(FULL + (-1, hi - lo)) for lo, hi in halves(block.shape[1])
+        ]
+    count = len(blocks)
+    small = jnp.concatenate([gain_one, gain_two, table_sum.reshape(-1)])
+    pad = -small.shape[0] % 1024
+    small = jnp.pad(small, (0, pad)).reshape(-1, 128)
+    buffers = []
+    for block in blocks:
+        one = block.shape[4:]
+        buffers += [
+            pltpu.VMEM((2, 4, 2) + one, jnp.bfloat16),
+            pltpu.VMEM((4, 2) + one, jnp.bfloat16),
+            pltpu.VMEM((4,) + one, jnp.bfloat16),
+            pltpu.VMEM((3,) + one, jnp.bfloat16),
+        ]
+    outs = pl.pallas_call(
+        partial(reduce_kernel, count),
+        out_shape=[jax.ShapeDtypeStruct(block.shape[4:], jnp.float32) for block in blocks]
+        + [jax.ShapeDtypeStruct(small.shape, jnp.float32)],
+        in_specs=[VMEM] * (count + 1),
+        out_specs=[VMEM] * (count + 1),
+        scratch_shapes=buffers
+        + [
+            pltpu.VMEM((10,) + small.shape, jnp.float32),
+            pltpu.SemaphoreType.DMA((count, Reduce.COPIES)),
+            pltpu.SemaphoreType.DMA((count, Reduce.COPIES)),
+            pltpu.SemaphoreType.DMA((6,)),
+            pltpu.SemaphoreType.DMA((6,)),
+        ],
+        compiler_params=pltpu.CompilerParams(collective_id=2, has_side_effects=True, vmem_limit_bytes=60 << 20),
+    )(*blocks, small)
+    sums = [narrow(jnp.concatenate(pair, axis=1)) for pair in zip(outs[0:count:2], outs[1:count:2])]
+    flat = outs[count].reshape(-1)
+    if inner_groups()[0] > 1:
+        flat = lax.psum(flat, "dp", axis_index_groups=inner_groups()[1])
+    each = D // lax.axis_size("dp")
+    start = lax.axis_index("dp") * each
+    gain_one_sum = lax.dynamic_slice(flat, (start,), (each,))
+    gain_two_sum = lax.dynamic_slice(flat, (D + start,), (each,))
+    table_total = flat[2 * D : 2 * D + NB * H].reshape(NB, H)
+    return *sums, gain_one_sum, gain_two_sum, table_total
 
 
 def per_device(
@@ -64,13 +425,10 @@
     cotangent,
 ):
     row_count = tokens.shape[0] // SEQ
-    gain_one, full_query, full_key, full_value, full_out = (
-        lax.all_gather(norm_gain, "dp", axis=0, tiled=True),
-        lax.all_gather(w_query, "dp", axis=0, tiled=True),
-        lax.all_gather(w_key, "dp", axis=0, tiled=True),
-        lax.all_gather(w_value, "dp", axis=0, tiled=True),
-        lax.all_gather(w_out, "dp", axis=0, tiled=True),
+    gain_one, gain_two, full_attn, full_in, full_ffn = gather_weights(
+        norm_gain, ffn_gain, (w_query, w_key, w_value, w_out), w_in, w_ffn_out
     )
+    full_query, full_key, full_value, full_out = jnp.split(full_attn, 4, axis=1)
     bucket = bucket_index(SEQ).reshape(1, SEQ * SEQ)
     onehot_flat = (bucket == jnp.arange(NB, dtype=jnp.int32)[:, None]).astype(jnp.bfloat16)
     rel_bias = jnp.dot(
@@ -106,11 +464,6 @@
     attn_mix, log_totals = lax.map(attend, (query_proj, key_proj, value_proj, seg_all))
     attn_mix = attn_mix.reshape(-1, D)
     residual = inputs + project(attn_mix, full_out)
-    gain_two, full_in, full_ffn = (
-        lax.all_gather(ffn_gain, "dp", axis=0, tiled=True),
-        lax.all_gather(w_in, "dp", axis=0, tiled=True),
-        lax.all_gather(w_ffn_out, "dp", axis=0, tiled=True),
-    )
     normed_two = rms_norm(residual, gain_two.astype(jnp.float32)).astype(jnp.bfloat16)
     ffn_inner = project(normed_two, full_in)
     ffn_act = jax.nn.gelu(ffn_inner, approximate=False).astype(jnp.bfloat16)
@@ -125,11 +478,6 @@
     norm_value, norm_pull = jax.vjp(rms_norm, residual, gain_two.astype(jnp.float32))
     grad_res_norm, grad_gain_two = norm_pull(grad_normed_two)
     grad_residual = grad_output + grad_res_norm
-    ffn_sums = (
-        lax.psum_scatter(grad_gain_two, "dp", scatter_dimension=0, tiled=True),
-        lax.psum_scatter(grad_wide, "dp", scatter_dimension=0, tiled=True),
-        lax.psum_scatter(grad_ffn, "dp", scatter_dimension=0, tiled=True),
-    )
     grad_attn = grad_residual.astype(jnp.bfloat16)
     grad_proj_out = weight_grad(attn_mix, grad_attn)
     grad_mix = project_back(grad_attn, full_out).astype(jnp.bfloat16).reshape(row_count, SEQ, H, DH)
@@ -185,26 +533,18 @@
     first_value, first_pull = jax.vjp(rms_norm, inputs, gain_one.astype(jnp.float32))
     grad_in_norm, grad_gain_one = first_pull(grad_normed_one)
     grad_tokens = grad_residual + grad_in_norm
-    attn_sums = (
-        lax.psum_scatter(grad_gain_one, "dp", scatter_dimension=0, tiled=True),
-        lax.psum_scatter(grad_proj_query, "dp", scatter_dimension=0, tiled=True),
-        lax.psum_scatter(grad_proj_key, "dp", scatter_dimension=0, tiled=True),
-        lax.psum_scatter(grad_proj_value, "dp", scatter_dimension=0, tiled=True),
-        lax.psum_scatter(grad_proj_out, "dp", scatter_dimension=0, tiled=True),
-    )
-    table_total = lax.psum(table_sum, "dp")
+    grad_attn_weights = jnp.concatenate([grad_proj_query, grad_proj_key, grad_proj_value, grad_proj_out], axis=1)
+    sums = reduce_grads(grad_attn_weights, grad_wide, grad_ffn, grad_gain_one, grad_gain_two, table_sum)
+    attn_sum, wide_sum, ffn_sum, gain_one_sum, gain_two_sum, table_total = sums
     return (
         output,
         grad_tokens,
-        attn_sums[0],
-        attn_sums[1],
-        attn_sums[2],
-        attn_sums[3],
-        attn_sums[4],
+        gain_one_sum,
+        *jnp.split(attn_sum, 4, axis=1),
         table_total,
-        ffn_sums[0],
-        ffn_sums[1],
-        ffn_sums[2],
+        gain_two_sum,
+        wide_sum,
+        ffn_sum,
     )
 
 

time: 1160 us -> 584 us (0.50)
  waiting for transfers between devices: 635 us -> 0 us
  Pallas kernels: 0 us -> 185 us
  blocking collectives: 82.3 us -> 0 us
  matrix products: 232 us -> 200 us
  between operations: 14.9 us -> 1.68 us
    reduce_scatter x6 -> x0, waiting for transfers between devices: 480 us -> none  [the longest x1 142 us: per_device(): lax.psum_scatter(grad_ffn, 'dp', scatter_dimension=0, tiled=True)]
    pallas_call x0 -> x2, Pallas kernels: none -> 185 us  [the longest x1 103 us: reduce_grads(): pl.pallas_call(partial(reduce_kernel, count), out_shape=[jax.ShapeDtypeSt...]
    all_gather x6 -> x0, waiting for transfers between devices: 151 us -> none  [the longest x1 59.8 us: per_device(): lax.all_gather(w_in, 'dp', axis=0, tiled=True)]
    unnamed x2 -> x0, blocking collectives: 82.3 us -> none
    slice x0 -> x6, local copies, waits for them, and re-layouts: none -> 14.8 us  [the longest x2 10 us: reduce_grads(): block[:, lo:hi].astype(jnp.bfloat16).reshape(FULL + (-1, hi - lo))]
    unnamed x94 -> x101, local copies, waits for them, and re-layouts: 49.1 us -> 34.7 us
    while x80 -> x28, local copies, waits for them, and re-layouts: 13.9 us -> 0.06 us
  transfers between devices with their start and end apart: 12 -> 0, of which waited for: 9 -> 0; matrix products, arithmetic and copies ran while one was open for 32% -> 0% of each run, Pallas kernels for 0% -> 0%
where the time goes in v1:
time: 584 us; the launch traced here: 573 us
  matrix products  200 us (34%)
  Pallas kernels  185 us (32%)
  local copies, waits for them, and re-layouts  150 us (26%)
  other arithmetic  35.7 us (6%)
    pallas_call x1, Pallas kernels, reduce_grads(): pl.pallas_call(partial(reduce_kernel, count), out_shape=[jax.ShapeDtypeSt...  103 us
    pallas_call x1, Pallas kernels, gather_weights(): pl.pallas_call(partial(gather_kernel, count), out_shape=[jax.ShapeDtypeSt...  81.9 us
    dot_general x6, matrix products, project(): return jnp.dot(left, right, preferred_element_type=jnp.float32)  56.8 us
    unnamed x101, local copies, waits for them, and re-layouts  34.7 us
    dot_general x4, matrix products, scores_of(): jnp.einsum('ihd,jhd->hij', query_row, key_row, preferred_element_type=jnp...  33.3 us
    dot_general x6, matrix products, project_back(): jnp.einsum('te,de->td', left, right, preferred_element_type=jnp.float32)  29.6 us
    convert_element_type x2, local copies, waits for them, and re-layouts, attend_back(): (probabilities * (grad_probs - inner_sum)).astype(jnp.bfloat16)  28.9 us
    while x5, local copies, waits for them, and re-layouts, per_device(): lax.map(attend, (query_proj, key_proj, value_proj, seg_all))  23.5 us

profile of v1, /device:TPU:0, one launch (start us, length us, event | category | flops | bytes accessed | tf_op | source)
XLA Modules:
  0.0 573.3 jit_solution(10212647146188611764)
XLA Ops:
  15.6 81.9 %shard_map.203 = (bf16[4,2,2,2,16,128]{5,4,3,2,1,0:T(8,128)(2,1)}, bf16[4,2,2,2,24,1536]{5,4,3,2,1,0:T(8,128)(2,1)}, bf16[4,2,2,2,24,1536]{5,4,3,2,1,0:T(8,128)(...) custom-call(bf16[16,128]{1,0:T(8,128)(2,1)} %scatter.4.refs_0_, ...), custom_call_target="tpu_custom_call" | custom-call | tf_op jit(solution)/shard_map/pallas_call | solution.py:299
  107.1 3.8 convolution_convert_fusion.6
  116.9 3.8 convolution_convert_fusion.7
  123.3 3.8 reshape.340
  130.2 8.5 %fusion.60 = f32[262144,12]{0,1:T(8,128)} fusion(bf16[32,12]{0,1:T(8,128)(2,1)S(1)} %copy-done, s32[262144]{0:T(1024)S(1)} %copy-done.17), kind=kOutput, calls=%fused_computation.65 | convolution fusion | flops 209715200 | bytes 13632256 | tf_op jit(solution)/shard_map/dot_general | solution.py:434
  138.7 17.8 %copy.154 = f32[2,8,512,512]{3,2,1,0:T(8,128)} copy(f32[2,8,512,512]{3,1,2,0:T(8,128)} %bitcast.242) | data formatting | bytes 33554432
  156.5 10.6 %slice.90 = f32[12,512,512]{2,1,0:T(8,128)} slice(f32[16,512,512]{2,1,0:T(8,128)} %bitcast.243), slice={[0:12], [0:512], [0:512]} | slice | bytes 25165824 | tf_op jit(solution)/shard_map/reshape | solution.py:436
  167.1 12.6 %copy.104 = f32[12,512,512]{1,2,0:T(8,128)} copy(f32[12,512,512]{2,1,0:T(8,128)} %slice.90) | data formatting | bytes 25165824 | tf_op jit(solution)/shard_map/while | solution.py:464
  181.0 22.6 %while.30 = (s32[]{:T(128)}, bf16[2,512,12,64]{1,3,2,0:T(8,128)(2,1)}, f32[2,12,512,1]{2,1,3,0:T(8,128)S(1)}, bf16[2,512,12,64]{1,3,2,0:T(8,128)(2,1)}, s32[2,51...) while((s32[]{:T(128)}, ...), condition=%wide.region_6.7_spmd, body=%wide.region_3.6_spmd.sunk | while | flops 827975680 | bytes 60539016 | solution.py:464
  181.6 6.1 %fusion.186 = (f32[12,512]{1,0:T(8,128)S(1)}, f32[12,512,512]{1,2,0:T(8,128)S(1)}) fusion(f32[12,512,512]{1,2,0:T(8,128)} %get-tuple-element.553, bf16[2,512,12,64]{1,3,2,0:T(8,128)(2,1)S(1)} %get-tuple-element.552, s32[]{:T(128)S(6)} %copy.171, bf16[2,512,12,64]{1,3,2,0:T(8,128)(2,1)S(1)} %get-tuple-element.551, ...), kind=kOutput, calls=%fused_computation.189.clone.1 | convolution fusion | flops 412084224 | bytes 27026432 | tf_op jit(solution)/shard_map/while/body/eval_jaxpr/ihd,jhd->hij/dot_general | solution.py:447
  192.7 6.1 %fusion.186 = (f32[12,512]{1,0:T(8,128)S(1)}, f32[12,512,512]{1,2,0:T(8,128)S(1)}) fusion(f32[12,512,512]{1,2,0:T(8,128)} %get-tuple-element.553, bf16[2,512,12,64]{1,3,2,0:T(8,128)(2,1)S(1)} %get-tuple-element.552, s32[]{:T(128)S(6)} %copy.171, bf16[2,512,12,64]{1,3,2,0:T(8,128)(2,1)S(1)} %get-tuple-element.551, ...), kind=kOutput, calls=%fused_computation.189.clone.1 | convolution fusion | flops 412084224 | bytes 27026432 | tf_op jit(solution)/shard_map/while/body/eval_jaxpr/ihd,jhd->hij/dot_general | solution.py:447
  203.6 4.2 copy.105
  211.3 35.8 %multiply_convert_fusion.1 = (bf16[1024,3072]{1,0:T(8,128)(2,1)}, f32[1024,3072]{1,0:T(8,128)}, f32[1024,3072]{1,0:T(8,128)}) fusion(bf16[768,1536]{1,0:T(8,128)(2,1)S(1)} %bitcast.279, bf16[768,1536]{1,0:T(8,128)(2,1)S(1)} %bitcast.277, f32[1024,768]{0,1:T(8,128)S(1)} %get-tuple-element.382, f32[768]{0:T(1024)S(1)} %reshape.363, f32[1024]{0:T(1024)S(1)} %fusion.131), kind=kOutput, calls=%fused_computation.78 | convolution fusion | flops 5048107008 | bytes 39328768 | tf_op jit(solution)/shard_map/dot_general | solution.py:44
  247.1 15.9 %fusion.68 = bf16[1024,3072]{1,0:T(8,128)(2,1)} fusion(f32[1024,3072]{1,0:T(8,128)} %get-tuple-element.360, f32[1024,3072]{1,0:T(8,128)} %get-tuple-element.383, bf16[1024,768]{1,0:T(8,128)(2,1)S(1)} %copy-done.19, bf16[3072,384]{1,0:T(8,128)(2,1)} %bitcast.283, bf16[3072,384]{1,0:T(8,128)(2,1)} %bitcast.281), kind=kOutput, calls=%fused_computation.76 | convolution fusion | flops 4885315584 | bytes 37748736 | tf_op jit(solution)/shard_map/te,de->td/dot_general | solution.py:48
  263.0 10.2 %add_convert_fusion = bf16[1024,768]{0,1:T(8,128)(2,1)} fusion(f32[1024,768]{0,1:T(8,128)S(1)} %get-tuple-element.382, bf16[1024,3072]{1,0:T(8,128)(2,1)} %get-tuple-element.359, bf16[3072,384]{1,0:T(8,128)(2,1)} %bitcast.284, bf16[3072,384]{1,0:T(8,128)(2,1)} %bitcast.282), kind=kOutput, calls=%fused_computation.114 | convolution fusion | flops 4842848256 | bytes 15728640 | tf_op jit(solution)/shard_map/dot_general | solution.py:44
  273.2 6.9 %convolution_convert_fusion.2 = bf16[3072,768]{1,0:T(8,128)(2,1)} fusion(bf16[1024,3072]{1,0:T(8,128)(2,1)S(1)} %copy-done.50, bf16[1024,768]{1,0:T(8,128)(2,1)S(1)} %copy-done.19), kind=kOutput, calls=%fused_computation.97 | convolution fusion | flops 4834197504 | bytes 12582912 | tf_op jit(solution)/shard_map/te,td->ed/dot_general | solution.py:52
  280.1 6.0 %multiply_reduce_fusion.1 = (f32[768]{0:T(1024)}, f32[1024]{0:T(1024)S(1)}, f32[1024,768]{0,1:T(8,128)S(1)}) fusion(f32[1024,768]{0,1:T(8,128)S(1)} %get-tuple-element.382, f32[1024]{0:T(1024)S(1)} %fusion.131, f32[768]{0:T(1024)S(1)} %reshape.363, bf16[1024,3072]{1,0:T(8,128)(2,1)S(1)} %copy-done.49, bf16[768,1536]{1,0:T(8,128)(2,1)S(1)} %bitcast.280, ...), kind=kOutput, calls=%fused_computation.111 | convolution fusion | flops 4845991936 | bytes 17315840 | tf_op jit(solution)/shard_map/te,de->td/dot_general | solution.py:48
  286.1 7.0 %convolution_convert_fusion.3 = bf16[768,3072]{1,0:T(8,128)(2,1)} fusion(bf16[1024,3072]{1,0:T(8,128)(2,1)S(1)} %copy-done.49, f32[1024,768]{0,1:T(8,128)S(1)} %get-tuple-element.382, f32[768]{0:T(1024)S(1)} %reshape.363, f32[1024]{0:T(1024)S(1)} %fusion.131), kind=kOutput, calls=%fused_computation.98 | convolution fusion | flops 4836556800 | bytes 14162944 | tf_op jit(solution)/shard_map/te,td->ed/dot_general | solution.py:52
  299.6 4.9 fusion.139
  304.5 5.2 fusion.138
  320.6 108.2 %while.31 = (s32[]{:T(128)}, f32[32,12]{0,1:T(8,128)S(1)}, bf16[2,512,12,64]{1,3,2,0:T(8,128)(2,1)}, bf16[2,512,12,64]{1,3,2,0:T(8,128)(2,1)}, bf16[2,512,12,64]...) while((s32[]{:T(128)}, f32[32,12]{0,1:T(8,128)S(1)}, ...), condition=%wide.region_11.12_spmd.clone, body=%wide.region_9.11_spmd.clone.sunk | while | flops 2261117696 | bytes 189938032 | solution.py:519
  321.1 7.7 %fusion.198 = f32[12,512,512]{1,2,0:T(8,128)} fusion(bf16[2,512,12,64]{1,3,2,0:T(8,128)(2,1)} %get-tuple-element.596, s32[]{:T(128)S(6)} %copy.182, bf16[2,512,12,64]{1,3,2,0:T(8,128)(2,1)} %get-tuple-element.595), kind=kOutput, calls=%fused_computation.41.clone.1 | convolution fusion | flops 402653184 | bytes 14156800 | tf_op jit(solution)/shard_map/while/body/eval_jaxpr/ihd,jhd->hij/dot_general | solution.py:495
  328.8 10.6 %multiply_reduce_fusion.5 = (f32[12,512]{1,0:T(8,128)S(1)}, f32[12,512,512]{1,2,0:T(8,128)S(1)}) fusion(f32[12,512,512]{1,2,0:T(8,128)} %fusion.198, f32[12,512]{1,0:T(8,128)S(1)} %dynamic-slice_bitcast_fusion.2, f32[12,512,512]{1,2,0:T(8,128)} %get-tuple-element.593, bf16[2,512,12,64]{1,3,2,0:T(8,128)(2,1)} %get-tuple-element.592, s32[]{:T(128)S(6)} %copy.182, ...), kind=kOutput, calls=%fused_computation.26.clone.1 | convolution fusion | flops 418375680 | bytes 39642112 | tf_op jit(solution)/shard_map/while/body/eval_jaxpr/ihd,jhd->hij/dot_general | solution.py:447
  339.4 6.9 %multiply_convert_fusion.6 = bf16[12,512,512]{1,2,0:T(8,128)(2,1)S(1)} fusion(f32[12,512,512]{1,2,0:T(8,128)S(1)} %get-tuple-element.526, f32[12,512,512]{1,2,0:T(8,128)} %fusion.198, f32[12,512]{1,0:T(8,128)S(1)} %get-tuple-element.527), kind=kLoop, calls=%fused_computation.25.clone.1 | loop fusion | flops 9437184 | bytes 31481856 | tf_op jit(solution)/shard_map/while/body/eval_jaxpr/convert_element_type | solution.py:499
  353.3 14.5 %copy.162 = bf16[12,512,512]{2,0,1:T(8,128)(2,1)} copy(bf16[12,512,512]{1,2,0:T(8,128)(2,1)} %copy-done.2) | data formatting | bytes 12582912 | tf_op jit(solution)/shard_map/while/body/eval_jaxpr/convert_element_type | solution.py:499
  367.8 6.9 %fusion.199 = f32[32,12]{0,1:T(8,128)S(1)} fusion(bf16[12,512,512]{2,0,1:T(8,128)(2,1)} %copy.162, s32[512,512]{1,0:T(8,128)S(1)} %copy-done.27, f32[32,12]{0,1:T(8,128)S(1)} %get-tuple-element.571, pred[]{:T(512)S(6)} %compare.16), kind=kOutput, calls=%fused_computation.40.clone.1 | convolution fusion | flops 218104576 | bytes 7343105 | tf_op jit(solution)/shard_map/while/body/eval_jaxpr/hij,bij->bh/dot_general | solution.py:506
  375.0 7.7 %fusion.198 = f32[12,512,512]{1,2,0:T(8,128)} fusion(bf16[2,512,12,64]{1,3,2,0:T(8,128)(2,1)} %get-tuple-element.596, s32[]{:T(128)S(6)} %copy.182, bf16[2,512,12,64]{1,3,2,0:T(8,128)(2,1)} %get-tuple-element.595), kind=kOutput, calls=%fused_computation.41.clone.1 | convolution fusion | flops 402653184 | bytes 14156800 | tf_op jit(solution)/shard_map/while/body/eval_jaxpr/ihd,jhd->hij/dot_general | solution.py:495
  382.7 10.6 %multiply_reduce_fusion.5 = (f32[12,512]{1,0:T(8,128)S(1)}, f32[12,512,512]{1,2,0:T(8,128)S(1)}) fusion(f32[12,512,512]{1,2,0:T(8,128)} %fusion.198, f32[12,512]{1,0:T(8,128)S(1)} %dynamic-slice_bitcast_fusion.2, f32[12,512,512]{1,2,0:T(8,128)} %get-tuple-element.593, bf16[2,512,12,64]{1,3,2,0:T(8,128)(2,1)} %get-tuple-element.592, s32[]{:T(128)S(6)} %copy.182, ...), kind=kOutput, calls=%fused_computation.26.clone.1 | convolution fusion | flops 418375680 | bytes 39642112 | tf_op jit(solution)/shard_map/while/body/eval_jaxpr/ihd,jhd->hij/dot_general | solution.py:447
  393.3 6.9 %multiply_convert_fusion.6 = bf16[12,512,512]{1,2,0:T(8,128)(2,1)S(1)} fusion(f32[12,512,512]{1,2,0:T(8,128)S(1)} %get-tuple-element.526, f32[12,512,512]{1,2,0:T(8,128)} %fusion.198, f32[12,512]{1,0:T(8,128)S(1)} %get-tuple-element.527), kind=kLoop, calls=%fused_computation.25.clone.1 | loop fusion | flops 9437184 | bytes 31481856 | tf_op jit(solution)/shard_map/while/body/eval_jaxpr/convert_element_type | solution.py:499
  407.3 14.5 %copy.162 = bf16[12,512,512]{2,0,1:T(8,128)(2,1)} copy(bf16[12,512,512]{1,2,0:T(8,128)(2,1)} %copy-done.2) | data formatting | bytes 12582912 | tf_op jit(solution)/shard_map/while/body/eval_jaxpr/convert_element_type | solution.py:499
  421.7 6.9 %fusion.199 = f32[32,12]{0,1:T(8,128)S(1)} fusion(bf16[12,512,512]{2,0,1:T(8,128)(2,1)} %copy.162, s32[512,512]{1,0:T(8,128)S(1)} %copy-done.27, f32[32,12]{0,1:T(8,128)S(1)} %get-tuple-element.571, pred[]{:T(512)S(6)} %compare.16), kind=kOutput, calls=%fused_computation.40.clone.1 | convolution fusion | flops 218104576 | bytes 7343105 | tf_op jit(solution)/shard_map/while/body/eval_jaxpr/hij,bij->bh/dot_general | solution.py:506
  460.6 102.9 %shard_map.204 = (f32[24,1536]{1,0:T(8,128)}, f32[24,1536]{1,0:T(8,128)}, f32[24,1536]{1,0:T(8,128)}, f32[24,1536]{1,0:T(8,128)}, f32[96,384]{1,0:T(8,128)}, /*index=5*/f32[96,384]{1,0:T(8,128)}, f32[16,128]{1,0:T(8,128)}) custom-call(bf16[4,2,2,2,24,1536]{5,4,3,2,1,0:T(8,128)(2,1)} %pad_maximum_fusion.6.refs_0_, ...), custom_call_target="tpu_custom_call" | custom-call | tf_op jit(solution)/shard_map/pallas_call | solution.py:385
  (216 shorter events, 123.4 us)
Async XLA Ops:
  0.6 129.5 %copy-start = (bf16[32,12]{0,1:T(8,128)(2,1)S(1)}, bf16[32,12]{0,1:T(8,128)(2,1)}, u32[]{:S(2)}) copy-start(bf16[32,12]{0,1:T(8,128)(2,1)} %param.25) | copy-start | bytes 2308
  12.5 86.6 %copy-start.9 = (bf16[1024,768]{0,1:T(8,128)(2,1)}, bf16[1024,768]{0,1:T(8,128)(2,1)S(1)}, u32[]{:S(2)}) copy-start(bf16[1024,768]{0,1:T(8,128)(2,1)S(1)} %copy.96) | copy-start | bytes 4718596
  12.8 85.7 %copy-start.39 = (f32[1024]{0:T(1024)}, f32[1024]{0:T(1024)S(1)}, u32[]{:S(2)}) copy-start(f32[1024]{0:T(1024)S(1)} %fusion.81) | copy-start | bytes 12292
  12.8 86.2 %copy-start.37 = (f32[1024]{0:T(1024)}, f32[1024]{0:T(1024)S(1)}, u32[]{:S(2)}) copy-start(f32[1024]{0:T(1024)S(1)} %fusion.130) | copy-start | bytes 12292
  203.6 4.7 copy-start.3
  203.6 4.7 copy-start.5
  203.6 4.7 copy-start.31
  203.6 4.7 copy-start.33
  203.6 4.7 copy-start.10
  203.6 4.7 copy-start.28
  211.3 35.8 %copy-start.19 = (bf16[1024,768]{1,0:T(8,128)(2,1)S(1)}, bf16[1024,768]{1,0:T(8,128)(2,1)}, u32[]{:S(2)}) copy-start(bf16[1024,768]{1,0:T(8,128)(2,1)} %param.29) | copy-start | bytes 4718596
  263.0 10.2 %copy-start.50 = (bf16[1024,3072]{1,0:T(8,128)(2,1)S(1)}, bf16[1024,3072]{1,0:T(8,128)(2,1)}, u32[]{:S(2)}) copy-start(bf16[1024,3072]{1,0:T(8,128)(2,1)} %get-tuple-element.359) | copy-start | bytes 18874372
  273.1 6.9 %copy-start.46 = (bf16[4,2,2,2,24,1536]{5,4,3,2,1,0:T(8,128)(2,1)S(1)}, bf16[4,2,2,2,24,1536]{5,4,3,2,1,0:T(8,128)(2,1)}, u32[]{:S(2)}) copy-start(bf16[4,2,2,2,24,1536]{5,4,3,2,1,0:T(8,128)(2,1)} %get-tuple-element.154) | copy-start | bytes 7077892
  273.1 6.9 %copy-start.48 = (bf16[4,2,2,2,24,1536]{5,4,3,2,1,0:T(8,128)(2,1)S(1)}, bf16[4,2,2,2,24,1536]{5,4,3,2,1,0:T(8,128)(2,1)}, u32[]{:S(2)}) copy-start(bf16[4,2,2,2,24,1536]{5,4,3,2,1,0:T(8,128)(2,1)} %get-tuple-element.155) | copy-start | bytes 7077892
  273.2 6.9 %copy-start.49 = (bf16[1024,3072]{1,0:T(8,128)(2,1)S(1)}, bf16[1024,3072]{1,0:T(8,128)(2,1)}, u32[]{:S(2)}) copy-start(bf16[1024,3072]{1,0:T(8,128)(2,1)} %fusion.68) | copy-start | bytes 18874372
  286.1 7.0 %copy-start.16 = (bf16[1024,768]{0,1:T(8,128)(2,1)S(1)}, bf16[1024,768]{0,1:T(8,128)(2,1)}, u32[]{:S(2)}) copy-start(bf16[1024,768]{0,1:T(8,128)(2,1)} %copy.108) | copy-start | bytes 4718596
  294.5 15.1 %copy-start.12 = (f32[1024,768]{0,1:T(8,128)}, f32[1024,768]{0,1:T(8,128)S(1)}, u32[]{:S(2)}) copy-start(f32[1024,768]{0,1:T(8,128)S(1)} %fusion.79) | copy-start | bytes 9437188
  304.5 5.2 copy-start.29
  316.6 4.0 copy-start.4
  316.6 4.0 copy-start.32
  316.6 4.0 copy-start.34
  316.6 4.0 copy-start.41
  339.4 7.0 %copy-start.8 = (bf16[2,512,12,64]{1,3,2,0:T(8,128)(2,1)S(1)}, bf16[2,512,12,64]{1,3,2,0:T(8,128)(2,1)}, u32[]{:S(2)}) copy-start(bf16[2,512,12,64]{1,3,2,0:T(8,128)(2,1)} %get-tuple-element.595) | copy-start | bytes 4718596 | tf_op jit(solution)/shard_map/while
  339.4 7.0 %copy-start.14 = (bf16[2,512,12,64]{1,3,2,0:T(8,128)(2,1)S(1)}, bf16[2,512,12,64]{1,3,2,0:T(8,128)(2,1)}, u32[]{:S(2)}) copy-start(bf16[2,512,12,64]{1,3,2,0:T(8,128)(2,1)} %get-tuple-element.574) | copy-start | bytes 4718596 | tf_op jit(solution)/shard_map/while
  346.4 4.9 copy-start.2
  353.3 14.5 %copy-start.27 = (s32[512,512]{1,0:T(8,128)S(1)}, s32[512,512]{1,0:T(8,128)}, u32[]{:S(2)}) copy-start(s32[512,512]{1,0:T(8,128)} %get-tuple-element.597) | copy-start | bytes 3145732 | tf_op jit(solution)/shard_map/while
  393.3 7.0 %copy-start.8 = (bf16[2,512,12,64]{1,3,2,0:T(8,128)(2,1)S(1)}, bf16[2,512,12,64]{1,3,2,0:T(8,128)(2,1)}, u32[]{:S(2)}) copy-start(bf16[2,512,12,64]{1,3,2,0:T(8,128)(2,1)} %get-tuple-element.595) | copy-start | bytes 4718596 | tf_op jit(solution)/shard_map/while
  393.3 7.0 %copy-start.14 = (bf16[2,512,12,64]{1,3,2,0:T(8,128)(2,1)S(1)}, bf16[2,512,12,64]{1,3,2,0:T(8,128)(2,1)}, u32[]{:S(2)}) copy-start(bf16[2,512,12,64]{1,3,2,0:T(8,128)(2,1)} %get-tuple-element.574) | copy-start | bytes 4718596 | tf_op jit(solution)/shard_map/while
  400.3 5.0 copy-start.2
  407.3 14.5 %copy-start.27 = (s32[512,512]{1,0:T(8,128)S(1)}, s32[512,512]{1,0:T(8,128)}, u32[]{:S(2)}) copy-start(s32[512,512]{1,0:T(8,128)} %get-tuple-element.597) | copy-start | bytes 3145732 | tf_op jit(solution)/shard_map/while
  428.9 3.8 copy-start.23
  460.6 112.3 %copy-start.1 = (bf16[32,12]{0,1:T(8,128)(2,1)S(1)}, bf16[32,12]{0,1:T(8,128)(2,1)}, u32[]{:S(2)}) copy-start(bf16[32,12]{0,1:T(8,128)(2,1)} %param.25) | copy-start | bytes 2308
  (26 other events, 57.7 us)

commit v2 on v1

--- a/solution.py
+++ b/solution.py
@@ -1,10 +1,8 @@
 from functools import partial
-
+from jax.sharding import PartitionSpec as P
 import jax
 import jax.numpy as jnp
 from jax import lax
-from jax.sharding import PartitionSpec as P
-
 from jax.experimental import pallas as pl
 from jax.experimental.pallas import tpu as pltpu
 
@@ -13,45 +11,297 @@
 DH = 64
 NB = 32
 SEQ = 512
-
-
-EPSILON = 1e-06
+FF = 3072
+PAIRS = 6
+EPSILON = 1e-6
 CUTOFFS = (12, 16, 23, 32, 46, 64, 91)
-
-
-def bucket_index(length):
-    positions = jnp.arange(length, dtype=jnp.int32)
-    offsets = positions[None, :] - positions[:, None]
+VMEM = pl.BlockSpec(memory_space=pltpu.VMEM)
+SMEM = pl.BlockSpec(memory_space=pltpu.SMEM)
+f32, bf16 = jnp.float32, jnp.bfloat16
+
+def nt(a, b):
+    return lax.dot_general(a, b, (((1,), (1,)), ((), ())), preferred_element_type=f32)
+
+def nn(a, b):
+    return jnp.dot(a, b, preferred_element_type=f32)
+
+def bucket_of(offsets):
     distance = jnp.abs(offsets)
     coarse = jnp.full_like(distance, 8)
     for cutoff in CUTOFFS:
         coarse = coarse + (distance >= cutoff).astype(jnp.int32)
     return jnp.where(distance < 8, distance, coarse) + jnp.where(offsets > 0, 16, 0)
 
-
-def segment_ids(lengths, length):
-    seg_ends = jnp.cumsum(lengths[:, 1:], axis=1)
-    positions = jnp.arange(length, dtype=jnp.int32)
-    return jnp.sum((positions[None, :, None] >= seg_ends[:, None, :]).astype(jnp.int32), axis=2)
-
-
-def rms_norm(values, gains):
-    inv_rms = lax.rsqrt(jnp.mean(values * values, axis=-1, keepdims=True) + EPSILON)
-    return values * inv_rms * gains
-
-
-def project(left, right):
-    return jnp.dot(left, right, preferred_element_type=jnp.float32)
-
-
-def project_back(left, right):
-    return jnp.einsum("te,de->td", left, right, preferred_element_type=jnp.float32)
-
-
-def weight_grad(left, right):
-    return jnp.einsum("te,td->ed", left, right, preferred_element_type=jnp.float32)
-
-
+def strip_onehot():
+    d = jnp.arange(-1, 2, dtype=jnp.int32)[:, None, None] * 128
+    jj = jnp.arange(128, dtype=jnp.int32)
+    off = d + jj[None, :, None] - jj[None, None, :]
+    return (bucket_of(off).reshape(1, -1) == jnp.arange(NB, dtype=jnp.int32)[:, None])
+
+def bias_strips(table):
+    oh = strip_onehot().astype(bf16)
+    return jnp.dot(table.T, oh, preferred_element_type=f32).reshape(H, 3, 128, 128)
+
+def seg_marks(lengths):
+    ends = jnp.cumsum(lengths[:, 1:], axis=1)
+    pos = jnp.arange(SEQ, dtype=jnp.int32)
+    seg = jnp.sum((pos[None, :, None] >= ends[:, None, :]).astype(jnp.int32), axis=2)
+    one = seg.reshape(-1)[:, None] == jnp.arange(128, dtype=jnp.int32)[None, :]
+    keep = jnp.arange(128)[None, :] < 5
+    return one.astype(bf16), jnp.where(one | ~keep, 0.0, -1e30).astype(bf16)
+
+def lane_mask(h):
+    lane = lax.broadcasted_iota(jnp.int32, (1, 128), 1)
+    return lane < 64 if h == 0 else lane >= 64
+
+def scores_t(km, qm, strips, far, head, ib):
+    s = nt(km, qm)
+    lo, hi = far[head, 0], far[head, 1]
+    rows = []
+    for bj in range(4):
+        blocks = []
+        for bi in (2 * ib, 2 * ib + 1):
+            d = bj - bi
+            b = s[128 * bj:128 * (bj + 1), 128 * (bi - 2 * ib):128 * (bi - 2 * ib + 1)]
+            if d <= -2: b = b + lo
+            elif d >= 2: b = b + hi
+            else: b = b + strips[head, d + 1]
+            blocks.append(b)
+        rows.append(jnp.concatenate(blocks, axis=1))
+    return jnp.concatenate(rows, axis=0)
+
+def attn_fwd_pair(q, k, v, km_marks, qm_marks, strips, far, mix, lse, row, hp):
+    rows = pl.ds(pl.multiple_of(row * 512, 512), 512)
+    cols = pl.ds(pl.multiple_of(hp * 128, 128), 128)
+    q2, k2 = q[rows, cols], k[rows, cols]
+    v2t = v[rows, cols].T
+    kmk, qmk = km_marks[rows, :], qm_marks[rows, :]
+    outs = []
+    for h in range(2):
+        head = hp * 2 + h
+        km = jnp.concatenate([jnp.where(lane_mask(h), k2, 0), kmk], axis=1)
+        for ib in range(2):
+            sl = slice(256 * ib, 256 * ib + 256)
+            qm = jnp.concatenate([q2[sl], qmk[sl]], axis=1)
+            s = scores_t(km, qm, strips, far, head, ib)
+            m = jnp.max(s, axis=0, keepdims=True)
+            e = jnp.exp(s - m)
+            l = jnp.sum(e, axis=0, keepdims=True)
+            p = (e * (1.0 / l)).astype(bf16)
+            lse[row, pl.ds(head, 1), sl] = m + jnp.log(l)
+            outs.append(nn(v2t[64 * h:64 * h + 64], p))
+    o0 = jnp.concatenate(outs[:2], axis=1)
+    o1 = jnp.concatenate(outs[2:], axis=1)
+    mix[rows, cols] = jnp.concatenate([o0, o1], axis=0).T.astype(bf16)
+
+def inv_rms(x):
+    return lax.rsqrt(jnp.mean(x * x, axis=-1, keepdims=True) + EPSILON)
+
+def attn_fwd_kernel(tokens, gain, wqkv, wo, gain2, km_marks, qm_marks, strips, far, n1, q, k, v, mix, lse, resid, n2):
+    def proj(c, _):
+        rows = pl.ds(pl.multiple_of(c * 256, 256), 256)
+        x = tokens[rows, :].astype(f32)
+        n = (x * inv_rms(x) * gain[...]).astype(bf16)
+        n1[rows, :] = n
+        for i, o in enumerate((q, k, v)):
+            o[rows, :] = nn(n, wqkv[:, i * D:(i + 1) * D]).astype(bf16)
+        return 0
+    lax.fori_loop(0, 4, proj, 0)
+    def body(i, _):
+        attn_fwd_pair(q, k, v, km_marks, qm_marks, strips, far, mix, lse, i // PAIRS, i % PAIRS)
+        return 0
+    lax.fori_loop(0, 2 * PAIRS, body, 0)
+    def out(c, _):
+        rows = pl.ds(pl.multiple_of(c * 256, 256), 256)
+        r = tokens[rows, :].astype(f32) + nn(mix[rows, :], wo[...])
+        resid[rows, :] = r
+        n2[rows, :] = (r * inv_rms(r) * gain2[...]).astype(bf16)
+        return 0
+    lax.fori_loop(0, 4, out, 0)
+
+def sds(*shape, dtype=bf16):
+    return jax.ShapeDtypeStruct(shape, dtype)
+
+def attn_fwd(tokens, gain, wqkv, wo, gain2, km_marks, qm_marks, strips, far):
+    T = tokens.shape[0]
+    return pl.pallas_call(attn_fwd_kernel,
+        out_shape=[sds(T, D), sds(T, D), sds(T, D), sds(T, D), sds(T, D), sds(T // SEQ, H, SEQ, dtype=f32), sds(T, D, dtype=f32), sds(T, D)],
+        in_specs=[VMEM] * 8 + [SMEM], out_specs=[VMEM] * 8,
+        compiler_params=pltpu.CompilerParams(vmem_limit_bytes=60 << 20),
+    )(tokens, gain.reshape(1, D).astype(f32), wqkv, wo, gain2.reshape(1, D).astype(f32), km_marks, qm_marks, strips, far)
+
+R2 = 0.7071067811865476
+PHI = 0.3989422804014327
+
+def gelu_pair(x):
+    cdf = 0.5 + 0.5 * lax.erf(x * R2)
+    return x * cdf, cdf + x * (jnp.exp(x * x * -0.5) * PHI)
+
+def gelu_pair_as(x):
+    z = jnp.abs(x) * R2
+    t = 1.0 / (1.0 + 0.3275911 * z)
+    e = jnp.exp(-(z * z))
+    poly = t * (0.254829592 + t * (-0.284496736 + t * (1.421413741 + t * (-1.453152027 + t * 1.061405429))))
+    tail = 0.5 * poly * e
+    cdf = jnp.where(x < 0, tail, 1.0 - tail)
+    return x * cdf, cdf + x * (e * PHI)
+
+FT = 512
+GELU = gelu_pair
+def ffn_kernel(n2, cot, resid, gain2, win, wff, out, gres, gn2sum, gin, gff, n2t, cott, oacc, gacc, act, ginn):
+    T = n2.shape[0]
+    C = 256
+    for c in range(T // C):
+        rows = slice(c * C, c * C + C)
+        n2t[:, rows] = n2[rows, :].T
+        cott[:, rows] = cot[rows, :].T
+    def tile(t, _):
+        cols = pl.ds(pl.multiple_of(t * FT, FT), FT)
+        wi = win.at[:, cols]
+        wf = wff.at[cols, :]
+        def chunk(c, _):
+            rows = pl.ds(pl.multiple_of(c * C, C), C)
+            inner = nn(n2[rows, :], wi[...])
+            ga = nt(cot[rows, :], wf[...])
+            a, dg = GELU(inner)
+            a = a.astype(bf16)
+            g = (dg * ga).astype(bf16)
+            act[rows, :] = a
+            ginn[rows, :] = g
+            o = nn(a, wf[...])
+            gn = nt(g, wi[...])
+            @pl.when(t == 0)
+            def _():
+                oacc[rows, :] = resid[rows, :] + o
+                gacc[rows, :] = gn
+            @pl.when(t > 0)
+            def _():
+                oacc[rows, :] += o
+                gacc[rows, :] += gn
+            return 0
+        lax.fori_loop(0, T // C, chunk, 0)
+        gin[:, cols] = nn(n2t[...], ginn[...]).astype(bf16)
+        gff[cols, :] = nn(cott[...], act[...]).astype(bf16).T
+        return 0
+    lax.fori_loop(0, FF // FT, tile, 0)
+    gn2sum[...] = jnp.zeros((1, D), f32)
+    def fin(c, _):
+        rows = pl.ds(pl.multiple_of(c * C, C), C)
+        out[rows, :] = oacc[rows, :].astype(bf16)
+        r = resid[rows, :]
+        s = inv_rms(r)
+        gn = gacc[rows, :]
+        gn2sum[...] += jnp.sum(gn * r * s, axis=0, keepdims=True)
+        gg = gn * gain2[...]
+        gres[rows, :] = cot[rows, :].astype(f32) + s * gg - r * (s * s * s * jnp.mean(gg * r, axis=-1, keepdims=True))
+        return 0
+    lax.fori_loop(0, T // C, fin, 0)
+
+def ffn(n2, cot, resid, gain2, win, wff):
+    T = n2.shape[0]
+    return pl.pallas_call(ffn_kernel,
+        out_shape=[sds(T, D), sds(T, D, dtype=f32), sds(1, D, dtype=f32), sds(D, FF), sds(FF, D)],
+        in_specs=[VMEM] * 6, out_specs=[VMEM] * 5,
+        scratch_shapes=[pltpu.VMEM((D, T), bf16), pltpu.VMEM((D, T), bf16), pltpu.VMEM((T, D), f32), pltpu.VMEM((T, D), f32),
+                        pltpu.VMEM((T, FT), bf16), pltpu.VMEM((T, FT), bf16)],
+        compiler_params=pltpu.CompilerParams(vmem_limit_bytes=60 << 20),
+    )(n2, cot, resid, gain2.reshape(1, D).astype(f32), win, wff)
+
+def attn_bwd_pair(q, k, v, gmix, km_marks, qm_marks, strips, far, lse, dq, dk, dv, tacc, facc, row, hp):
+    rows = pl.ds(pl.multiple_of(row * 512, 512), 512)
+    cols = pl.ds(pl.multiple_of(hp * 128, 128), 128)
+    q2, k2, v2, g2 = q[rows, cols], k[rows, cols], v[rows, cols], gmix[rows, cols]
+    k2t = k2.T
+    kmk, qmk = km_marks[rows, :], qm_marks[rows, :]
+    dvs, dks, dqs = None, None, []
+    for h in range(2):
+        head = hp * 2 + h
+        msk = lane_mask(h)
+        km = jnp.concatenate([jnp.where(msk, k2, 0), kmk], axis=1)
+        vm = jnp.where(msk, v2, 0)
+        qh = jnp.where(msk, q2, 0)
+        gh = jnp.where(msk, g2, 0)
+        for ib in range(2):
+            sl = slice(256 * ib, 256 * ib + 256)
+            qm = jnp.concatenate([q2[sl], qmk[sl]], axis=1)
+            s = scores_t(km, qm, strips, far, head, ib)
+            p = jnp.exp(s - lse[row, pl.ds(head, 1), sl])
+            dp = nt(vm, g2[sl])
+            dsum = jnp.sum(p * dp, axis=0, keepdims=True)
+            ds = p * (dp - dsum)
+            dsl = ds.astype(bf16)
+            dv1 = nn(p.astype(bf16), gh[sl])
+            dk1 = nn(dsl, qh[sl])
+            dvs = dv1 if dvs is None else dvs + dv1
+            dks = dk1 if dks is None else dks + dk1
+            dqs.append(nn(k2t[64 * h:64 * h + 64], dsl))
+            for bi in (2 * ib, 2 * ib + 1):
+                los, his = [], []
+                for bj in range(4):
+                    d = bj - bi
+                    b = ds[128 * bj:128 * (bj + 1), 128 * (bi - 2 * ib):128 * (bi - 2 * ib + 1)]
+                    if abs(d) <= 1: tacc[head, d + 1] += b
+                    else: (los if d < 0 else his).append(jnp.sum(b.reshape(16, 8, 128), axis=0))
+                for lst, idx in ((los, 0), (his, 1)):
+                    if lst: facc[head, idx] += sum(lst[1:], lst[0])
+    dv[rows, cols] = dvs.astype(bf16)
+    dk[rows, cols] = dks.astype(bf16)
+    dqt = jnp.concatenate([jnp.concatenate(dqs[:2], axis=1), jnp.concatenate(dqs[2:], axis=1)], axis=0)
+    dq[rows, cols] = dqt.T.astype(bf16)
+
+def attn_bwd_kernel(tokens, gain, n1, wqkv, wo, mix, q, k, v, gres, km_marks, qm_marks, strips, lse, far,
+                    gtok, gn1sum, gattn, gout, tacc, facc, n1t, ga, gmix, dq, dk, dv):
+    T = tokens.shape[0]
+    C = 256
+    tacc[...] = jnp.zeros(tacc.shape, f32)
+    facc[...] = jnp.zeros(facc.shape, f32)
+    def pre(c, _):
+        rows = pl.ds(pl.multiple_of(c * C, C), C)
+        g = gres[rows, :].astype(bf16)
+        ga[rows, :] = g
+        gmix[rows, :] = nt(g, wo[...]).astype(bf16)
+        n1t[:, rows] = n1[rows, :].T
+        return 0
+    lax.fori_loop(0, T // C, pre, 0)
+    def wout(c, _):
+        cols = pl.ds(pl.multiple_of(c * C, C), C)
+        gout[cols, :] = nn(mix[:, cols].T, ga[...]).astype(bf16)
+        return 0
+    lax.fori_loop(0, D // C, wout, 0)
+    def body(hp, _):
+        for row in range(T // SEQ):
+            attn_bwd_pair(q, k, v, gmix, km_marks, qm_marks, strips, far, lse, dq, dk, dv, tacc, facc, row, hp)
+        cols = pl.ds(pl.multiple_of(hp * 128, 128), 128)
+        for i, dd in enumerate((dq, dk, dv)):
+            gattn[i, :, cols] = nn(n1t[...], dd[:, cols]).astype(bf16)
+        return 0
+    lax.fori_loop(0, PAIRS, body, 0)
+    gn1sum[...] = jnp.zeros((1, D), f32)
+    def fin(c, _):
+        rows = pl.ds(pl.multiple_of(c * C, C), C)
+        gn = nt(dq[rows, :], wqkv[:, :D]) + nt(dk[rows, :], wqkv[:, D:2 * D]) + nt(dv[rows, :], wqkv[:, 2 * D:])
+        r = tokens[rows, :].astype(f32)
+        s = inv_rms(r)
+        gn1sum[...] += jnp.sum(gn * r * s, axis=0, keepdims=True)
+        gg = gn * gain[...]
+        gtok[rows, :] = gres[rows, :] + s * gg - r * (s * s * s * jnp.mean(gg * r, axis=-1, keepdims=True))
+        return 0
+    lax.fori_loop(0, T // C, fin, 0)
+
+def attn_bwd(tokens, gain, n1, wqkv, wo, mix, q, k, v, gres, km_marks, qm_marks, strips, lse, far):
+    T = tokens.shape[0]
+    return pl.pallas_call(attn_bwd_kernel,
+        out_shape=[sds(T, D, dtype=f32), sds(1, D, dtype=f32), sds(3, D, D), sds(D, D), sds(H, 3, 128, 128, dtype=f32), sds(H, 2, 8, 128, dtype=f32)],
+        in_specs=[VMEM] * 14 + [SMEM], out_specs=[VMEM] * 6,
+        scratch_shapes=[pltpu.VMEM((D, T), bf16)] + [pltpu.VMEM((T, D), bf16)] * 5,
+        compiler_params=pltpu.CompilerParams(vmem_limit_bytes=60 << 20),
+    )(tokens, gain.reshape(1, D).astype(f32), n1, wqkv, wo, mix, q, k, v, gres, km_marks, qm_marks, strips, lse, far)
+
+def table_grad(tacc, facc):
+    oh = strip_onehot().astype(f32)
+    g = jnp.dot(oh, tacc.reshape(H, -1).T, precision=lax.Precision.HIGHEST)
+    far = jnp.sum(facc, axis=(2, 3))
+    return g.at[15].add(far[:, 0]).at[31].add(far[:, 1])
 MESH_ID = pl.DeviceIdType.MESH
 RANKS = 32
 
@@ -244,7 +494,6 @@
 
 ORDERS = ("xy", "yx")
 ANY = pl.BlockSpec(memory_space=pl.ANY)
-VMEM = pl.BlockSpec(memory_space=pltpu.VMEM)
 FULL = (4, 2, 2, 2)
 
 
@@ -424,128 +673,22 @@
     w_ffn_out,
     cotangent,
 ):
-    row_count = tokens.shape[0] // SEQ
     gain_one, gain_two, full_attn, full_in, full_ffn = gather_weights(
         norm_gain, ffn_gain, (w_query, w_key, w_value, w_out), w_in, w_ffn_out
     )
-    full_query, full_key, full_value, full_out = jnp.split(full_attn, 4, axis=1)
-    bucket = bucket_index(SEQ).reshape(1, SEQ * SEQ)
-    onehot_flat = (bucket == jnp.arange(NB, dtype=jnp.int32)[:, None]).astype(jnp.bfloat16)
-    rel_bias = jnp.dot(
-        jnp.transpose(bias_table), onehot_flat, preferred_element_type=jnp.float32
-    ).reshape(H, SEQ, SEQ)
-    onehot = onehot_flat.reshape(NB, SEQ, SEQ)
-    seg_all = segment_ids(lengths, SEQ)
-    inputs = tokens.astype(jnp.float32)
-    normed_one = rms_norm(inputs, gain_one.astype(jnp.float32)).astype(jnp.bfloat16)
-    query_proj = project(normed_one, full_query).astype(jnp.bfloat16).reshape(row_count, SEQ, H, DH)
-    key_proj = project(normed_one, full_key).astype(jnp.bfloat16).reshape(row_count, SEQ, H, DH)
-    value_proj = project(normed_one, full_value).astype(jnp.bfloat16).reshape(row_count, SEQ, H, DH)
-
-    def scores_of(query_row, key_row, seg_row):
-        raw_scores = (
-            jnp.einsum("ihd,jhd->hij", query_row, key_row, preferred_element_type=jnp.float32)
-            + rel_bias
-        )
-        same_seg = seg_row[:, None] == seg_row[None, :]
-        return jnp.where(same_seg[None], raw_scores, -1e30)
-
-    def attend(row_items):
-        query_row, key_row, value_row, seg_row = row_items
-        scores = scores_of(query_row, key_row, seg_row)
-        row_peak = jnp.max(scores, axis=2, keepdims=True)
-        log_total = row_peak + jnp.log(jnp.sum(jnp.exp(scores - row_peak), axis=2, keepdims=True))
-        probs_low = jnp.exp(scores - log_total).astype(jnp.bfloat16)
-        attn_row = jnp.einsum(
-            "hij,jhd->ihd", probs_low, value_row, preferred_element_type=jnp.float32
-        )
-        return (attn_row.astype(jnp.bfloat16), log_total)
-
-    attn_mix, log_totals = lax.map(attend, (query_proj, key_proj, value_proj, seg_all))
-    attn_mix = attn_mix.reshape(-1, D)
-    residual = inputs + project(attn_mix, full_out)
-    normed_two = rms_norm(residual, gain_two.astype(jnp.float32)).astype(jnp.bfloat16)
-    ffn_inner = project(normed_two, full_in)
-    ffn_act = jax.nn.gelu(ffn_inner, approximate=False).astype(jnp.bfloat16)
-    output = (residual + project(ffn_act, full_ffn)).astype(jnp.bfloat16)
-    grad_output = cotangent.astype(jnp.float32)
-    grad_ffn = weight_grad(ffn_act, cotangent)
-    grad_act = project_back(cotangent, full_ffn)
-    gelu_value, gelu_pull = jax.vjp(partial(jax.nn.gelu, approximate=False), ffn_inner)
-    grad_inner = gelu_pull(grad_act)[0].astype(jnp.bfloat16)
-    grad_wide = weight_grad(normed_two, grad_inner)
-    grad_normed_two = project_back(grad_inner, full_in)
-    norm_value, norm_pull = jax.vjp(rms_norm, residual, gain_two.astype(jnp.float32))
-    grad_res_norm, grad_gain_two = norm_pull(grad_normed_two)
-    grad_residual = grad_output + grad_res_norm
-    grad_attn = grad_residual.astype(jnp.bfloat16)
-    grad_proj_out = weight_grad(attn_mix, grad_attn)
-    grad_mix = project_back(grad_attn, full_out).astype(jnp.bfloat16).reshape(row_count, SEQ, H, DH)
-
-    def attend_back(table_sum, row_items):
-        query_row, key_row, value_row, seg_row, log_total, grad_row = row_items
-        scores = scores_of(query_row, key_row, seg_row)
-        probabilities = jnp.exp(scores - log_total)
-        grad_values = jnp.einsum(
-            "hij,ihd->jhd",
-            probabilities.astype(jnp.bfloat16),
-            grad_row,
-            preferred_element_type=jnp.float32,
-        )
-        grad_probs = jnp.einsum(
-            "ihd,jhd->hij", grad_row, value_row, preferred_element_type=jnp.float32
-        )
-        inner_sum = jnp.sum(probabilities * grad_probs, axis=2, keepdims=True)
-        grad_scores = (probabilities * (grad_probs - inner_sum)).astype(jnp.bfloat16)
-        grad_queries = jnp.einsum(
-            "hij,jhd->ihd", grad_scores, key_row, preferred_element_type=jnp.float32
-        )
-        grad_keys = jnp.einsum(
-            "hij,ihd->jhd", grad_scores, query_row, preferred_element_type=jnp.float32
-        )
-        table_sum = table_sum + jnp.einsum(
-            "hij,bij->bh", grad_scores, onehot, preferred_element_type=jnp.float32
-        )
-        return (
-            table_sum,
-            (
-                grad_queries.astype(jnp.bfloat16),
-                grad_keys.astype(jnp.bfloat16),
-                grad_values.astype(jnp.bfloat16),
-            ),
-        )
-
-    table_start = jnp.zeros((NB, H), jnp.float32)
-    table_sum, grad_heads = lax.scan(
-        attend_back, table_start, (query_proj, key_proj, value_proj, seg_all, log_totals, grad_mix)
+    wqkv, wo = full_attn[:, : 3 * D], full_attn[:, 3 * D :]
+    km_marks, qm_marks = seg_marks(lengths)
+    strips = bias_strips(bias_table)
+    far = jnp.stack([bias_table[15], bias_table[31]], axis=1).astype(f32)
+    n1, q, k, v, mix, lse, resid, n2 = attn_fwd(tokens, gain_one, wqkv, wo, gain_two, km_marks, qm_marks, strips, far)
+    out, gres, g2, gin, gff = ffn(n2, cotangent, resid, gain_two, full_in, full_ffn)
+    gtok, g1, gat, gout, tacc, facc = attn_bwd(
+        tokens, gain_one, n1, wqkv, wo, mix, q, k, v, gres, km_marks, qm_marks, strips, lse, far
     )
-    grad_queries = grad_heads[0].reshape(-1, D)
-    grad_keys = grad_heads[1].reshape(-1, D)
-    grad_values = grad_heads[2].reshape(-1, D)
-    grad_proj_query = weight_grad(normed_one, grad_queries)
-    grad_proj_key = weight_grad(normed_one, grad_keys)
-    grad_proj_value = weight_grad(normed_one, grad_values)
-    grad_normed_one = (
-        project_back(grad_queries, full_query)
-        + project_back(grad_keys, full_key)
-        + project_back(grad_values, full_value)
-    )
-    first_value, first_pull = jax.vjp(rms_norm, inputs, gain_one.astype(jnp.float32))
-    grad_in_norm, grad_gain_one = first_pull(grad_normed_one)
-    grad_tokens = grad_residual + grad_in_norm
-    grad_attn_weights = jnp.concatenate([grad_proj_query, grad_proj_key, grad_proj_value, grad_proj_out], axis=1)
-    sums = reduce_grads(grad_attn_weights, grad_wide, grad_ffn, grad_gain_one, grad_gain_two, table_sum)
-    attn_sum, wide_sum, ffn_sum, gain_one_sum, gain_two_sum, table_total = sums
-    return (
-        output,
-        grad_tokens,
-        gain_one_sum,
-        *jnp.split(attn_sum, 4, axis=1),
-        table_total,
-        gain_two_sum,
-        wide_sum,
-        ffn_sum,
-    )
+    table = table_grad(tacc, facc)
+    gattn = jnp.concatenate([gat[0], gat[1], gat[2], gout], axis=1)
+    attn_sum, wide_sum, ffn_sum, g1s, g2s, table_total = reduce_grads(gattn, gin, gff, g1[0], g2[0], table)
+    return (out, gtok, g1s, *jnp.split(attn_sum, 4, axis=1), table_total, g2s, wide_sum, ffn_sum)
 
 
 def solution(mesh):

time: 584 us -> 393 us (0.67); the launches traced: 573 us -> 392 us
  matrix products: 200 us -> 4.35 us
  Pallas kernels: 185 us -> 329 us
  local copies, waits for them, and re-layouts: 150 us -> 30.6 us
  other arithmetic: 35.7 us -> 27.7 us
    dot_general x35 -> x2, matrix products: 200 us -> 4.35 us  [the longest x1 3.31 us: table_grad(): g = jnp.dot(oh, tacc.reshape(H, -1).T, precision=lax.Precision.HIGHEST)]
    pallas_call x0 -> x3, Pallas kernels: none -> 144 us  [the longest x1 53.1 us: attn_bwd(): pl.pallas_call(attn_bwd_kernel, out_shape=[sds(T, D, dtype=f32), sds(1, D...]
    convert_element_type x8 -> x2, local copies, waits for them, and re-layouts: 35.8 us -> 1.34 us  [the longest x1 0.67 us: attn_fwd(): gain2.reshape(1, D).astype(f32)]
    while x37 -> x0, local copies, waits for them, and re-layouts: 32.9 us -> none  [the longest x5 23.5 us: per_device(): lax.map(attend, (query_proj, key_proj, value_proj, seg_all))]
    unnamed x101 -> x34, local copies, waits for them, and re-layouts: 34.7 us -> 8.98 us
    reshape x5 -> x0, local copies, waits for them, and re-layouts: 20.3 us -> none  [the longest x1 10.6 us: per_device(): rel_bias = jnp.dot(jnp.transpose(bias_table), onehot_flat, preferred_elem...]
    convert_element_type x5, other arithmetic: 14.3 us -> 2.44 us  [the longest x2 1.81 us: seg_marks(): return (one.astype(bf16), jnp.where(one | ~keep, 0.0, -1e+30).astype(bf16))]
    concatenate x2 -> x5, other arithmetic: 4.93 us -> 14.7 us  [the longest x3 11.3 us: gather_weights(): jnp.concatenate([a.reshape(-1, a.shape[-1]), b.reshape(-1, b.shape[-1])],...]
where the time goes in v2:
time: 393 us; the launch traced here: 392 us
  Pallas kernels  329 us (84%)
  local copies, waits for them, and re-layouts  30.6 us (8%)
  other arithmetic  27.7 us (7%)
  matrix products  4.35 us (1%)
    pallas_call x1, Pallas kernels, reduce_grads(): pl.pallas_call(partial(reduce_kernel, count), out_shape=[jax.ShapeDtypeSt...  103 us
    pallas_call x1, Pallas kernels, gather_weights(): pl.pallas_call(partial(gather_kernel, count), out_shape=[jax.ShapeDtypeSt...  81.9 us
    pallas_call x1, Pallas kernels, attn_bwd(): pl.pallas_call(attn_bwd_kernel, out_shape=[sds(T, D, dtype=f32), sds(1, D...  53.1 us
    pallas_call x1, Pallas kernels, ffn(): pl.pallas_call(ffn_kernel, out_shape=[sds(T, D), sds(T, D, dtype=f32), sd...  52.9 us
    pallas_call x1, Pallas kernels, attn_fwd(): pl.pallas_call(attn_fwd_kernel, out_shape=[sds(T, D), sds(T, D), sds(T, D...  37.9 us
    concatenate x3, other arithmetic, gather_weights(): jnp.concatenate([a.reshape(-1, a.shape[-1]), b.reshape(-1, b.shape[-1])],...  11.3 us
    unnamed x34, local copies, waits for them, and re-layouts  8.98 us

profile of v2, /device:TPU:0, one launch (start us, length us, event | category | flops | bytes accessed | tf_op | source)
XLA Modules:
  0.0 392.2 jit_solution(14244573082947855647)
XLA Ops:
  0.6 1.6 fusion.18
  2.2 1.6 fusion.19
  3.8 1.5 pad_maximum_fusion.7
  6.6 81.9 %shard_map.203 = (bf16[4,2,2,2,16,128]{5,4,3,2,1,0:T(8,128)(2,1)}, bf16[4,2,2,2,24,1536]{5,4,3,2,1,0:T(8,128)(2,1)}, bf16[4,2,2,2,24,1536]{5,4,3,2,1,0:T(8,128)(...) custom-call(bf16[16,128]{1,0:T(8,128)(2,1)} %scatter.4.refs_0_, ...), custom_call_target="tpu_custom_call" | custom-call | tf_op jit(solution)/shard_map/pallas_call | solution.py:548
  88.5 4.2 %pad_maximum_fusion.2.wqkv = bf16[768,2304]{1,0:T(8,128)(2,1)} fusion(bf16[768,1536]{1,0:T(8,128)(2,1)} %bitcast.61, bf16[768,1536]{1,0:T(8,128)(2,1)} %bitcast.75), kind=kLoop, calls=%fused_computation.5 | loop fusion | flops 7077888 | bytes 8257536 | tf_op jit(solution)/shard_map/concatenate | solution.py:562
  92.7 1.1 slice.153.wo
  93.8 0.9 fusion.20
  96.5 1.0 fusion.1
  98.1 1.6 slice.159
  101.1 0.9 select_convert_fusion.qm_marks
  102.9 37.9 %shard_map.204 = (bf16[1024,768]{1,0:T(8,128)(2,1)}, bf16[1024,768]{1,0:T(8,128)(2,1)}, bf16[1024,768]{1,0:T(8,128)(2,1)}, bf16[1024,768]{1,0:T(8,128)(2,1)}, bf...) custom-call(bf16[1024,768]{1,0:T(8,128)(2,1)} %tokens.3, ...), custom_call_target="tpu_custom_call" | custom-call | tf_op jit(solution)/shard_map/pallas_call | solution.py:127
  140.8 4.6 %pad_maximum_fusion.win = bf16[768,3072]{1,0:T(8,128)(2,1)} fusion(bf16[768,1536]{1,0:T(8,128)(2,1)} %bitcast.74, bf16[768,1536]{1,0:T(8,128)(2,1)S(1)} %bitcast.73), kind=kLoop, calls=%fused_computation.3 | loop fusion | flops 9437184 | bytes 9437184 | tf_op jit(solution)/shard_map/concatenate | solution.py:562
  145.3 2.5 pad_maximum_fusion.1.wff
  147.8 52.9 %shard_map.205 = (bf16[1024,768]{1,0:T(8,128)(2,1)}, f32[1024,768]{1,0:T(8,128)}, f32[1,768]{1,0:T(1,128)}, bf16[768,3072]{1,0:T(8,128)(2,1)}, bf16[3072,768]{1,0:T(8,128)(2,1)}) custom-call(bf16[1024,768]{1,0:T(8,128)(2,1)} %get-tuple-element.83.n2, bf16[1024,768]{1,0:T(8,128)(2,1)} %cot.1, f32[1024,768]{1,0:T(8,128)} %get-tuple-element.84.resid, ...), custom_call_target="tpu_custom_call" | custom-call | tf_op jit(solution)/shard_map/pallas_call | solution.py:202
  200.8 53.1 %shard_map.206 = (f32[1024,768]{1,0:T(8,128)}, f32[1,768]{1,0:T(1,128)}, bf16[3,768,768]{2,1,0:T(8,128)(2,1)}, bf16[768,768]{1,0:T(8,128)(2,1)}, f32[12,3,128,128]{3,2,1,0:T(8,128)}, /*index=5*/f32[12,2,8,128]{3,2,1,0:T(8,128)}) custom-call(bf16[1024,768]{1,0:T(8,128)(2,1)} %tokens.3, f32[1,768]{1,0:T(1,128)} %reshape.301.gain, ...), custom_call_target="tpu_custom_call" | custom-call | tf_op jit(solution)/shard_map/pallas_call | solution.py:293
  253.8 1.9 pad.45
  255.8 1.8 copy.63
  257.6 3.3 fusion
  261.0 1.0 reduce_sum.19
  264.1 1.0 scatter-add.9
  268.9 1.0 copy-done.7
  269.9 1.7 pad_maximum_fusion.4.refs_1_
  271.6 1.7 pad_maximum_fusion.3.refs_0_
  273.3 2.8 fusion.14
  276.1 1.1 slice-done
  277.3 2.6 fusion.13
  279.9 102.9 %shard_map.207 = (f32[24,1536]{1,0:T(8,128)}, f32[24,1536]{1,0:T(8,128)}, f32[24,1536]{1,0:T(8,128)}, f32[24,1536]{1,0:T(8,128)}, f32[96,384]{1,0:T(8,128)}, /*index=5*/f32[96,384]{1,0:T(8,128)}, f32[16,128]{1,0:T(8,128)}) custom-call(bf16[4,2,2,2,24,1536]{5,4,3,2,1,0:T(8,128)(2,1)} %pad_maximum_fusion.3.refs_0_, ...), custom_call_target="tpu_custom_call" | custom-call | tf_op jit(solution)/shard_map/pallas_call | solution.py:634
  382.8 1.7 pad_maximum_fusion.6
  384.5 1.7 pad_maximum_fusion.5
  386.2 1.6 fusion.16
  387.8 1.6 fusion.17
  390.9 1.4 fusion.21
  (61 shorter events, 13.3 us)
Async XLA Ops:
  88.5 4.2 %copy-start = (bf16[4,2,2,2,24,1536]{5,4,3,2,1,0:T(8,128)(2,1)S(1)}, bf16[4,2,2,2,24,1536]{5,4,3,2,1,0:T(8,128)(2,1)}, u32[]{:S(2)}) copy-start(bf16[4,2,2,2,24,1536]{5,4,3,2,1,0:T(8,128)(2,1)} %get-tuple-element.82) | copy-start | bytes 7077892
  92.7 3.8 copy-start.8
  96.5 1.0 copy-start.2
  98.1 2.6 copy-start.9
  102.9 37.9 %copy-start.6 = (bf16[4,2,2,2,24,1536]{5,4,3,2,1,0:T(8,128)(2,1)S(1)}, bf16[4,2,2,2,24,1536]{5,4,3,2,1,0:T(8,128)(2,1)}, u32[]{:S(2)}) copy-start(bf16[4,2,2,2,24,1536]{5,4,3,2,1,0:T(8,128)(2,1)} %get-tuple-element.85) | copy-start | bytes 7077892
  140.8 4.6 %copy-start.4 = (bf16[4,2,2,2,96,384]{5,4,3,2,1,0:T(8,128)(2,1)S(1)}, bf16[4,2,2,2,96,384]{5,4,3,2,1,0:T(8,128)(2,1)}, u32[]{:S(2)}) copy-start(bf16[4,2,2,2,96,384]{5,4,3,2,1,0:T(8,128)(2,1)} %get-tuple-element.87) | copy-start | bytes 7077892
  140.8 4.6 %copy-start.5 = (bf16[4,2,2,2,96,384]{5,4,3,2,1,0:T(8,128)(2,1)S(1)}, bf16[4,2,2,2,96,384]{5,4,3,2,1,0:T(8,128)(2,1)}, u32[]{:S(2)}) copy-start(bf16[4,2,2,2,96,384]{5,4,3,2,1,0:T(8,128)(2,1)} %get-tuple-element.88) | copy-start | bytes 7077892
  255.8 1.9 copy-start.3
  257.6 11.0 %copy-start.1 = (bf16[3,768,768]{2,1,0:T(8,128)(2,1)S(1)}, bf16[3,768,768]{2,1,0:T(8,128)(2,1)}, u32[]{:S(2)}) copy-start(bf16[3,768,768]{2,1,0:T(8,128)(2,1)} %get-tuple-element.98) | copy-start | bytes 10616836
  268.6 1.3 copy-start.7
  268.6 4.7 %slice-start.2 = ((s8[4718592]{0:T(1024)(128)(4,1)}), s8[4194304]{0:T(1024)(128)(4,1)S(1)}, s32[]{:S(2)}) async-start(s8[4718592]{0:T(1024)(128)(4,1)} %bitcast.65), calls=%async_computation.2 | async-start | bytes 8388608
  269.9 3.4 slice-start.3
  273.3 3.9 slice-start
  273.3 4.0 %slice-start.1 = ((s8[4718592]{0:T(1024)(128)(4,1)}), s8[524288]{0:T(1024)(128)(4,1)S(1)}, s32[]{:S(2)}) async-start(s8[4718592]{0:T(1024)(128)(4,1)} %bitcast.63), calls=%async_computation.1 | async-start | bytes 1048576

commit v3 on v0

v3 whole, which is shorter than its diff:
```python
from functools import partial

import jax
import jax.numpy as jnp
from jax import lax
from jax.experimental import pallas as pl
from jax.experimental.pallas import tpu as pltpu
from jax.sharding import PartitionSpec as P

D = 768
H = 12
NB = 32
SEQ = 512
FF = 3072
EPSILON = 1e-6
CUTOFFS = (12, 16, 23, 32, 46, 64, 91)
RANKS = 32
GROUPS = 3
TILES = 4
TILE = 768
MESH_ID = pl.DeviceIdType.MESH
f32, bf16 = jnp.float32, jnp.bfloat16

GROUP_PIECE, OUT_PIECE, FFN_PIECE, IN_PIECE, PIECES = 0, 3, 4, 8, 12
ROWS, COLS = 48, 384


def nt(a, b):
    return lax.dot_general(a, b, (((1,), (1,)), ((), ())), preferred_element_type=f32)


def nn(a, b):
    return jnp.dot(a, b, preferred_element_type=f32)


def exact(a, b, dims=(((1,), (0,)), ((), ()))):
    return lax.dot_general(a, b, dims, precision=lax.Precision.HIGHEST, preferred_element_type=f32)


def part_of(index, size):
    return pl.ds(pl.multiple_of(index * size, size), size)


def place():
    me = lax.axis_index("dp")
    group = lax.axis_size("dp") // RANKS
    rank, low = me // group, me % group
    digits = dict(z=rank // 8, y=(rank // 4) % 2, x=(rank // 2) % 2, c=rank % 2)

    def device(**changed):
        d = {**digits, **changed}
        return ((((d["z"] * 2 + d["y"]) * 2 + d["x"]) * 2 + d["c"]) * group + low,)

    return digits, device


def partners(digits, device):
    line = [device(z=(digits["z"] + step) % 4) for step in (1, 2, 3)]
    return line + [device(**{axis: 1 - digits[axis]}) for axis in "yxc"]


def greet(digits, device):
    barrier = pltpu.get_barrier_semaphore()
    others = partners(digits, device)
    for other in others:
        pl.semaphore_signal(barrier, inc=1, device_id=other, device_id_type=MESH_ID)
    pl.semaphore_wait(barrier, len(others))


class Transfers:
    def __init__(self, send_sems, recv_sems, digits, device):
        self.send_sems, self.recv_sems, self.digits, self.device = send_sems, recv_sems, digits, device

    def flip(self, *axes):
        return {axis: 1 - self.digits[axis] for axis in axes}

    def copy(self, slot):
        source, target, device_id = self.spec(slot)
        return pltpu.make_async_remote_copy(
            src_ref=source,
            dst_ref=target,
            send_sem=self.send_sems.at[slot],
            recv_sem=self.recv_sems.at[slot],
            device_id=device_id,
            device_id_type=MESH_ID,
        )

    def go(self, *slots):
        for slot in slots:
            self.copy(slot).start()

    def arrived(self, *slots):
        for slot in slots:
            landing = self.landing(slot)
            pltpu.make_async_remote_copy(
                src_ref=landing,
                dst_ref=landing,
                send_sem=self.send_sems.at[slot],
                recv_sem=self.recv_sems.at[slot],
                device_id=self.device(c=1 - self.digits["c"]),
                device_id_type=MESH_ID,
            ).wait_recv()

    def sent(self, count):
        for slot in range(count):
            self.copy(slot).wait_send()


class Gather(Transfers):
    SLOTS = 10

    def __init__(self, full, send_sems, recv_sems, order, digits, device):
        super().__init__(send_sems, recv_sems, digits, device)
        self.full = full
        self.first, self.second = order

    def line_of(self, *flipped):
        d = {**self.digits, **self.flip(*flipped)}
        return self.full.at[:, d["y"], d["x"], d["c"]]

    def block_of(self, z):
        d = self.digits
        return self.full.at[z, d["y"], d["x"], d["c"]]

    def spec(self, slot):
        z, a, b = self.digits["z"], self.first, self.second
        if slot < 3:
            own = self.block_of(z)
            return own, own, self.device(z=(z + slot + 1) % 4)
        flipped, towards = ((), (), (), (a,), (a,), (b,), (b, a))[slot - 3], (a, b, "c", b, "c", "c", "c")[slot - 3]
        line = self.line_of(*flipped)
        return line, line, self.device(**self.flip(towards))

    def landing(self, slot):
        a, b = self.first, self.second
        if slot < 3:
            return self.block_of((self.digits["z"] + 3 - slot) % 4)
        return self.line_of(*((a,), (b,), ("c",), (b, a), ("c", a), ("c", b), ("c", b, a))[slot - 3])

    def start(self):
        self.go(0, 1, 2)

    def line(self):
        self.arrived(0, 1, 2)
        self.go(3, 4, 5)

    def across(self):
        self.arrived(3)
        self.go(6, 7)

    def along(self):
        self.arrived(4)
        self.go(8)
        self.arrived(6)
        self.go(9)

    def finish(self):
        self.arrived(5, 7, 8, 9)
        self.sent(self.SLOTS)


class Reduce(Transfers):
    SLOTS = 7

    def __init__(self, parts, received, send_sems, recv_sems, order, digits, device, credits=None, grants=None):
        super().__init__(send_sems, recv_sems, digits, device)
        self.parts = parts
        self.from_core, self.from_first, self.from_second, self.from_line = received
        self.first, self.second = order
        self.credits, self.grants = credits, grants

    def half(self, first, c):
        if self.first == "y":
            return self.parts.at[:, first, :, c]
        return self.parts.at[:, :, first, c]

    def at(self, z, first, second):
        d = {self.first: first, self.second: second}
        return (z, d["y"], d["x"], self.digits["c"])

    def spec(self, slot):
        d, a, b = self.digits, self.first, self.second
        if slot < 2:
            side = (1 - d[a], d[a])[slot]
            return self.half(side, 1 - d["c"]), self.from_core.at[slot], self.device(**self.flip("c"))
        if slot == 2:
            return self.half(1 - d[a], d["c"]), self.from_first, self.device(**self.flip(a))
        if slot == 3:
            q = {**d, **self.flip(b)}
            return self.parts.at[:, q["y"], q["x"], d["c"]], self.from_second, self.device(**self.flip(b))
        z = (d["z"] + slot - 3) % 4
        return self.parts.at[z, d["y"], d["x"], d["c"]], self.from_line.at[slot - 4], self.device(z=z)

    def landing(self, slot):
        if slot < 2:
            return self.from_core.at[slot]
        if slot < 4:
            return (self.from_first, self.from_second)[slot - 2]
        return self.from_line.at[slot - 4]

    def spend(self, *kinds):
        if self.credits is not None:
            for kind in kinds:
                pl.semaphore_wait(self.credits.at[kind], 1)

    def grant(self):
        d = self.digits
        if self.grants is not None:
            others = [self.device(**self.flip(axis)) for axis in ("c", self.first, self.second)]
            others += [self.device(z=(d["z"] + 4 - step) % 4) for step in (1, 2, 3)]
            for kind, other in enumerate(others):
                pl.semaphore_signal(self.grants.at[kind], inc=1, device_id=other, device_id_type=MESH_ID)

    def add(self, place_of, received, count):
        def body(i, carry):
            index = place_of(i)
            self.parts[index] = (self.parts[index].astype(f32) + received(i).astype(f32)).astype(bf16)
            return carry

        lax.fori_loop(0, count, body, 0)

    def start(self):
        self.spend(0)
        self.go(0, 1)

    def core(self):
        d, a = self.digits, self.first
        self.arrived(0)
        self.add(lambda i: self.at(i // 2, 1 - d[a], i % 2), lambda i: self.received_core(0, i), 8)
        self.spend(1)
        self.go(2)
        self.arrived(1)
        self.add(lambda i: self.at(i // 2, d[a], i % 2), lambda i: self.received_core(1, i), 8)

    def received_core(self, side, i):
        return self.from_core[side, i // 2, i % 2]

    def across(self):
        d, a, b = self.digits, self.first, self.second
        self.arrived(2)
        self.add(lambda i: self.at(i, d[a], 1 - d[b]), lambda i: self.from_first[i, 1 - d[b]], 4)
        self.spend(2)
        self.go(3)
        self.add(lambda i: self.at(i, d[a], d[b]), lambda i: self.from_first[i, d[b]], 4)

    def along(self):
        d, a, b = self.digits, self.first, self.second
        self.arrived(3)
        self.add(lambda i: self.at(i, d[a], d[b]), lambda i: self.from_second[i], 4)
        self.spend(3, 4, 5)
        self.go(4, 5, 6)

    def finish(self, store):
        d = self.digits
        total = self.parts[d["z"], d["y"], d["x"], d["c"]].astype(f32)
        for slot in (4, 5, 6):
            self.arrived(slot)
            total = total + self.from_line[slot - 4].astype(f32)
        store(total)
        self.sent(self.SLOTS)
        self.grant()


class SmallSum(Transfers):
    SLOTS = 6

    def __init__(self, total, buffer, send_sems, recv_sems, digits, device):
        super().__init__(send_sems, recv_sems, digits, device)
        self.total, self.buffer = total, buffer

    def spec(self, slot):
        z = self.digits["z"]
        if slot < 3:
            return self.buffer.at[2 * slot], self.buffer.at[2 * slot + 1], self.device(**self.flip("cxy"[slot]))
        mine = self.buffer.at[6 + z]
        return mine, mine, self.device(z=(z + slot - 2) % 4)

    def landing(self, slot):
        if slot < 3:
            return self.buffer.at[2 * slot + 1]
        return self.buffer.at[6 + (self.digits["z"] + 6 - slot) % 4]

    def start(self, slot):
        if slot < 3:
            self.buffer[2 * slot] = self.total[...]
            self.go(slot)
        else:
            self.buffer[6 + self.digits["z"]] = self.total[...]
            self.go(3, 4, 5)

    def finish(self, slot):
        if slot < 3:
            self.arrived(slot)
            self.total[...] = self.total[...] + self.buffer[2 * slot + 1]
        else:
            self.arrived(3, 4, 5)
            self.total[...] = (self.buffer[6] + self.buffer[7]) + (self.buffer[8] + self.buffer[9])
            self.sent(self.SLOTS)


def pack(block):
    rows = block.reshape(-1, 8, 2 * COLS)
    return jnp.concatenate([rows[:, :, :COLS], rows[:, :, COLS:]], axis=1).reshape(-1, COLS)


def unpack(block):
    rows = block.reshape(-1, 2, 8, COLS)
    return jnp.concatenate([rows[:, 0].reshape(-1, COLS), rows[:, 1].reshape(-1, COLS)], axis=1)


def unpack_piece(piece, target):
    def plane(z, carry):
        target[part_of(z, 192), :] = unpack(piece[z].astype(f32).reshape(8 * ROWS, COLS)).astype(bf16)
        return carry

    lax.fori_loop(0, 4, plane, 0)


def pack_piece(piece, z, grad):
    piece[z] = pack(grad).astype(bf16).reshape(2, 2, 2, ROWS, COLS)


def bucket_of(offsets):
    distance = jnp.abs(offsets)
    coarse = jnp.full_like(distance, 8)
    for cutoff in CUTOFFS:
        coarse = coarse + (distance >= cutoff).astype(jnp.int32)
    return jnp.where(distance < 8, distance, coarse) + jnp.where(offsets > 0, 16, 0)


def strip_onehot(shift):
    column = lax.broadcasted_iota(jnp.int32, (128, 512), 1)
    column = jnp.where(column >= shift, column - shift, column - shift + 512)
    offset = jnp.where(column < 384, 128 - column, 640 - column)
    return bucket_of(offset) == lax.broadcasted_iota(jnp.int32, (128, 512), 0)


def make_strips(table_t, strips):
    line = nn(table_t[...], strip_onehot(0).astype(bf16))
    for head in range(H):
        rows = jnp.broadcast_to(line[head : head + 1], (128, 512))
        strips[head] = pltpu.roll(rows, 0, 1, stride=1, stride_axis=0)[:, :384].astype(strips.dtype)


def strip_sums(strip):
    wide = jnp.concatenate([strip, jnp.zeros((128, 128), f32)], axis=1)
    total = wide[:8]
    for r in range(1, 16):
        total = total + pltpu.roll(wide[8 * r : 8 * r + 8], 512 - 8 * r, 1)
    return total


def table_sums(sums, far_sums):
    row = lax.broadcasted_iota(jnp.int32, (8 * H, 8 * H), 0)
    column = lax.broadcasted_iota(jnp.int32, (8 * H, 8 * H), 1)
    turned = exact((column == (row // 8) * 8 + 7 - row % 8).astype(f32), sums)
    lines = [
        jnp.sum(pltpu.roll(turned[8 * h : 8 * h + 8], 0, 1, stride=1, stride_axis=0), axis=0, keepdims=True)
        for h in range(H)
    ]
    lines.append(jnp.zeros((128 - H, 512), f32))
    table = exact(strip_onehot(7).astype(f32)[:NB], jnp.concatenate(lines, axis=0), (((1,), (1,)), ((), ())))
    bucket = lax.broadcasted_iota(jnp.int32, (NB, 128), 0)
    head = lax.broadcasted_iota(jnp.int32, (NB, 128), 1)
    for h in range(H):
        for side, index in ((0, 15), (1, 31)):
            total = jnp.sum(jnp.sum(far_sums[h, side], axis=0, keepdims=True), axis=1, keepdims=True)
            table = table + jnp.where((bucket == index) & (head == h), total, 0.0)
    return table


def make_marks(lengths, key_marks, query_marks):
    position = lax.broadcasted_iota(jnp.int32, (SEQ, 128), 0)
    lane = lax.broadcasted_iota(jnp.int32, (SEQ, 128), 1)
    for row in range(key_marks.shape[0] // SEQ):
        segment = jnp.zeros((SEQ, 128), jnp.int32)
        end = 0
        for k in range(1, 5):
            end = end + lengths[row, k]
            segment = segment + (position >= end).astype(jnp.int32)
        own = segment == lane
        rows = slice(row * SEQ, (row + 1) * SEQ)
        key_marks[rows, :] = jnp.where(own, 1.0, 0.0).astype(bf16)
        query_marks[rows, :] = jnp.where(own | (lane >= 5), 0.0, -1e30).astype(bf16)


def lane_mask(h):
    lane = lax.broadcasted_iota(jnp.int32, (1, 128), 1)
    return lane < 64 if h == 0 else lane >= 64


def scores_t(keys, queries, strip, low, high, half):
    raw = nt(keys, queries)
    rows = []
    for bj in range(4):
        blocks = []
        for bi in (0, 1):
            d = bj - bi - 2 * half
            block = raw[128 * bj : 128 * (bj + 1), 128 * bi : 128 * (bi + 1)]
            if d <= -2:
                block = block + low
            elif d >= 2:
                block = block + high
            else:
                block = block + strip[:, 128 * (1 - d) : 128 * (2 - d)].astype(f32)
            blocks.append(block)
        rows.append(jnp.concatenate(blocks, axis=1))
    return jnp.concatenate(rows, axis=0)


def heads_of(ref, rows, which, pair):
    return ref[rows, pl.ds(pl.multiple_of(which * 256 + pair * 128, 128), 128)]


def attend(qkv, key_marks, query_marks, strips, table, mix, lse, row, group, pair):
    rows = part_of(row, SEQ)
    q2, k2, v2 = (heads_of(qkv, rows, which, pair) for which in range(3))
    v2t = v2.T
    kmk, qmk = key_marks[rows, :], query_marks[rows, :]
    outs = []
    for h in range(2):
        head = (group * 2 + pair) * 2 + h
        keys = jnp.concatenate([jnp.where(lane_mask(h), k2, 0), kmk], axis=1)
        for half in range(2):
            span = slice(256 * half, 256 * half + 256)
            queries = jnp.concatenate([q2[span], qmk[span]], axis=1)
            scores = scores_t(keys, queries, strips[head], table[15, head], table[31, head], half)
            peak = jnp.max(scores, axis=0, keepdims=True)
            expo = jnp.exp(scores - peak)
            total = jnp.sum(expo, axis=0, keepdims=True)
            probs = (expo * (1.0 / total)).astype(bf16)
            lse[row, pl.ds(head, 1), span] = peak + jnp.log(total)
            outs.append(nn(v2t[64 * h : 64 * h + 64], probs))
    both = jnp.concatenate([jnp.concatenate(outs[:2], axis=1), jnp.concatenate(outs[2:], axis=1)], axis=0)
    mix[rows, part_of(group * 2 + pair, 128)] = both.T.astype(bf16)


def attend_back(qkv, gmix, key_marks, query_marks, strips, table, lse, strip_grads, far_sums, row, group, pair):
    rows = part_of(row, SEQ)
    q2, k2, v2 = (heads_of(qkv, rows, which, pair) for which in range(3))
    g2 = gmix[rows, part_of(group * 2 + pair, 128)]
    k2t = k2.T
    kmk, qmk = key_marks[rows, :], query_marks[rows, :]
    grad_v, grad_k, grad_q = 0.0, 0.0, []
    for h in range(2):
        head = (group * 2 + pair) * 2 + h
        mask = lane_mask(h)
        keys = jnp.concatenate([jnp.where(mask, k2, 0), kmk], axis=1)
        vm, qh, gh = jnp.where(mask, v2, 0), jnp.where(mask, q2, 0), jnp.where(mask, g2, 0)
        for half in range(2):
            span = slice(256 * half, 256 * half + 256)
            queries = jnp.concatenate([q2[span], qmk[span]], axis=1)
            scores = scores_t(keys, queries, strips[head], table[15, head], table[31, head], half)
            probs = jnp.exp(scores - lse[row, pl.ds(head, 1), span])
            grad_probs = nt(vm, g2[span])
            inner = jnp.sum(probs * grad_probs, axis=0, keepdims=True)
            grad = probs * (grad_probs - inner)
            low = grad.astype(bf16)
            grad_v = grad_v + nn(probs.astype(bf16), gh[span])
            grad_k = grad_k + nn(low, qh[span])
            grad_q.append(nn(k2t[64 * h : 64 * h + 64], low))
            strip_rows, strip_base = part_of(group * 2 + pair, 128), 384 * h
            for bi in (0, 1):
                far = [[], []]
                for bj in range(4):
                    d = bj - bi - 2 * half
                    block = grad[128 * bj : 128 * (bj + 1), 128 * bi : 128 * (bi + 1)]
                    if abs(d) <= 1:
                        span_d = slice(strip_base + 128 * (1 - d), strip_base + 128 * (2 - d))
                        strip_grads[strip_rows, span_d] += block
                    else:
                        far[d > 0].append(jnp.sum(block.reshape(16, 8, 128), axis=0))
                for side in (0, 1):
                    if far[side]:
                        far_sums[head, side] += sum(far[side][1:], far[side][0])
    qt = jnp.concatenate([jnp.concatenate(grad_q[:2], axis=1), jnp.concatenate(grad_q[2:], axis=1)], axis=0)
    for which, value in enumerate((qt.T, grad_k, grad_v)):
        qkv[rows, pl.ds(pl.multiple_of(which * 256 + pair * 128, 128), 128)] = value.astype(bf16)


def inv_rms(x):
    return lax.rsqrt(jnp.mean(x * x, axis=-1, keepdims=True) + EPSILON)


def norm_back(grad, x, gain):
    s = inv_rms(x)
    gg = grad * gain
    return s * gg - x * (s * s * s * jnp.mean(gg * x, axis=-1, keepdims=True)), jnp.sum(grad * x * s, axis=0, keepdims=True)


def gelu_both(x):
    cdf = 0.5 + 0.5 * lax.erf(x * 0.7071067811865476)
    return x * cdf, cdf + x * (jnp.exp(x * x * -0.5) * 0.3989422804014327)


def gain_line(gains, which):
    blocks = gains[...].reshape(8 * RANKS, 128).astype(bf16)
    lane = lax.broadcasted_iota(jnp.int32, (128, D), 1)
    spread = nn(blocks, (lane % 24 == lax.broadcasted_iota(jnp.int32, (128, D), 0)).astype(bf16))
    row = lax.broadcasted_iota(jnp.int32, (8 * RANKS, D), 0)
    column = lax.broadcasted_iota(jnp.int32, (8 * RANKS, D), 1)
    return jnp.sum(jnp.where(row == (column // 24) * 8 + which, spread, 0.0), axis=0, keepdims=True)


def run_at(step, plan):
    for when, stages in plan.items():

        @pl.when(step == when)
        def _(stages=stages):
            for stage in stages:
                stage()


def layer_kernel(
    tokens, cot_hbm, lengths, norm_gain, ffn_gain, w_query, w_key, w_value, w_out, w_in, w_ffn, table, table_t,
    out_hbm, gtok_hbm, grad_q, grad_k, grad_v, grad_o, grad_in, grad_ffn, small,
    pieces, gains, weights, win, wff, qkv, mix, normed, turned, cot, cot_t, resid, out_sum, grad_sum, act, grad_inner,
    strips, key_marks, query_marks, lse, far_sums, diagonals, from_core, from_first, from_second, from_line, small_buffer,
    gather_send, gather_recv, gain_send, gain_recv, reduce_send, reduce_recv, small_send, small_recv, credits, local_sems,
):
    count = tokens.shape[0]
    halves = count // SEQ
    digits, device = place()
    me = (digits["z"], digits["y"], digits["x"], digits["c"])

    load_cot = pltpu.make_async_copy(cot_hbm, cot, local_sems.at[0])
    load_cot.start()

    gains[me] = jnp.zeros((8, 128), f32)
    gains[(*me, slice(0, 1), slice(0, 24))] = norm_gain[...].astype(f32)
    gains[(*me, slice(1, 2), slice(0, 24))] = ffn_gain[...].astype(f32)
    for g in range(GROUPS):
        span = slice(256 * g, 256 * g + 256)
        block = jnp.concatenate([w[:, span] for w in (w_query, w_key, w_value)], axis=1)
        pieces[(GROUP_PIECE + g, *me)] = pack(block.astype(f32)).astype(bf16)
    pieces[(OUT_PIECE, *me)] = pack(w_out[...].astype(f32)).astype(bf16)
    for i in range(4):
        pieces[(FFN_PIECE + i, *me)] = w_ffn[ROWS * (i // 2) : ROWS * (i // 2 + 1), COLS * (i % 2) : COLS * (i % 2 + 1)]
        pieces[(IN_PIECE + i, *me)] = pack(w_in[:, TILE * i : TILE * (i + 1)].astype(f32)).astype(bf16)

    greet(digits, device)
    orders = ("xy", "yx")
    gain_gather = Gather(gains, gain_send, gain_recv, "xy", digits, device)
    gathers = [
        Gather(pieces.at[i], gather_send.at[i], gather_recv.at[i], orders[i % 2], digits, device) for i in range(PIECES)
    ]
    order = [IN_PIECE + t for t in range(4)] + [FFN_PIECE + i for i in range(4)] + [OUT_PIECE] + [0, 1, 2]
    reduces = []
    for n, i in enumerate(order):
        slot = n if n < 8 else n - 8
        received = (from_core.at[slot], from_first.at[slot], from_second.at[slot], from_line.at[slot])
        reduces.append(
            Reduce(
                pieces.at[i],
                received,
                reduce_send.at[n],
                reduce_recv.at[n],
                orders[n % 2],
                digits,
                device,
                credits=credits.at[slot] if n >= 8 else None,
                grants=credits.at[slot] if n < 4 else None,
            )
        )

    def store_in(t):
        def store(total):
            grad_in[:, TILE * t : TILE * (t + 1)] = unpack(total)

        return store

    def store_ffn(i):
        def store(total):
            grad_ffn[ROWS * (i // 2) : ROWS * (i // 2 + 1), COLS * (i % 2) : COLS * (i % 2 + 1)] = total

        return store

    def store_out(total):
        grad_o[...] = unpack(total)

    def store_group(g):
        def store(total):
            block = unpack(total)
            for which, target in enumerate((grad_q, grad_k, grad_v)):
                target[:, 256 * g : 256 * (g + 1)] = block[:, 256 * which : 256 * (which + 1)]

        return store

    stores = [store_in(t) for t in range(4)] + [store_ffn(i) for i in range(4)] + [store_out]
    stores += [store_group(g) for g in range(3)]

    def gather_wave(k):
        stages = []
        if k < PIECES:
            stages.append(gathers[k].line)
        if 0 <= k - 1 < PIECES:
            stages.append(gathers[k - 1].across)
        if 0 <= k - 2 < PIECES:
            stages.append(gathers[k - 2].along)
        if 0 <= k - 3 < PIECES:
            stages.append(gathers[k - 3].finish)
            if k - 3 < FFN_PIECE:
                stages.append(partial(unpack_piece, pieces.at[k - 3], weights.at[k - 3]))
        return stages

    def reduce_wave(k):
        stages = []
        if k < PIECES:
            stages.append(reduces[k].core)
        if 0 <= k - 1 < PIECES:
            stages.append(reduces[k - 1].across)
        if 0 <= k - 2 < PIECES:
            stages.append(reduces[k - 2].along)
        if 0 <= k - 3 < PIECES:
            stages.append(partial(reduces[k - 3].finish, stores[k - 3]))
        return stages

    def run(stages):
        for stage in stages:
            stage()

    gain_gather.start()
    for gather in gathers:
        gather.start()
    make_marks(lengths, key_marks, query_marks)
    make_strips(table_t, strips)
    gain_gather.line()
    gain_gather.across()
    gain_gather.along()
    run(gather_wave(0))
    gain_gather.finish()
    gain_one, gain_two = gain_line(gains, 0), gain_line(gains, 1)

    def norm_one(i, carry):
        rows = part_of(i, 256)
        x = tokens[rows, :].astype(f32)
        normed[rows, :] = (x * inv_rms(x) * gain_one).astype(bf16)
        return carry

    lax.fori_loop(0, count // 256, norm_one, 0)
    for k in (1, 2, 3):
        run(gather_wave(k))

    steps = 2 * halves
    forward_plan = {0: gather_wave(4), 2: gather_wave(5), 4: gather_wave(6), 6: gather_wave(7), 8: gather_wave(8), 10: gather_wave(9)}

    def forward_group(g, carry):
        def project(i, carry):
            rows = part_of(i, 256)
            qkv[g, rows, :] = nn(normed[rows, :], weights[GROUP_PIECE + g]).astype(bf16)
            return carry

        lax.fori_loop(0, count // 256, project, 0)

        def forward(s, carry):
            attend(qkv.at[g], key_marks, query_marks, strips, table, mix, lse, s % halves, g, s // halves)
            run_at(g * steps + s, forward_plan)
            return carry

        lax.fori_loop(0, steps, forward, 0)
        return carry

    lax.fori_loop(0, GROUPS, forward_group, 0)

    load_cot.wait()

    def after_attention(i, carry):
        rows = part_of(i, 256)
        r = tokens[rows, :].astype(f32) + nn(mix[rows, :], weights[OUT_PIECE])
        resid[rows, :] = r
        n = (r * inv_rms(r) * gain_two).astype(bf16)
        turned[:, rows] = n.T
        normed[rows, :] = n
        cot_t[:, rows] = cot[rows, :].T
        return carry

    lax.fori_loop(0, count // 256, after_attention, 0)
    run(gather_wave(10))
    run(gather_wave(11))

    ffn_plan = {
        1: gather_wave(12),
        3: gather_wave(13),
        5: gather_wave(14),
        6: [reduces[0].core],
        7: [reduces[0].across],
        8: [reduces[0].along],
        9: [partial(reduces[0].finish, stores[0])],
        11: [reduces[1].core],
        12: [reduces[1].across],
        13: [reduces[1].along],
        14: [partial(reduces[1].finish, stores[1])],
        16: [reduces[2].core],
        17: [reduces[2].across],
        18: [reduces[2].along],
        19: [partial(reduces[2].finish, stores[2])],
    }
    width = 256

    def ffn_tile(t, carry):
        unpack_piece(pieces.at[IN_PIECE + t], win)
        for i in range(4):
            blocks = pieces[FFN_PIECE + i, t].reshape(8, ROWS, COLS)
            for b in range(8):
                rows = slice(96 * b + ROWS * (i // 2), 96 * b + ROWS * (i // 2 + 1))
                wff[rows, COLS * (i % 2) : COLS * (i % 2 + 1)] = blocks[b]

        def columns(w, carry):
            span = part_of(w, width)

            def chunk(i, carry):
                rows = part_of(i, 512)
                inner = nn(normed[rows, :], win[:, span])
                grad_act = nt(cot[rows, :], wff[span, :])
                value, slope = gelu_both(inner)
                act[rows, span] = value.astype(bf16)
                grad_inner[rows, span] = (slope * grad_act).astype(bf16)
                return carry

            lax.fori_loop(0, count // 512, chunk, 0)
            run_at(5 * t + w, ffn_plan)
            return carry

        lax.fori_loop(0, TILE // width, columns, 0)

        def sums(i, carry):
            rows = part_of(i, 512)
            o = nn(act[rows, :], wff[...])
            gn = nt(grad_inner[rows, :], win[...])

            @pl.when(t == 0)
            def _():
                out_sum[rows, :] = resid[rows, :] + o
                grad_sum[rows, :] = gn

            @pl.when(t > 0)
            def _():
                out_sum[rows, :] += o
                grad_sum[rows, :] += gn

            return carry

        lax.fori_loop(0, count // 512, sums, 0)
        run_at(5 * t + 3, ffn_plan)

        def grads_in(z, carry):
            pack_piece(pieces.at[IN_PIECE + t], z, nn(turned[part_of(z, 192), :], grad_inner[...]))
            return carry

        lax.fori_loop(0, 4, grads_in, 0)
        run_at(t, {k: [reduces[k].start] for k in range(TILES)})

        for ch in range(2):
            grad = nn(cot_t[COLS * ch : COLS * (ch + 1), :], act[...]).astype(bf16).T
            for b in range(8):
                for rh in range(2):
                    pieces[FFN_PIECE + 2 * rh + ch, t, b // 4, (b // 2) % 2, b % 2] = grad[
                        96 * b + ROWS * rh : 96 * b + ROWS * (rh + 1)
                    ]
        run_at(5 * t + 4, ffn_plan)
        return carry

    lax.fori_loop(0, TILES, ffn_tile, 0)
    for n in range(4, 8):
        reduces[n].start()

    small[...] = jnp.zeros(small.shape, f32)

    def spread_line(row, line):
        for j in range(D // 128):
            small[row + j : row + j + 1, :] += line[:, 128 * j : 128 * (j + 1)]

    def before_back(i, carry):
        rows = part_of(i, 256)
        act[rows, :] = out_sum[rows, :].astype(bf16)
        r = resid[rows, :]
        into, gain_sum = norm_back(grad_sum[rows, :], r, gain_two)
        spread_line(6, gain_sum)
        grad = cot[rows, :].astype(f32) + into
        grad_sum[rows, :] = grad
        low = grad.astype(bf16)
        cot[rows, :] = low
        normed[rows, :] = nt(low, weights[OUT_PIECE]).astype(bf16)
        x = tokens[rows, :].astype(f32)
        turned[:, rows] = (x * inv_rms(x) * gain_one).astype(bf16).T
        return carry

    lax.fori_loop(0, count // 256, before_back, 0)
    store_output = pltpu.make_async_copy(act, out_hbm, local_sems.at[1])
    store_output.start()
    out_sum[...] = jnp.zeros(out_sum.shape, f32)
    far_sums[...] = jnp.zeros(far_sums.shape, f32)
    run(reduce_wave(3)[:1])

    for z in range(4):
        pack_piece(pieces.at[OUT_PIECE], z, nn(mix[:, 192 * z : 192 * (z + 1)].T, cot[...]))

    def wave(core=None, across=None, along=None, finish=None, start=None):
        stages = []
        if start is not None:
            stages.append(reduces[start].start)
        if core is not None:
            stages.append(reduces[core].core)
        if across is not None:
            stages.append(reduces[across].across)
        if along is not None:
            stages.append(reduces[along].along)
        if finish is not None:
            stages.append(partial(reduces[finish].finish, stores[finish]))
        return stages

    back_plan = {
        0: wave(core=4, across=3),
        1: wave(core=5, across=4, along=3),
        2: wave(core=6, across=5, along=4, finish=3, start=8),
        3: wave(core=7, across=6, along=5, finish=4),
        4: wave(core=8, across=7, along=6, finish=5),
        5: wave(across=8, along=7, finish=6, core=9),
        6: wave(along=8, finish=7, across=9),
        7: wave(finish=8, along=9),
        8: wave(finish=9),
        9: wave(core=10),
        10: wave(across=10),
        11: wave(along=10),
    }

    def back_group(g, carry):
        def back(s, carry):
            attend_back(
                qkv.at[g], normed, key_marks, query_marks, strips, table, lse, out_sum, far_sums, s % halves, g, s // halves
            )
            run_at(g * steps + s, back_plan)
            return carry

        lax.fori_loop(0, steps, back, 0)

        def grads(z, carry):
            pack_piece(pieces.at[GROUP_PIECE + g], z, nn(turned[part_of(z, 192), :], qkv[g]))
            return carry

        lax.fori_loop(0, 4, grads, 0)
        run_at(g, {k: [reduces[9 + k].start] for k in range(GROUPS)})
        return carry

    lax.fori_loop(0, GROUPS, back_group, 0)

    last_plan = {0: wave(core=11, finish=10), 2: wave(across=11)}

    def last(i, carry):
        rows = part_of(i, 256)
        grad = nt(qkv[0, rows, :], weights[0]) + nt(qkv[1, rows, :], weights[1]) + nt(qkv[2, rows, :], weights[2])
        into, gain_sum = norm_back(grad, tokens[rows, :].astype(f32), gain_one)
        spread_line(0, gain_sum)
        grad_sum[rows, :] = grad_sum[rows, :] + into
        run_at(i, last_plan)
        return carry

    lax.fori_loop(0, count // 256, last, 0)
    store_gtok = pltpu.make_async_copy(grad_sum, gtok_hbm, local_sems.at[2])
    store_gtok.start()
    for pair in range(H // 2):
        for h in range(2):
            head = 2 * pair + h
            diagonals[8 * head : 8 * head + 8, :] = strip_sums(out_sum[128 * pair : 128 * pair + 128, 384 * h : 384 * h + 384])
    small[16:48, :] = table_sums(diagonals[...], far_sums)
    sums = SmallSum(small, small_buffer, small_send, small_recv, digits, device)
    sums.start(0)
    reduces[11].along()
    sums.finish(0)
    sums.start(1)
    sums.finish(1)
    sums.start(2)
    reduces[11].finish(stores[11])
    sums.finish(2)
    sums.start(3)
    sums.finish(3)
    store_output.wait()
    store_gtok.wait()


def inner_groups():
    total = lax.axis_size("dp")
    group = total // RANKS
    return group, [list(range(i * group, (i + 1) * group)) for i in range(RANKS)]


def widen(block):
    group, groups = inner_groups()
    if group == 1:
        return block
    return lax.all_gather(block, "dp", axis=0, tiled=True, axis_index_groups=groups)


def narrow(block):
    group, groups = inner_groups()
    if group == 1:
        return block
    return lax.psum_scatter(block, "dp", scatter_dimension=0, tiled=True, axis_index_groups=groups)


def per_device(
    tokens, lengths, norm_gain, w_query, w_key, w_value, w_out, bias_table, ffn_gain, w_in, w_ffn_out, cotangent
):
    count = tokens.shape[0]
    norm_gain, ffn_gain, w_query, w_key, w_value, w_out, w_in, w_ffn_out = (
        widen(w) for w in (norm_gain, ffn_gain, w_query, w_key, w_value, w_out, w_in, w_ffn_out)
    )
    table_t = jnp.pad(bias_table.T, ((0, 4), (0, 128 - NB)))
    any_space = pl.BlockSpec(memory_space=pl.ANY)
    vmem = pl.BlockSpec(memory_space=pltpu.VMEM)
    smem = pl.BlockSpec(memory_space=pltpu.SMEM)
    full = (4, 2, 2, 2)
    out = jax.ShapeDtypeStruct
    outs = pl.pallas_call(
        layer_kernel,
        out_shape=[out((count, D), bf16), out((count, D), f32)]
        + [out((24, D), f32)] * 4
        + [out((24, FF), f32), out((96, D), f32), out((48, 128), f32)],
        in_specs=[vmem, any_space, smem] + [vmem] * 8 + [smem, vmem],
        out_specs=[any_space] * 2 + [vmem] * 7,
        scratch_shapes=[
            pltpu.VMEM((PIECES,) + full + (ROWS, COLS), bf16),
            pltpu.VMEM(full + (8, 128), f32),
            pltpu.VMEM((4, D, D), bf16),
            pltpu.VMEM((D, TILE), bf16),
            pltpu.VMEM((TILE, D), bf16),
            pltpu.VMEM((GROUPS, count, D), bf16),
            pltpu.VMEM((count, D), bf16),
            pltpu.VMEM((count, D), bf16),
            pltpu.VMEM((D, count), bf16),
            pltpu.VMEM((count, D), bf16),
            pltpu.VMEM((D, count), bf16),
            pltpu.VMEM((count, D), f32),
            pltpu.VMEM((count, D), f32),
            pltpu.VMEM((count, D), f32),
            pltpu.VMEM((count, TILE), bf16),
            pltpu.VMEM((count, TILE), bf16),
            pltpu.VMEM((H, 128, 384), bf16),
            pltpu.VMEM((count, 128), bf16),
            pltpu.VMEM((count, 128), bf16),
            pltpu.VMEM((count // SEQ, H, SEQ), f32),
            pltpu.VMEM((H, 2, 8, 128), f32),
            pltpu.VMEM((8 * H, 512), f32),
            pltpu.VMEM((8, 2, 4, 2, ROWS, COLS), bf16),
            pltpu.VMEM((8, 4, 2, ROWS, COLS), bf16),
            pltpu.VMEM((8, 4, ROWS, COLS), bf16),
            pltpu.VMEM((8, 3, ROWS, COLS), bf16),
            pltpu.VMEM((10, 48, 128), f32),
            pltpu.SemaphoreType.DMA((PIECES, Gather.SLOTS)),
            pltpu.SemaphoreType.DMA((PIECES, Gather.SLOTS)),
            pltpu.SemaphoreType.DMA((Gather.SLOTS,)),
            pltpu.SemaphoreType.DMA((Gather.SLOTS,)),
            pltpu.SemaphoreType.DMA((PIECES, Reduce.SLOTS)),
            pltpu.SemaphoreType.DMA((PIECES, Reduce.SLOTS)),
            pltpu.SemaphoreType.DMA((SmallSum.SLOTS,)),
            pltpu.SemaphoreType.DMA((SmallSum.SLOTS,)),
            pltpu.SemaphoreType.REGULAR((4, 6)),
            pltpu.SemaphoreType.DMA((3,)),
        ],
        compiler_params=pltpu.CompilerParams(collective_id=1, has_side_effects=True, vmem_limit_bytes=63 << 20),
    )(
        tokens,
        cotangent,
        lengths,
        norm_gain.reshape(1, -1),
        ffn_gain.reshape(1, -1),
        w_query,
        w_key,
        w_value,
        w_out,
        w_in,
        w_ffn_out,
        bias_table.astype(f32),
        table_t,
    )
    output, grad_tokens, grad_q, grad_k, grad_v, grad_o, grad_in, grad_ffn, small = outs
    group, groups = inner_groups()
    if group > 1:
        small = lax.psum(small, "dp", axis_index_groups=groups)
    each = D // lax.axis_size("dp")
    start = lax.axis_index("dp") * each
    grad_norm_gain = lax.dynamic_slice(small[:6].reshape(-1), (start,), (each,))
    grad_ffn_gain = lax.dynamic_slice(small[6:12].reshape(-1), (start,), (each,))
    return (
        output,
        grad_tokens,
        grad_norm_gain,
        narrow(grad_q),
        narrow(grad_k),
        narrow(grad_v),
        narrow(grad_o),
        small[16:48, :H],
        grad_ffn_gain,
        narrow(grad_in),
        narrow(grad_ffn),
    )


def solution(mesh):
    rows, whole = P("dp", None), P("dp")
    return jax.shard_map(
        per_device,
        mesh=mesh,
        in_specs=(rows, rows, whole, rows, rows, rows, rows, P(), whole, rows, rows, rows),
        out_specs=(rows, rows, whole, rows, rows, rows, rows, P(), whole, rows, rows),
        check_vma=False,
    )
```

time: 1160 us -> 256 us (0.22)
  waiting for transfers between devices: 635 us -> 0 us
  Pallas kernels: 0 us -> 240 us
  matrix products: 232 us -> 0 us
  local copies, waits for them, and re-layouts: 155 us -> 14.4 us
  blocking collectives: 82.3 us -> 0 us
  other arithmetic: 35.1 us -> 0 us
  between operations: 14.9 us -> 0.69 us
    reduce_scatter x6 -> x0, waiting for transfers between devices: 480 us -> none  [the longest x1 142 us: per_device(): lax.psum_scatter(grad_ffn, 'dp', scatter_dimension=0, tiled=True)]
    pallas_call x0 -> x1, Pallas kernels: none -> 240 us  [per_device(): pl.pallas_call(layer_kernel, out_shape=[out((count, D), bf16), out((count...]
    dot_general x35 -> x0, matrix products: 232 us -> none  [the longest x6 64.5 us: project(): return jnp.dot(left, right, preferred_element_type=jnp.float32)]
    all_gather x6 -> x0, waiting for transfers between devices: 151 us -> none  [the longest x1 59.8 us: per_device(): lax.all_gather(w_in, 'dp', axis=0, tiled=True)]
    unnamed x2 -> x0, blocking collectives: 82.3 us -> none
    while x88 -> x0, local copies, waits for them, and re-layouts: 42.4 us -> none  [the longest x5 22.2 us: per_device(): lax.map(attend, (query_proj, key_proj, value_proj, seg_all))]
    unnamed x94 -> x23, local copies, waits for them, and re-layouts: 49.1 us -> 9.13 us
    convert_element_type x6 -> x1, local copies, waits for them, and re-layouts: 36.8 us -> 1.38 us  [per_device(): bias_table.astype(f32)]
  transfers between devices with their start and end apart: 12 -> 0, of which waited for: 9 -> 0; matrix products, arithmetic and copies ran while one was open for 32% -> 0% of each run, Pallas kernels for 0% -> 0%
where the time goes in v3:
time: 256 us
  Pallas kernels  240 us (94%)
  local copies, waits for them, and re-layouts  14.4 us (6%)
    pallas_call x1, Pallas kernels, per_device(): pl.pallas_call(layer_kernel, out_shape=[out((count, D), bf16), out((count...  240 us
    unnamed x23, local copies, waits for them, and re-layouts  9.13 us

profile of v3, /device:TPU:0, one launch (start us, length us, event | category | flops | bytes accessed | tf_op | source)
XLA Modules:
  0.0 255.5 jit_solution(4970746114438585288)
XLA Ops:
  0.6 1.3 pad.4.table_t
  1.9 1.4 copy.25.table
  3.3 240.4 %shard_map.203 = (bf16[1024,768]{1,0:T(8,128)(2,1)}, f32[1024,768]{1,0:T(8,128)}, f32[24,768]{1,0:T(8,128)}, f32[24,768]{1,0:T(8,128)}, f32[24,768]{1,0:T(8,128)...) custom-call(bf16[1024,768]{1,0:T(8,128)(2,1)} %tokens.1, ...), custom_call_target="tpu_custom_call" | custom-call | tf_op jit(solution)/shard_map/pallas_call | solution.py:914
  243.7 0.8 slice_bitcast_fusion
  244.5 0.7 slice.10
  245.2 0.7 copy.26
  245.9 0.6 dynamic_slice.7
  246.5 0.6 dynamic_slice.6
  247.1 0.0 copy-start
  247.1 2.8 %copy.35 = bf16[1024,768]{1,0:T(8,128)(2,1)} copy(bf16[1024,768]{1,0:T(8,128)(2,1)} %get-tuple-element.64) | data formatting | bytes 3145728
  249.9 0.0 copy-done
  249.9 0.0 copy-start.6
  249.9 0.0 copy-start.5
  249.9 0.0 copy-start.4
  249.9 0.0 copy-start.3
  249.9 0.0 copy-start.2
  249.9 0.0 copy-start.1
  249.9 1.7 copy.36
  251.6 0.0 copy-done.6
  251.6 0.6 copy.37
  252.2 0.0 copy-done.5
  252.2 0.6 copy.38
  252.8 0.0 copy-done.4
  252.8 0.6 copy.39
  253.5 0.0 copy-done.3
  253.5 0.6 copy.40
  254.1 0.0 copy-done.2
  254.1 0.7 copy.41
  254.8 0.0 copy-done.1
  254.8 0.7 copy.42
Async XLA Ops:
  247.1 2.8 %copy-start = (f32[1024,768]{1,0:T(8,128)S(1)}, f32[1024,768]{1,0:T(8,128)}, u32[]{:S(2)}) copy-start(f32[1024,768]{1,0:T(8,128)} %get-tuple-element.65) | copy-start | bytes 9437188
  249.9 1.7 copy-start.6
  249.9 2.3 copy-start.5
  249.9 3.0 %copy-start.4 = (f32[24,768]{1,0:T(8,128)S(1)}, f32[24,768]{1,0:T(8,128)}, u32[]{:S(2)}) copy-start(f32[24,768]{1,0:T(8,128)} %get-tuple-element.69) | copy-start | bytes 221188
  249.9 3.6 %copy-start.3 = (f32[24,768]{1,0:T(8,128)S(1)}, f32[24,768]{1,0:T(8,128)}, u32[]{:S(2)}) copy-start(f32[24,768]{1,0:T(8,128)} %get-tuple-element.70) | copy-start | bytes 221188
  249.9 4.2 %copy-start.2 = (f32[24,3072]{1,0:T(8,128)S(1)}, f32[24,3072]{1,0:T(8,128)}, u32[]{:S(2)}) copy-start(f32[24,3072]{1,0:T(8,128)} %get-tuple-element.73) | copy-start | bytes 884740
  249.9 4.9 %copy-start.1 = (f32[96,768]{1,0:T(8,128)S(1)}, f32[96,768]{1,0:T(8,128)}, u32[]{:S(2)}) copy-start(f32[96,768]{1,0:T(8,128)} %get-tuple-element.74) | copy-start | bytes 884740

commit v4 on v3

v4 whole, which is shorter than its diff:
```python
from functools import partial

import jax
import jax.numpy as jnp
from jax import lax
from jax.experimental import pallas as pl
from jax.experimental.pallas import tpu as pltpu
from jax.sharding import PartitionSpec as P

D = 768
H = 12
NB = 32
SEQ = 512
FF = 3072
EPSILON = 1e-6
CUTOFFS = (12, 16, 23, 32, 46, 64, 91)
RANKS = 32
GROUPS = 3
TILES = 4
TILE = 768
MESH_ID = pl.DeviceIdType.MESH
f32, bf16 = jnp.float32, jnp.bfloat16

GROUP_PIECE, OUT_PIECE, PIECES = 0, 3, 12
FFN_PIECES, IN_PIECES = (4, 6, 8, 10), (5, 7, 9, 11)
ROWS, COLS = 48, 384
LANDINGS = 6


PLAN = {
    "S": [("g", 1, "line"), ("g", 0, "across"), ("g", 2, "line"), ("g", 1, "across"), ("g", 3, "line"), ("g", 0, "along"), ("g", 2, "across"), ("g", 0, "finish")],
    "F0": [("g", 1, "along"), ("g", 3, "across"), ("g", 4, "line"), ("g", 5, "line")],
    "F1": [("g", 1, "finish")],
    "F2": [("g", 2, "along")],
    "F3": [("g", 3, "along"), ("g", 2, "finish")],
    "F4": [("g", 3, "finish"), ("g", 4, "across"), ("g", 5, "across"), ("g", 6, "line"), ("g", 7, "line")],
    "A": [("g", 4, "along"), ("g", 5, "along"), ("g", 4, "finish"), ("g", 6, "across"), ("g", 8, "line"), ("g", 5, "finish")],
    "T1": [("g", 7, "across"), ("g", 9, "line")],
    "T4": [("g", 6, "along"), ("g", 8, "across"), ("g", 10, "line")],
    "T5": [("g", 7, "along"), ("g", 6, "finish")],
    "T6": [("g", 9, "across"), ("g", 11, "line"), ("r", 0, "core"), ("g", 7, "finish")],
    "T7": [("r", 1, "core"), ("g", 8, "along"), ("g", 10, "across")],
    "T9": [("g", 8, "finish"), ("g", 9, "along")],
    "T11": [("g", 9, "finish"), ("g", 11, "across")],
    "T16": [("r", 0, "across"), ("r", 1, "across"), ("r", 2, "core"), ("r", 3, "core"), ("g", 10, "along"), ("g", 11, "along")],
    "T18": [("g", 10, "finish"), ("g", 11, "finish")],
    "T19": [("r", 0, "along"), ("r", 1, "along")],
    "T23": [("r", 2, "across"), ("r", 3, "across"), ("r", 4, "core"), ("r", 5, "core"), ("r", 0, "finish")],
    "T26": [("r", 2, "along"), ("r", 1, "finish")],
    "T27": [("r", 3, "along")],
    "B2": [("r", 2, "finish"), ("r", 4, "across"), ("r", 5, "across"), ("r", 6, "core"), ("r", 7, "core")],
    "B4": [("r", 8, "start")],
    "K0": [("r", 4, "along")],
    "K1": [("r", 3, "finish"), ("r", 5, "along")],
    "K2": [("r", 4, "finish"), ("r", 6, "across"), ("r", 7, "across"), ("r", 8, "core"), ("r", 9, "core")],
    "K4": [("r", 5, "finish"), ("r", 6, "along"), ("r", 7, "along")],
    "K5": [("r", 8, "across"), ("r", 9, "across"), ("r", 10, "core")],
    "L0": [("r", 6, "finish")],
    "L1": [("r", 8, "along"), ("r", 11, "core")],
    "E": [("r", 7, "finish"), ("r", 9, "along"), ("r", 10, "across"), ("r", 8, "finish"), ("r", 11, "across"), ("r", 9, "finish"), ("r", 10, "along"), ("r", 11, "along"), ("r", 10, "finish"), ("r", 11, "finish")],
}


def nt(a, b):
    return lax.dot_general(a, b, (((1,), (1,)), ((), ())), preferred_element_type=f32)


def nn(a, b):
    return jnp.dot(a, b, preferred_element_type=f32)


def tn(a, b):
    return lax.dot_general(a, b, (((0,), (0,)), ((), ())), preferred_element_type=f32)


def exact(a, b, dims=(((1,), (0,)), ((), ()))):
    return lax.dot_general(a, b, dims, precision=lax.Precision.HIGHEST, preferred_element_type=f32)


def part_of(index, size):
    return pl.ds(pl.multiple_of(index * size, size), size)


def place():
    me = lax.axis_index("dp")
    group = lax.axis_size("dp") // RANKS
    rank, low = me // group, me % group
    digits = dict(z=rank // 8, y=(rank // 4) % 2, x=(rank // 2) % 2, c=rank % 2)

    def device(**changed):
        d = {**digits, **changed}
        return ((((d["z"] * 2 + d["y"]) * 2 + d["x"]) * 2 + d["c"]) * group + low,)

    return digits, device


def partners(digits, device):
    line = [device(z=(digits["z"] + step) % 4) for step in (1, 2, 3)]
    return line + [device(**{axis: 1 - digits[axis]}) for axis in "yxc"]


def greet(digits, device):
    barrier = pltpu.get_barrier_semaphore()
    others = partners(digits, device)
    for other in others:
        pl.semaphore_signal(barrier, inc=1, device_id=other, device_id_type=MESH_ID)
    return lambda: pl.semaphore_wait(barrier, len(others))


class Transfers:
    def __init__(self, send_sems, recv_sems, digits, device):
        self.send_sems, self.recv_sems, self.digits, self.device = send_sems, recv_sems, digits, device

    def flip(self, *axes):
        return {axis: 1 - self.digits[axis] for axis in axes}

    def copy(self, slot):
        source, target, device_id = self.spec(slot)
        return pltpu.make_async_remote_copy(
            src_ref=source,
            dst_ref=target,
            send_sem=self.send_sems.at[slot],
            recv_sem=self.recv_sems.at[slot],
            device_id=device_id,
            device_id_type=MESH_ID,
        )

    def go(self, *slots):
        for slot in slots:
            self.copy(slot).start()

    def arrived_at(self, slot, landing):
        pltpu.make_async_remote_copy(
            src_ref=landing,
            dst_ref=landing,
            send_sem=self.send_sems.at[slot],
            recv_sem=self.recv_sems.at[slot],
            device_id=self.device(c=1 - self.digits["c"]),
            device_id_type=MESH_ID,
        ).wait_recv()

    def arrived(self, *slots):
        for slot in slots:
            self.arrived_at(slot, self.landing(slot))

    def sent(self, count):
        for slot in range(count):
            self.copy(slot).wait_send()


class Gather(Transfers):
    SLOTS = 10

    def __init__(self, full, send_sems, recv_sems, order, digits, device):
        super().__init__(send_sems, recv_sems, digits, device)
        self.full = full
        self.first, self.second = order

    def line_of(self, *flipped):
        d = {**self.digits, **self.flip(*flipped)}
        return self.full.at[:, d["y"], d["x"], d["c"]]

    def block_of(self, z):
        d = self.digits
        return self.full.at[z, d["y"], d["x"], d["c"]]

    def spec(self, slot):
        z, a, b = self.digits["z"], self.first, self.second
        if slot < 3:
            own = self.block_of(z)
            return own, own, self.device(z=(z + slot + 1) % 4)
        flipped, towards = ((), (), (), (a,), (a,), (b,), (b, a))[slot - 3], (a, b, "c", b, "c", "c", "c")[slot - 3]
        line = self.line_of(*flipped)
        return line, line, self.device(**self.flip(towards))

    def landing(self, slot):
        a, b = self.first, self.second
        if slot < 3:
            return self.block_of((self.digits["z"] + 3 - slot) % 4)
        return self.line_of(*((a,), (b,), ("c",), (b, a), ("c", a), ("c", b), ("c", b, a))[slot - 3])

    def start(self):
        self.go(0, 1, 2)

    def line(self):
        self.arrived(0, 1, 2)
        self.go(3, 4, 5)

    def across(self):
        self.arrived(3)
        self.go(6, 7)

    def along(self):
        self.arrived(4)
        self.go(8)
        self.arrived(6)
        self.go(9)

    def finish(self):
        self.arrived(5, 7, 8, 9)
        self.sent(self.SLOTS)


class PlaneGather(Gather):
    def __init__(self, full, send_sems, recv_sems, order, digits, device, plane):
        super().__init__(full, send_sems, recv_sems, order, digits, device)
        self.plane = plane

    def spec(self, slot):
        if slot < 3:
            line = self.line_of()
            return line, line, self.device(z=(self.digits["z"] + slot + 1) % 4)
        return super().spec(slot)

    def start(self):
        @pl.when(self.digits["z"] == self.plane)
        def _():
            self.go(0, 1, 2)

    def line(self):
        z = self.digits["z"]
        for slot in range(3):

            @pl.when(z == (self.plane + slot + 1) % 4)
            def _(slot=slot):
                line = self.line_of()
                self.arrived_at(slot, line)

        self.go(3, 4, 5)

    def sent(self, count):
        for slot in range(3, count):
            self.copy(slot).wait_send()

        @pl.when(self.digits["z"] == self.plane)
        def _():
            for slot in range(3):
                self.copy(slot).wait_send()


class Reduce(Transfers):
    SLOTS = 7

    def __init__(self, parts, received, send_sems, recv_sems, order, digits, device, credits=None, grants=None):
        super().__init__(send_sems, recv_sems, digits, device)
        self.parts = parts
        self.from_core, self.from_first, self.from_second, self.from_line = received
        self.first, self.second = order
        self.credits, self.grants = credits, grants

    def half(self, first, c):
        if self.first == "y":
            return self.parts.at[:, first, :, c]
        return self.parts.at[:, :, first, c]

    def at(self, z, first, second):
        d = {self.first: first, self.second: second}
        return (z, d["y"], d["x"], self.digits["c"])

    def spec(self, slot):
        d, a, b = self.digits, self.first, self.second
        if slot < 2:
            side = (1 - d[a], d[a])[slot]
            return self.half(side, 1 - d["c"]), self.from_core.at[slot], self.device(**self.flip("c"))
        if slot == 2:
            return self.half(1 - d[a], d["c"]), self.from_first, self.device(**self.flip(a))
        if slot == 3:
            q = {**d, **self.flip(b)}
            return self.parts.at[:, q["y"], q["x"], d["c"]], self.from_second, self.device(**self.flip(b))
        z = (d["z"] + slot - 3) % 4
        return self.parts.at[z, d["y"], d["x"], d["c"]], self.from_line.at[slot - 4], self.device(z=z)

    def landing(self, slot):
        if slot < 2:
            return self.from_core.at[slot]
        if slot < 4:
            return (self.from_first, self.from_second)[slot - 2]
        return self.from_line.at[slot - 4]

    def spend(self, *kinds):
        if self.credits is not None:
            for kind in kinds:
                pl.semaphore_wait(self.credits.at[kind], 1)

    def grant(self):
        d = self.digits
        if self.grants is not None:
            others = [self.device(**self.flip(axis)) for axis in ("c", self.first, self.second)]
            others += [self.device(z=(d["z"] + 4 - step) % 4) for step in (1, 2, 3)]
            for kind, other in enumerate(others):
                pl.semaphore_signal(self.grants.at[kind], inc=1, device_id=other, device_id_type=MESH_ID)

    def add(self, first, second, received):
        d = {self.first: first, self.second: slice(None) if second is None else second}
        index = (slice(None), d["y"], d["x"], self.digits["c"])
        self.parts[index] = (self.parts[index].astype(f32) + received.astype(f32)).astype(bf16)

    def start(self):
        self.spend(0)
        self.go(0, 1)

    def core(self):
        d, a = self.digits, self.first
        self.arrived(0)
        self.add(1 - d[a], None, self.from_core[0])
        self.spend(1)
        self.go(2)
        self.arrived(1)
        self.add(d[a], None, self.from_core[1])

    def across(self):
        d, a, b = self.digits, self.first, self.second
        self.arrived(2)
        self.add(d[a], 1 - d[b], self.from_first[:, 1 - d[b]])
        self.spend(2)
        self.go(3)
        self.add(d[a], d[b], self.from_first[:, d[b]])

    def along(self):
        d, a, b = self.digits, self.first, self.second
        self.arrived(3)
        self.add(d[a], d[b], self.from_second[...])
        self.spend(3, 4, 5)
        self.go(4, 5, 6)

    def finish(self, store):
        d = self.digits
        total = self.parts[d["z"], d["y"], d["x"], d["c"]].astype(f32)
        for slot in (4, 5, 6):
            self.arrived(slot)
            total = total + self.from_line[slot - 4].astype(f32)
        store(total)
        self.sent(self.SLOTS)
        self.grant()


class PlaneReduce(Reduce):
    def __init__(self, parts, received, plane_in, send_sems, recv_sems, order, digits, device, credits, grants, plane):
        super().__init__(parts, received, send_sems, recv_sems, order, digits, device, credits, grants)
        self.plane_in, self.plane = plane_in, plane

    def along(self):
        d, a, b = self.digits, self.first, self.second
        self.arrived(3)
        self.add(d[a], d[b], self.from_second[...])
        self.spend(3, 4, 5)
        for step in (1, 2, 3):

            @pl.when(d["z"] == (self.plane + step) % 4)
            def _(step=step):
                self.to_plane(step).start()

    def to_plane(self, step):
        d = self.digits
        return pltpu.make_async_remote_copy(
            src_ref=self.parts.at[:, d["y"], d["x"], d["c"]],
            dst_ref=self.plane_in.at[step - 1],
            send_sem=self.send_sems.at[3 + step],
            recv_sem=self.recv_sems.at[3 + step],
            device_id=self.device(z=self.plane),
            device_id_type=MESH_ID,
        )

    def finish(self, store):
        d = self.digits

        @pl.when(d["z"] == self.plane)
        def _():
            total = self.parts[:, d["y"], d["x"], d["c"]].astype(f32)
            for step in (1, 2, 3):
                self.arrived_at(3 + step, self.plane_in.at[step - 1])
                total = total + self.plane_in[step - 1].astype(f32)
            store(total)

        for step in (1, 2, 3):

            @pl.when(d["z"] == (self.plane + step) % 4)
            def _(step=step):
                self.to_plane(step).wait_send()

        for slot in range(4):
            self.copy(slot).wait_send()
        self.grant()


class SmallSum(Transfers):
    SLOTS = 6

    def __init__(self, total, buffer, send_sems, recv_sems, digits, device):
        super().__init__(send_sems, recv_sems, digits, device)
        self.total, self.buffer = total, buffer

    def spec(self, slot):
        z = self.digits["z"]
        if slot < 3:
            return self.buffer.at[2 * slot], self.buffer.at[2 * slot + 1], self.device(**self.flip("cxy"[slot]))
        mine = self.buffer.at[6 + z]
        return mine, mine, self.device(z=(z + slot - 2) % 4)

    def landing(self, slot):
        if slot < 3:
            return self.buffer.at[2 * slot + 1]
        return self.buffer.at[6 + (self.digits["z"] + 6 - slot) % 4]

    def start(self, slot):
        if slot < 3:
            self.buffer[2 * slot] = self.total[...]
            self.go(slot)
        else:
            self.buffer[6 + self.digits["z"]] = self.total[...]
            self.go(3, 4, 5)

    def finish(self, slot):
        if slot < 3:
            self.arrived(slot)
            self.total[...] = self.total[...] + self.buffer[2 * slot + 1]
        else:
            self.arrived(3, 4, 5)
            self.total[...] = (self.buffer[6] + self.buffer[7]) + (self.buffer[8] + self.buffer[9])
            self.sent(self.SLOTS)


def pack(block):
    rows = block.reshape(-1, 8, 2 * COLS)
    return jnp.concatenate([rows[:, :, :COLS], rows[:, :, COLS:]], axis=1).reshape(-1, COLS)


def unpack(block):
    rows = block.reshape(-1, 2, 8, COLS)
    return jnp.concatenate([rows[:, 0].reshape(-1, COLS), rows[:, 1].reshape(-1, COLS)], axis=1)


def unpack_piece(piece, target):
    def plane(z, carry):
        target[part_of(z, 192), :] = unpack(piece[z].astype(f32).reshape(8 * ROWS, COLS)).astype(bf16)
        return carry

    lax.fori_loop(0, 4, plane, 0)


def pack_piece(piece, z, grad):
    piece[z] = pack(grad).astype(bf16).reshape(2, 2, 2, ROWS, COLS)


def bucket_of(offsets):
    distance = jnp.abs(offsets)
    coarse = jnp.full_like(distance, 8)
    for cutoff in CUTOFFS:
        coarse = coarse + (distance >= cutoff).astype(jnp.int32)
    return jnp.where(distance < 8, distance, coarse) + jnp.where(offsets > 0, 16, 0)


def strip_onehot(shift):
    column = lax.broadcasted_iota(jnp.int32, (128, 512), 1)
    column = jnp.where(column >= shift, column - shift, column - shift + 512)
    offset = jnp.where(column < 384, 128 - column, 640 - column)
    return bucket_of(offset) == lax.broadcasted_iota(jnp.int32, (128, 512), 0)


def make_strips(table_t, strips):
    line = nn(table_t[...], strip_onehot(0).astype(bf16)[:NB])
    for head in range(H):
        rows = jnp.broadcast_to(line[head : head + 1], (128, 512))
        strips[head] = pltpu.roll(rows, 0, 1, stride=1, stride_axis=0)[:, :384].astype(strips.dtype)


def strip_sums(strip):
    wide = jnp.concatenate([strip, jnp.zeros((128, 128), f32)], axis=1)
    total = wide[:8]
    for r in range(1, 16):
        total = total + pltpu.roll(wide[8 * r : 8 * r + 8], 512 - 8 * r, 1)
    return total


def table_sums(sums, far_sums):
    row = lax.broadcasted_iota(jnp.int32, (8 * H, 8 * H), 0)
    column = lax.broadcasted_iota(jnp.int32, (8 * H, 8 * H), 1)
    turned = exact((column == (row // 8) * 8 + 7 - row % 8).astype(f32), sums)
    lines = [
        jnp.sum(pltpu.roll(turned[8 * h : 8 * h + 8], 0, 1, stride=1, stride_axis=0), axis=0, keepdims=True)
        for h in range(H)
    ]
    lines.append(jnp.zeros((16 - H, 512), f32))
    table = exact(jnp.concatenate(lines, axis=0), strip_onehot(7).astype(f32), (((1,), (1,)), ((), ())))
    head = lax.broadcasted_iota(jnp.int32, (16, 128), 0)
    bucket = lax.broadcasted_iota(jnp.int32, (16, 128), 1)
    for side, index in ((0, 15), (1, 31)):
        rows = [jnp.sum(far_sums[h, side], axis=0, keepdims=True) for h in range(H)] + [jnp.zeros((16 - H, 128), f32)]
        total = jnp.sum(jnp.concatenate(rows, axis=0), axis=1, keepdims=True)
        table = table + jnp.where((bucket == index) & (head < H), total, 0.0)
    return table


def make_marks(lengths, key_marks, query_marks):
    position = lax.broadcasted_iota(jnp.int32, (SEQ, 128), 0)
    lane = lax.broadcasted_iota(jnp.int32, (SEQ, 128), 1)
    for row in range(key_marks.shape[0] // SEQ):
        segment = jnp.zeros((SEQ, 128), jnp.int32)
        end = 0
        for k in range(1, 5):
            end = end + lengths[row, k]
            segment = segment + (position >= end).astype(jnp.int32)
        own = segment == lane
        rows = slice(row * SEQ, (row + 1) * SEQ)
        key_marks[rows, :] = jnp.where(own, 1.0, 0.0).astype(bf16)
        query_marks[rows, :] = jnp.where(own | (lane >= 5), 0.0, -1e30).astype(bf16)


def lane_mask(h):
    lane = lax.broadcasted_iota(jnp.int32, (1, 128), 1)
    return lane < 64 if h == 0 else lane >= 64


def biased(raw, strip, half):
    low, high = strip[0:1, 383:384].astype(f32), strip[127:128, 0:1].astype(f32)
    rows = []
    for bj in range(4):
        blocks = []
        for bi in (0, 1):
            d = bj - bi - 2 * half
            block = raw[128 * bj : 128 * (bj + 1), 128 * bi : 128 * (bi + 1)]
            if d <= -2:
                block = block + low
            elif d >= 2:
                block = block + high
            else:
                block = block + strip[:, 128 * (1 - d) : 128 * (2 - d)].astype(f32)
            blocks.append(block)
        rows.append(jnp.concatenate(blocks, axis=1))
    return jnp.concatenate(rows, axis=0)


def heads_of(ref, rows, which, pair):
    return ref[rows, pl.ds(pl.multiple_of(which * 256 + pair * 128, 128), 128)]


def raw_scores(q2, k2, key_marks, query_marks):
    queries = jnp.concatenate([q2, query_marks], axis=1)
    return [nt(jnp.concatenate([jnp.where(lane_mask(h), k2, 0), key_marks], axis=1), queries) for h in range(2)]


def attend(qkv, key_marks, query_marks, strips, mix, lse, group, pair):
    count = mix.shape[0] // SEQ
    raws, values = [], []
    for row in range(count):
        rows = slice(row * SEQ, (row + 1) * SEQ)
        q2, k2, v2 = (heads_of(qkv, rows, which, pair) for which in range(3))
        raws.append(raw_scores(q2, k2, key_marks[rows, :], query_marks[rows, :]))
        values.append(v2.T)
    for row in range(count):
        outs = []
        for h in range(2):
            head = (group * 2 + pair) * 2 + h
            halves = []
            for half in range(2):
                span = slice(256 * half, 256 * half + 256)
                scores = biased(raws[row][h][:, span], strips[head], half)
                peak = jnp.max(scores, axis=0, keepdims=True)
                expo = jnp.exp(scores - peak)
                total = jnp.sum(expo, axis=0, keepdims=True)
                lse[row, pl.ds(head, 1), span] = peak + jnp.log(total)
                halves.append(nn(values[row][64 * h : 64 * h + 64], expo.astype(bf16)) * (1.0 / total))
            outs.append(jnp.concatenate(halves, axis=1))
        mix[row * SEQ : (row + 1) * SEQ, part_of(group * 2 + pair, 128)] = jnp.concatenate(outs, axis=0).T.astype(bf16)


def attend_back(qkv, gmix, key_marks, query_marks, strips, lse, inner, strip_grads, far_sums, group, pair):
    count = gmix.shape[0] // SEQ
    lanes = part_of(group * 2 + pair, 128)
    held = []
    for row in range(count):
        rows = slice(row * SEQ, (row + 1) * SEQ)
        q2, k2, v2 = (heads_of(qkv, rows, which, pair) for which in range(3))
        g2 = gmix[rows, lanes]
        raws = raw_scores(q2, k2, key_marks[rows, :], query_marks[rows, :])
        held.append((q2, k2.T, v2, g2, raws))
    for row in range(count):
        rows = slice(row * SEQ, (row + 1) * SEQ)
        q2, k2t, v2, g2, raws = held[row]
        grads = [nt(jnp.where(lane_mask(h), v2, 0), g2) for h in range(2)]
        grad_v, grad_k, grad_q = 0.0, 0.0, []
        for h in range(2):
            head = (group * 2 + pair) * 2 + h
            mask = lane_mask(h)
            near, far = {}, ([], [])
            probs_low, scores_low = [], []
            for half in range(2):
                span = slice(256 * half, 256 * half + 256)
                probs = jnp.exp(biased(raws[h][:, span], strips[head], half) - lse[row, pl.ds(head, 1), span])
                grad = probs * (grads[h][:, span] - inner[row, pl.ds(head, 1), span])
                probs_low.append(probs.astype(bf16))
                scores_low.append(grad.astype(bf16))
                for bi in (0, 1):
                    for bj in range(4):
                        d = bj - bi - 2 * half
                        block = grad[128 * bj : 128 * (bj + 1), 128 * bi : 128 * (bi + 1)]
                        if abs(d) <= 1:
                            near[d] = near[d] + block if d in near else block
                        else:
                            far[d > 0].append(jnp.sum(block.reshape(16, 8, 128), axis=0))
            strip_rows = part_of(group * 2 + pair, 128)
            for d, block in near.items():
                strip_grads[strip_rows, 384 * h + 128 * (1 - d) : 384 * h + 128 * (2 - d)] += block
            for side in (0, 1):
                far_sums[head, side] += sum(far[side][1:], far[side][0])
            grad_v = grad_v + nn(jnp.concatenate(probs_low, axis=1), jnp.where(mask, g2, 0))
            low = jnp.concatenate(scores_low, axis=1)
            grad_k = grad_k + nn(low, jnp.where(mask, q2, 0))
            grad_q.append(nn(k2t[64 * h : 64 * h + 64], low))
        for which, value in enumerate((jnp.concatenate(grad_q, axis=0).T, grad_k, grad_v)):
            qkv[rows, pl.ds(pl.multiple_of(which * 256 + pair * 128, 128), 128)] = value.astype(bf16)


def inner_sums(gmix, mix):
    product = gmix.astype(f32) * mix.astype(f32)
    high = product.astype(bf16)
    low = (product - high.astype(f32)).astype(bf16)
    feature = lax.broadcasted_iota(jnp.int32, (16, D), 1)
    first = lax.broadcasted_iota(jnp.int32, (16, D), 0) * 64
    own = jnp.where((feature >= first) & (feature < first + 64), 1.0, 0.0).astype(bf16)
    return nt(own, high) + nt(own, low)


def inv_rms(x):
    return lax.rsqrt(jnp.mean(x * x, axis=-1, keepdims=True) + EPSILON)


def norm_back(grad, x, gain):
    s = inv_rms(x)
    gg = grad * gain
    return s * gg - x * (s * s * s * jnp.mean(gg * x, axis=-1, keepdims=True)), jnp.sum(grad * x * s, axis=0, keepdims=True)


def gelu_both(x):
    cdf = 0.5 + 0.5 * lax.erf(x * 0.7071067811865476)
    return x * cdf, cdf + x * (jnp.exp(x * x * -0.5) * 0.3989422804014327)


def gain_line(gains, which):
    blocks = gains[...].reshape(8 * RANKS, 128).astype(bf16)
    lane = lax.broadcasted_iota(jnp.int32, (128, D), 1)
    spread = nn(blocks, (lane % 24 == lax.broadcasted_iota(jnp.int32, (128, D), 0)).astype(bf16))
    row = lax.broadcasted_iota(jnp.int32, (8 * RANKS, D), 0)
    column = lax.broadcasted_iota(jnp.int32, (8 * RANKS, D), 1)
    return jnp.sum(jnp.where(row == (column // 24) * 8 + which, spread, 0.0), axis=0, keepdims=True)


def run_at(step, plan):
    for when, stages in plan.items():

        @pl.when(step == when)
        def _(stages=stages):
            for stage in stages:
                stage()


def layer_kernel(
    tokens_hbm, cot_hbm, lengths, norm_gain, ffn_gain, w_query, w_key, w_value, w_out, w_in, w_ffn, table_t,
    out_hbm, gtok_hbm, grad_one, grad_two, grad_table, grad_q, grad_k, grad_v, grad_o, grad_in, grad_ffn,
    pieces, gains, weights, win, wff, qkv, mix, normed, tokens, cot, resid, out_sum, grad_sum, act, grad_inner,
    strips, key_marks, query_marks, lse, inner, far_sums, small, from_core, from_first, from_second, from_line,
    plane_in, small_buffer,
    gather_send, gather_recv, gain_send, gain_recv, reduce_send, reduce_recv, small_send, small_recv, credits, local_sems,
):
    count = tokens.shape[0]
    digits, device = place()
    me = (digits["z"], digits["y"], digits["x"], digits["c"])
    all_here = greet(digits, device)

    load_tokens = pltpu.make_async_copy(tokens_hbm, tokens, local_sems.at[0])
    load_tokens.start()
    load_cot = pltpu.make_async_copy(cot_hbm, cot, local_sems.at[1])
    load_cot.start()

    orders = ("xy", "yx")
    gain_gather = Gather(gains, gain_send, gain_recv, "xy", digits, device)
    gathers = []
    for i in range(PIECES):
        common = (pieces.at[i], gather_send.at[i], gather_recv.at[i], orders[i % 2], digits, device)
        gathers.append(PlaneGather(*common, FFN_PIECES.index(i)) if i in FFN_PIECES else Gather(*common))
    order = [i for t in range(TILES) for i in (IN_PIECES[t], FFN_PIECES[t])] + [OUT_PIECE, 0, 1, 2]
    reduces = []
    for n, i in enumerate(order):
        slot = n % LANDINGS
        received = (from_core.at[slot], from_first.at[slot], from_second.at[slot], from_line.at[slot])
        sems = (reduce_send.at[n], reduce_recv.at[n], orders[n % 2], digits, device)
        limits = (credits.at[slot] if n >= LANDINGS else None, credits.at[slot] if n + LANDINGS < PIECES else None)
        if i in FFN_PIECES:
            reduces.append(PlaneReduce(pieces.at[i], received, plane_in, *sems, *limits, FFN_PIECES.index(i)))
        else:
            reduces.append(Reduce(pieces.at[i], received, *sems, *limits))

    def store_in(t):
        def store(total):
            grad_in[:, TILE * t : TILE * (t + 1)] = unpack(total)

        return store

    def store_ffn(total):
        for i in range(4):
            grad_ffn[ROWS * (i // 2) : ROWS * (i // 2 + 1), COLS * (i % 2) : COLS * (i % 2 + 1)] = total[i]

    def store_out(total):
        grad_o[...] = unpack(total)

    def store_group(g):
        def store(total):
            block = unpack(total)
            for which, target in enumerate((grad_q, grad_k, grad_v)):
                target[:, 256 * g : 256 * (g + 1)] = block[:, 256 * which : 256 * (which + 1)]

        return store

    stores = [store for t in range(TILES) for store in (store_in(t), store_ffn)] + [store_out]
    stores += [store_group(g) for g in range(GROUPS)]

    def stage(kind, n, name):
        if kind == "r":
            return partial(reduces[n].finish, stores[n]) if name == "finish" else getattr(reduces[n], name)
        if name == "finish" and n <= OUT_PIECE:
            return partial(arrive, n)
        return getattr(gathers[n], name)

    def arrive(n):
        gathers[n].finish()
        unpack_piece(pieces.at[n], weights.at[n])

    def plan(letter):
        return {int(key[1:]): [stage(*entry) for entry in PLAN[key]] for key in PLAN if key[0] == letter}

    def run(stages):
        for each in stages:
            each()

    for g in range(GROUPS):
        span = slice(256 * g, 256 * g + 256)
        block = jnp.concatenate([w[:, span] for w in (w_query, w_key, w_value)], axis=1)
        pieces[(GROUP_PIECE + g, *me)] = pack(block.astype(f32)).astype(bf16)
    gains[me] = jnp.zeros((8, 128), f32)
    gains[(*me, slice(0, 1), slice(0, 24))] = norm_gain[...].astype(f32)
    gains[(*me, slice(1, 2), slice(0, 24))] = ffn_gain[...].astype(f32)
    all_here()
    gathers[0].start()
    gain_gather.start()
    gathers[1].start()
    gathers[2].start()
    pieces[(OUT_PIECE, *me)] = pack(w_out[...].astype(f32)).astype(bf16)
    gathers[3].start()
    for t in range(TILES):

        @pl.when(digits["z"] == t)
        def _(t=t):
            for i in range(4):
                block = w_ffn[ROWS * (i // 2) : ROWS * (i // 2 + 1), COLS * (i % 2) : COLS * (i % 2 + 1)]
                pieces[FFN_PIECES[t], i, digits["y"], digits["x"], digits["c"]] = block

        gathers[FFN_PIECES[t]].start()
        pieces[(IN_PIECES[t], *me)] = pack(w_in[:, TILE * t : TILE * (t + 1)].astype(f32)).astype(bf16)
        gathers[IN_PIECES[t]].start()

    make_marks(lengths, key_marks, query_marks)
    make_strips(table_t, strips)
    gain_gather.line()
    gathers[0].line()
    gain_gather.across()
    gain_gather.along()
    gain_gather.finish()
    gain_one, gain_two = gain_line(gains, 0), gain_line(gains, 1)
    load_tokens.wait()

    def norm_one(i, carry):
        rows = part_of(i, 256)
        x = tokens[rows, :].astype(f32)
        normed[rows, :] = (x * inv_rms(x) * gain_one).astype(bf16)
        return carry

    lax.fori_loop(0, count // 256, norm_one, 0)
    run([stage(*entry) for entry in PLAN["S"]])

    forward_plan = plan("F")

    def forward_group(g, carry):
        qkv[g] = nn(normed[...], weights[GROUP_PIECE + g]).astype(bf16)

        def forward(pair, carry):
            attend(qkv.at[g], key_marks, query_marks, strips, mix, lse, g, pair)
            run_at(2 * g + pair, forward_plan)
            return carry

        lax.fori_loop(0, 2, forward, 0)
        return carry

    lax.fori_loop(0, GROUPS, forward_group, 0)

    def after_attention(i, carry):
        rows = part_of(i, 512)
        r = tokens[rows, :].astype(f32) + nn(mix[rows, :], weights[OUT_PIECE])
        resid[rows, :] = r
        normed[rows, :] = (r * inv_rms(r) * gain_two).astype(bf16)
        return carry

    lax.fori_loop(0, count // 512, after_attention, 0)
    load_cot.wait()
    run([stage(*entry) for entry in PLAN["A"]])

    ffn_plan = plan("T")
    width = 256

    def tile_piece(t, which):
        return pieces.at[4 + 2 * t + which]

    def ffn_tile(t, carry):
        unpack_piece(tile_piece(t, 1), win)
        for b in range(8):
            for i in range(4):
                rows = slice(96 * b + ROWS * (i // 2), 96 * b + ROWS * (i // 2 + 1))
                block = pieces[4 + 2 * t, i, b // 4, (b // 2) % 2, b % 2]
                wff[rows, COLS * (i % 2) : COLS * (i % 2 + 1)] = block

        def columns(w, carry):
            span = part_of(w, width)
            ffn_in = nn(normed[...], win[:, span])
            grad_act = nt(cot[...], wff[span, :])
            value, slope = gelu_both(ffn_in)
            act[:, span] = value.astype(bf16)
            grad_inner[:, span] = (slope * grad_act).astype(bf16)
            run_at(7 * t + w, ffn_plan)
            return carry

        lax.fori_loop(0, TILE // width, columns, 0)

        for i in range(2):
            rows = slice(i * count // 2, (i + 1) * count // 2)
            value = nn(act[rows, :], wff[...])
            out_sum[rows, :] = jnp.where(t == 0, resid[rows, :], out_sum[rows, :]) + value

        run_at(7 * t + 3, ffn_plan)

        for i in range(2):
            rows = slice(i * count // 2, (i + 1) * count // 2)
            value = nt(grad_inner[rows, :], win[...])
            grad_sum[rows, :] = jnp.where(t == 0, 0.0, grad_sum[rows, :]) + value

        run_at(7 * t + 4, ffn_plan)
        grad = tn(normed[...], grad_inner[...])
        for z in range(4):
            pack_piece(tile_piece(t, 1), z, grad[192 * z : 192 * (z + 1)])
        run_at(t, {k: [reduces[2 * k].start] for k in range(TILES)})
        run_at(7 * t + 5, ffn_plan)
        grad = tn(act[...], cot[...]).astype(bf16)
        for b in range(8):
            for i in range(4):
                block = grad[96 * b + ROWS * (i // 2) : 96 * b + ROWS * (i // 2 + 1), COLS * (i % 2) : COLS * (i % 2 + 1)]
                pieces[4 + 2 * t, i, b // 4, (b // 2) % 2, b % 2] = block
        run_at(t, {k: [reduces[2 * k + 1].start] for k in range(TILES)})
        run_at(7 * t + 6, ffn_plan)
        return carry

    lax.fori_loop(0, TILES, ffn_tile, 0)

    before_plan = plan("B")
    small[...] = jnp.zeros(small.shape, f32)

    def spread_line(row, line):
        for j in range(D // 128):
            small[row + j : row + j + 1, :] += line[:, 128 * j : 128 * (j + 1)]

    def before_back(i, carry):
        rows = part_of(i, 256)
        act[rows, :] = out_sum[rows, :].astype(bf16)
        into, gain_sum = norm_back(grad_sum[rows, :], resid[rows, :], gain_two)
        spread_line(6, gain_sum)
        grad = cot[rows, :].astype(f32) + into
        grad_sum[rows, :] = grad
        low = grad.astype(bf16)
        cot[rows, :] = low
        gmix = nt(low, weights[OUT_PIECE]).astype(bf16)
        inner[i // 2, :, part_of(i % 2, 256)] = inner_sums(gmix, mix[rows, :])
        x = tokens[rows, :].astype(f32)
        grad_inner[rows, :] = (x * inv_rms(x) * gain_one).astype(bf16)
        normed[rows, :] = gmix
        run_at(i, before_plan)
        return carry

    lax.fori_loop(0, count // 256, before_back, 0)
    store_output = pltpu.make_async_copy(act, out_hbm, local_sems.at[2])
    store_output.start()
    out_sum[...] = jnp.zeros(out_sum.shape, f32)
    far_sums[...] = jnp.zeros(far_sums.shape, f32)
    grad = tn(mix[...], cot[...])
    for z in range(4):
        pack_piece(pieces.at[OUT_PIECE], z, grad[192 * z : 192 * (z + 1)])
    run(before_plan.get(4, []))
    back_plan = plan("K")

    def back_group(g, carry):
        def back(pair, carry):
            attend_back(qkv.at[g], normed, key_marks, query_marks, strips, lse, inner, out_sum, far_sums, g, pair)
            run_at(2 * g + pair, back_plan)
            return carry

        lax.fori_loop(0, 2, back, 0)
        grad = tn(grad_inner[...], qkv[g])
        for z in range(4):
            pack_piece(pieces.at[GROUP_PIECE + g], z, grad[192 * z : 192 * (z + 1)])
        run_at(g, {k: [reduces[9 + k].start] for k in range(GROUPS)})
        return carry

    lax.fori_loop(0, GROUPS, back_group, 0)
    last_plan = plan("L")

    def last(i, carry):
        rows = part_of(i, 512)
        grad = nt(qkv[0, rows, :], weights[0]) + nt(qkv[1, rows, :], weights[1]) + nt(qkv[2, rows, :], weights[2])
        into, gain_sum = norm_back(grad, tokens[rows, :].astype(f32), gain_one)
        spread_line(0, gain_sum)
        grad_sum[rows, :] = grad_sum[rows, :] + into
        run_at(i, last_plan)
        return carry

    lax.fori_loop(0, count // 512, last, 0)
    store_gtok = pltpu.make_async_copy(grad_sum, gtok_hbm, local_sems.at[3])
    store_gtok.start()
    for pair in range(H // 2):
        for h in range(2):
            head = 2 * pair + h
            strip = out_sum[128 * pair : 128 * pair + 128, 384 * h : 384 * h + 384]
            resid[8 * head : 8 * head + 8, :512] = strip_sums(strip)
    small[16:32, :] = table_sums(resid[: 8 * H, :512], far_sums)
    sums = SmallSum(small, small_buffer, small_send, small_recv, digits, device)
    tail = [stage(*entry) for entry in PLAN["E"]]
    for slot in range(4):
        sums.start(slot)
        if tail:
            tail.pop(0)()
        sums.finish(slot)
    for target, row in ((grad_one, 0), (grad_two, 6)):
        line = jnp.concatenate([small[row + j : row + j + 1, :] for j in range(D // 128)], axis=1)
        rank = (lax.axis_index("dp") // (lax.axis_size("dp") // RANKS)).astype(jnp.int32)
        own = pltpu.roll(jnp.broadcast_to(line, (8, D)), (D - 24 * rank) % D, 1)
        target[...] = own[0:1, :24]
    grad_table[...] = small[16 : 16 + H, :NB]
    run(tail)
    store_output.wait()
    store_gtok.wait()


def deliver_kernel(*refs):
    count = (len(refs) - 1) // 3
    sources, targets, held, sems = refs[:count], refs[count : 2 * count], refs[2 * count : 3 * count], refs[-1]
    loads = [pltpu.make_async_copy(sources[i], held[i], sems.at[0, i]) for i in range(count)]
    stores = [pltpu.make_async_copy(held[i], targets[i], sems.at[1, i]) for i in range(count)]
    for load in loads:
        load.start()
    for load, store in zip(loads, stores):
        load.wait()
        store.start()
    for store in stores:
        store.wait()


def inner_groups():
    total = lax.axis_size("dp")
    group = total // RANKS
    return group, [list(range(i * group, (i + 1) * group)) for i in range(RANKS)]


def widen(block):
    group, groups = inner_groups()
    if group == 1:
        return block
    return lax.all_gather(block, "dp", axis=0, tiled=True, axis_index_groups=groups)


def narrow(block):
    group, groups = inner_groups()
    if group == 1:
        return block
    return lax.psum_scatter(block, "dp", scatter_dimension=0, tiled=True, axis_index_groups=groups)


def per_device(
    tokens, lengths, norm_gain, w_query, w_key, w_value, w_out, bias_table, ffn_gain, w_in, w_ffn_out, cotangent
):
    count = tokens.shape[0]
    norm_gain, ffn_gain, w_query, w_key, w_value, w_out, w_in, w_ffn_out = (
        widen(w) for w in (norm_gain, ffn_gain, w_query, w_key, w_value, w_out, w_in, w_ffn_out)
    )
    any_space = pl.BlockSpec(memory_space=pl.ANY)
    vmem = pl.BlockSpec(memory_space=pltpu.VMEM)
    smem = pl.BlockSpec(memory_space=pltpu.SMEM)
    full = (4, 2, 2, 2)
    out = jax.ShapeDtypeStruct
    shapes = [out((count, D), bf16), out((count, D), f32), out((1, 24), f32), out((1, 24), f32), out((H, NB), f32)]
    shapes += [out((24, D), f32)] * 4 + [out((24, FF), f32), out((96, D), f32)]
    results = pl.pallas_call(
        layer_kernel,
        out_shape=shapes,
        in_specs=[any_space] * 2 + [smem] + [vmem] * 9,
        out_specs=[any_space] * 2 + [vmem] * 9,
        scratch_shapes=[
            pltpu.VMEM((PIECES,) + full + (ROWS, COLS), bf16),
            pltpu.VMEM(full + (8, 128), f32),
            pltpu.VMEM((4, D, D), bf16),
            pltpu.VMEM((D, TILE), bf16),
            pltpu.VMEM((TILE, D), bf16),
            pltpu.VMEM((GROUPS, count, D), bf16),
            pltpu.VMEM((count, D), bf16),
            pltpu.VMEM((count, D), bf16),
            pltpu.VMEM((count, D), bf16),
            pltpu.VMEM((count, D), bf16),
            pltpu.VMEM((count, D), f32),
            pltpu.VMEM((count, D), f32),
            pltpu.VMEM((count, D), f32),
            pltpu.VMEM((count, TILE), bf16),
            pltpu.VMEM((count, TILE), bf16),
            pltpu.VMEM((H, 128, 384), bf16),
            pltpu.VMEM((count, 128), bf16),
            pltpu.VMEM((count, 128), bf16),
            pltpu.VMEM((count // SEQ, H, SEQ), f32),
            pltpu.VMEM((count // SEQ, 16, SEQ), f32),
            pltpu.VMEM((H, 2, 8, 128), f32),
            pltpu.VMEM((32, 128), f32),
            pltpu.VMEM((LANDINGS, 2, 4, 2, ROWS, COLS), bf16),
            pltpu.VMEM((LANDINGS, 4, 2, ROWS, COLS), bf16),
            pltpu.VMEM((LANDINGS, 4, ROWS, COLS), bf16),
            pltpu.VMEM((LANDINGS, 3, ROWS, COLS), bf16),
            pltpu.VMEM((3, 4, ROWS, COLS), bf16),
            pltpu.VMEM((10, 32, 128), f32),
            pltpu.SemaphoreType.DMA((PIECES, Gather.SLOTS)),
            pltpu.SemaphoreType.DMA((PIECES, Gather.SLOTS)),
            pltpu.SemaphoreType.DMA((Gather.SLOTS,)),
            pltpu.SemaphoreType.DMA((Gather.SLOTS,)),
            pltpu.SemaphoreType.DMA((PIECES, Reduce.SLOTS)),
            pltpu.SemaphoreType.DMA((PIECES, Reduce.SLOTS)),
            pltpu.SemaphoreType.DMA((SmallSum.SLOTS,)),
            pltpu.SemaphoreType.DMA((SmallSum.SLOTS,)),
            pltpu.SemaphoreType.REGULAR((LANDINGS, 6)),
            pltpu.SemaphoreType.DMA((4,)),
        ],
        compiler_params=pltpu.CompilerParams(collective_id=1, has_side_effects=True, vmem_limit_bytes=63 << 20),
    )(
        tokens,
        cotangent,
        lengths,
        norm_gain.reshape(1, -1),
        ffn_gain.reshape(1, -1),
        w_query,
        w_key,
        w_value,
        w_out,
        w_in,
        w_ffn_out,
        bias_table.T,
    )
    results = pl.pallas_call(
        deliver_kernel,
        out_shape=shapes,
        in_specs=[any_space] * len(shapes),
        out_specs=[any_space] * len(shapes),
        scratch_shapes=[pltpu.VMEM(shape.shape, shape.dtype) for shape in shapes]
        + [pltpu.SemaphoreType.DMA((2, len(shapes)))],
        compiler_params=pltpu.CompilerParams(vmem_limit_bytes=32 << 20),
    )(*results)
    output, grad_tokens, grad_one, grad_two, grad_table, *weight_grads = results
    group, groups = inner_groups()
    if group > 1:
        grad_table = lax.psum(grad_table, "dp", axis_index_groups=groups)
    grad_q, grad_k, grad_v, grad_o, grad_in, grad_ffn = (narrow(grad) for grad in weight_grads)
    return (
        output,
        grad_tokens,
        narrow(grad_one[0]),
        grad_q,
        grad_k,
        grad_v,
        grad_o,
        grad_table.T,
        narrow(grad_two[0]),
        grad_in,
        grad_ffn,
    )


def solution(mesh):
    rows, whole = P("dp", None), P("dp")
    return jax.shard_map(
        per_device,
        mesh=mesh,
        in_specs=(rows, rows, whole, rows, rows, rows, rows, P(), whole, rows, rows, rows),
        out_specs=(rows, rows, whole, rows, rows, rows, rows, P(), whole, rows, rows),
        check_vma=False,
    )
```

time: 256 us -> 190 us (0.74)
  Pallas kernels: 240 us -> 178 us
  local copies, waits for them, and re-layouts: 14.4 us -> 10.7 us
    pallas_call x1 -> x2, Pallas kernels: 240 us -> 178 us  [the longest x1 175 us: per_device(): pl.pallas_call(layer_kernel, out_shape=shapes, in_specs=[any_space] * 2 +...]
    unnamed x23 -> x22, local copies, waits for them, and re-layouts: 9.13 us -> 10.7 us
where the time goes in v4:
time: 190 us
  Pallas kernels  178 us (94%)
  local copies, waits for them, and re-layouts  10.7 us (6%)
    pallas_call x1, Pallas kernels, per_device(): pl.pallas_call(layer_kernel, out_shape=shapes, in_specs=[any_space] * 2 +...  175 us
    unnamed x22, local copies, waits for them, and re-layouts  10.7 us

profile of v4, /device:TPU:0, one launch (start us, length us, event | category | flops | bytes accessed | tf_op | source)
XLA Modules:
  0.0 189.7 jit_solution(16281178191180284410)
XLA Ops:
  0.6 174.7 %shard_map.203 = (bf16[1024,768]{1,0:T(8,128)(2,1)}, f32[1024,768]{1,0:T(8,128)}, f32[1,24]{1,0:T(1,128)}, f32[1,24]{1,0:T(1,128)}, f32[12,32]{1,0:T(8,128)}, /*...) custom-call(bf16[1024,768]{1,0:T(8,128)(2,1)} %tokens_hbm.1, ...), custom_call_target="tpu_custom_call" | custom-call | tf_op jit(solution)/shard_map/pallas_call | solution.py:996
  175.3 0.0 copy-start
  175.3 1.9 copy-done
  177.2 0.0 copy-start.1
  177.2 1.4 copy-done.1
  178.6 0.0 copy-start.2
  178.6 1.0 copy-done.2
  179.6 0.0 copy-start.3
  179.6 1.0 copy-done.3
  180.5 0.0 copy-start.4
  180.5 0.9 copy-done.4
  181.4 0.0 copy-start.5
  181.4 0.9 copy-done.5
  182.3 0.0 copy-start.6
  182.3 0.9 copy-done.6
  183.2 0.0 copy-start.7
  183.2 0.9 copy-done.7
  184.1 0.0 copy-start.8
  184.1 0.7 copy-done.8
  184.8 0.0 copy-start.9
  184.8 0.7 copy-done.9
  185.4 0.0 copy-start.10
  185.4 0.6 copy-done.10
  186.0 3.5 %shard_map.204 = (bf16[1024,768]{1,0:T(8,128)(2,1)}, f32[1024,768]{1,0:T(8,128)}, f32[1,24]{1,0:T(1,128)}, f32[1,24]{1,0:T(1,128)}, f32[12,32]{1,0:T(8,128)}, /*...) custom-call(bf16[1024,768]{1,0:T(8,128)(2,1)S(1)} %copy-done.1, ...), custom_call_target="tpu_custom_call" | custom-call | tf_op jit(solution)/shard_map/pallas_call | solution.py:1056
Async XLA Ops:
  175.3 1.9 copy-start
  177.2 1.4 copy-start.1
  178.6 1.0 copy-start.2
  179.6 1.0 copy-start.3
  180.5 0.9 copy-start.4
  181.4 0.9 copy-start.5
  182.3 0.9 copy-start.6
  183.2 0.9 copy-start.7
  184.1 0.7 copy-start.8
  184.8 0.7 copy-start.9
  185.4 0.6 copy-start.10

commit v5 on v4

--- a/solution.py
+++ b/solution.py
@@ -28,7 +28,11 @@
 
 
 PLAN = {
-    "S": [("g", 1, "line"), ("g", 0, "across"), ("g", 2, "line"), ("g", 1, "across"), ("g", 3, "line"), ("g", 0, "along"), ("g", 2, "across"), ("g", 0, "finish")],
+    "S0": [("g", 0, "line")],
+    "S1": [("g", 1, "line"), ("g", 0, "across")],
+    "S2": [("g", 2, "line"), ("g", 1, "across"), ("g", 3, "line"), ("g", 0, "along")],
+    "S3": [("g", 2, "across")],
+    "S": [("g", 0, "finish")],
     "F0": [("g", 1, "along"), ("g", 3, "across"), ("g", 4, "line"), ("g", 5, "line")],
     "F1": [("g", 1, "finish")],
     "F2": [("g", 2, "along")],
@@ -293,7 +297,7 @@
     def add(self, first, second, received):
         d = {self.first: first, self.second: slice(None) if second is None else second}
         index = (slice(None), d["y"], d["x"], self.digits["c"])
-        self.parts[index] = (self.parts[index].astype(f32) + received.astype(f32)).astype(bf16)
+        self.parts[index] = self.parts[index] + received
 
     def start(self):
         self.spend(0)
@@ -760,11 +764,9 @@
 
     make_marks(lengths, key_marks, query_marks)
     make_strips(table_t, strips)
-    gain_gather.line()
-    gathers[0].line()
-    gain_gather.across()
-    gain_gather.along()
-    gain_gather.finish()
+    for i, gain_stage in enumerate((gain_gather.line, gain_gather.across, gain_gather.along, gain_gather.finish)):
+        run([stage(*entry) for entry in PLAN[f"S{i}"]])
+        gain_stage()
     gain_one, gain_two = gain_line(gains, 0), gain_line(gains, 1)
     load_tokens.wait()
 
@@ -1060,7 +1062,7 @@
         out_specs=[any_space] * len(shapes),
         scratch_shapes=[pltpu.VMEM(shape.shape, shape.dtype) for shape in shapes]
         + [pltpu.SemaphoreType.DMA((2, len(shapes)))],
-        compiler_params=pltpu.CompilerParams(vmem_limit_bytes=32 << 20),
+        compiler_params=pltpu.CompilerParams(vmem_limit_bytes=63 << 20),
     )(*results)
     output, grad_tokens, grad_one, grad_two, grad_table, *weight_grads = results
     group, groups = inner_groups()

time: 190 us -> 178 us (0.937)
  local copies, waits for them, and re-layouts: 10.7 us -> 0 us
    unnamed x22 -> x0, local copies, waits for them, and re-layouts: 10.7 us -> none
where the time goes in v5:
time: 178 us
  Pallas kernels  177 us (99%)
    pallas_call x1, Pallas kernels, per_device(): pl.pallas_call(layer_kernel, out_shape=shapes, in_specs=[any_space] * 2 +...  173 us
    pallas_call x1, Pallas kernels, per_device(): pl.pallas_call(deliver_kernel, out_shape=shapes, in_specs=[any_space] * l...  4.51 us

profile of v5, /device:TPU:0, one launch (start us, length us, event | category | flops | bytes accessed | tf_op | source)
XLA Modules:
  0.0 178.2 jit_solution(14166213750868905341)
XLA Ops:
  0.6 172.8 %shard_map.203 = (bf16[1024,768]{1,0:T(8,128)(2,1)}, f32[1024,768]{1,0:T(8,128)}, f32[1,24]{1,0:T(1,128)}, f32[1,24]{1,0:T(1,128)}, f32[12,32]{1,0:T(8,128)}, /*...) custom-call(bf16[1024,768]{1,0:T(8,128)(2,1)} %tokens_hbm.1, ...), custom_call_target="tpu_custom_call" | custom-call | tf_op jit(solution)/shard_map/pallas_call | solution.py:998
  173.5 4.5 %shard_map.204 = (bf16[1024,768]{1,0:T(8,128)(2,1)}, f32[1024,768]{1,0:T(8,128)}, f32[1,24]{1,0:T(1,128)}, f32[1,24]{1,0:T(1,128)}, f32[12,32]{1,0:T(8,128)}, /*...) custom-call(bf16[1024,768]{1,0:T(8,128)(2,1)} %get-tuple-element.33., ...), custom_call_target="tpu_custom_call" | custom-call | tf_op jit(solution)/shard_map/pallas_call | solution.py:1058

commit v6 on v5

--- a/solution.py
+++ b/solution.py
@@ -25,43 +25,61 @@
 FFN_PIECES, IN_PIECES = (4, 6, 8, 10), (5, 7, 9, 11)
 ROWS, COLS = 48, 384
 LANDINGS = 6
+LOW, HIGH = slice(0, 2), slice(2, 4)
 
 
 PLAN = {
+    "S": [("g", 0, "finish")],
+    "P0": [("g", 3, "across"), ("g", 4, "line")],
+    "F0": [("g", 1, "along"), ("g", 2, "along")],
+    "F1": [("g", 1, "finish")],
+    "P1": [("g", 2, "finish"), ("g", 5, "across")],
+    "F2": [("g", 3, "along"), ("g", 6, "line")],
+    "P2": [("g", 3, "finish"), ("g", 4, "across"), ("g", 7, "line")],
+    "F4": [("g", 5, "along"), ("g", 8, "line")],
+    "F5": [("g", 6, "across"), ("g", 9, "line")],
+    "A": [("g", 4, "along"), ("g", 5, "finish"), ("g", 7, "across"), ("g", 10, "line"), ("g", 4, "finish")],
+    "T1": [("g", 8, "across"), ("g", 11, "line")],
+    "T2": [("g", 6, "along")],
+    "T4": [("g", 6, "finish"), ("g", 9, "across")],
+    "T5": [("g", 7, "along")],
+    "T6": [("g", 10, "across"), ("r", 0, "core"), ("g", 7, "finish")],
+    "T7": [("g", 8, "along"), ("r", 1, "core")],
+    "T9": [("g", 8, "finish"), ("g", 11, "across")],
+    "T10": [("g", 9, "along")],
+    "T11": [("g", 10, "along")],
+    "T12": [("g", 9, "finish")],
+    "T13": [("g", 10, "finish"), ("r", 0, "across")],
+    "T14": [("r", 2, "core")],
+    "T15": [("r", 1, "across"), ("r", 3, "core")],
+    "T16": [("g", 11, "along")],
+    "T17": [("r", 0, "along")],
+    "T18": [("g", 11, "finish")],
+    "T19": [("r", 2, "across")],
+    "T20": [("r", 1, "along")],
+    "T21": [("r", 0, "finish"), ("r", 4, "core")],
+    "T22": [("r", 3, "across"), ("r", 5, "core")],
+    "T23": [("r", 2, "along")],
+    "T26": [("r", 4, "across"), ("r", 3, "along"), ("r", 2, "finish"), ("r", 1, "finish")],
+    "T27": [("r", 5, "across"), ("r", 6, "core")],
+    "B0": [("r", 4, "along")],
+    "B2": [("r", 7, "core")],
+    "B3": [("r", 5, "along")],
+    "B4": [("r", 8, "start")],
+    "K0": [("r", 3, "finish"), ("r", 4, "finish"), ("r", 6, "across"), ("r", 8, "core")],
+    "K1": [("r", 7, "across")],
+    "G0": [("r", 6, "along")],
+    "K2": [("r", 5, "finish"), ("r", 8, "across"), ("r", 9, "core")],
+    "K3": [("r", 6, "finish"), ("r", 7, "along")],
+    "G1": [("r", 8, "along")],
+    "K4": [("r", 9, "across"), ("r", 10, "core")],
+    "G2": [("r", 8, "finish"), ("r", 9, "along")],
+    "L0": [("r", 7, "finish"), ("r", 10, "across"), ("r", 11, "core")],
+    "E": [("r", 9, "finish"), ("r", 10, "along"), ("r", 11, "across"), ("r", 10, "finish"), ("r", 11, "along"), ("r", 11, "finish")],
     "S0": [("g", 0, "line")],
-    "S1": [("g", 1, "line"), ("g", 0, "across")],
-    "S2": [("g", 2, "line"), ("g", 1, "across"), ("g", 3, "line"), ("g", 0, "along")],
-    "S3": [("g", 2, "across")],
-    "S": [("g", 0, "finish")],
-    "F0": [("g", 1, "along"), ("g", 3, "across"), ("g", 4, "line"), ("g", 5, "line")],
-    "F1": [("g", 1, "finish")],
-    "F2": [("g", 2, "along")],
-    "F3": [("g", 3, "along"), ("g", 2, "finish")],
-    "F4": [("g", 3, "finish"), ("g", 4, "across"), ("g", 5, "across"), ("g", 6, "line"), ("g", 7, "line")],
-    "A": [("g", 4, "along"), ("g", 5, "along"), ("g", 4, "finish"), ("g", 6, "across"), ("g", 8, "line"), ("g", 5, "finish")],
-    "T1": [("g", 7, "across"), ("g", 9, "line")],
-    "T4": [("g", 6, "along"), ("g", 8, "across"), ("g", 10, "line")],
-    "T5": [("g", 7, "along"), ("g", 6, "finish")],
-    "T6": [("g", 9, "across"), ("g", 11, "line"), ("r", 0, "core"), ("g", 7, "finish")],
-    "T7": [("r", 1, "core"), ("g", 8, "along"), ("g", 10, "across")],
-    "T9": [("g", 8, "finish"), ("g", 9, "along")],
-    "T11": [("g", 9, "finish"), ("g", 11, "across")],
-    "T16": [("r", 0, "across"), ("r", 1, "across"), ("r", 2, "core"), ("r", 3, "core"), ("g", 10, "along"), ("g", 11, "along")],
-    "T18": [("g", 10, "finish"), ("g", 11, "finish")],
-    "T19": [("r", 0, "along"), ("r", 1, "along")],
-    "T23": [("r", 2, "across"), ("r", 3, "across"), ("r", 4, "core"), ("r", 5, "core"), ("r", 0, "finish")],
-    "T26": [("r", 2, "along"), ("r", 1, "finish")],
-    "T27": [("r", 3, "along")],
-    "B2": [("r", 2, "finish"), ("r", 4, "across"), ("r", 5, "across"), ("r", 6, "core"), ("r", 7, "core")],
-    "B4": [("r", 8, "start")],
-    "K0": [("r", 4, "along")],
-    "K1": [("r", 3, "finish"), ("r", 5, "along")],
-    "K2": [("r", 4, "finish"), ("r", 6, "across"), ("r", 7, "across"), ("r", 8, "core"), ("r", 9, "core")],
-    "K4": [("r", 5, "finish"), ("r", 6, "along"), ("r", 7, "along")],
-    "K5": [("r", 8, "across"), ("r", 9, "across"), ("r", 10, "core")],
-    "L0": [("r", 6, "finish")],
-    "L1": [("r", 8, "along"), ("r", 11, "core")],
-    "E": [("r", 7, "finish"), ("r", 9, "along"), ("r", 10, "across"), ("r", 8, "finish"), ("r", 11, "across"), ("r", 9, "finish"), ("r", 10, "along"), ("r", 11, "along"), ("r", 10, "finish"), ("r", 11, "finish")],
+    "S1": [("g", 1, "line"), ("g", 2, "line"), ("g", 0, "across")],
+    "S2": [("g", 3, "line"), ("g", 1, "across"), ("g", 2, "across"), ("g", 0, "along")],
+    "S3": [("g", 5, "line")],
 }
 
 
@@ -153,35 +171,49 @@
 
 
 class Gather(Transfers):
-    SLOTS = 10
-
-    def __init__(self, full, send_sems, recv_sems, order, digits, device):
+    SLOTS = 11
+
+    def __init__(self, full, send_sems, recv_sems, digits, device):
         super().__init__(send_sems, recv_sems, digits, device)
         self.full = full
-        self.first, self.second = order
-
-    def line_of(self, *flipped):
+
+    def line_of(self, *flipped, z=slice(None)):
         d = {**self.digits, **self.flip(*flipped)}
-        return self.full.at[:, d["y"], d["x"], d["c"]]
+        return self.full.at[z, d["y"], d["x"], d["c"]]
 
     def block_of(self, z):
-        d = self.digits
-        return self.full.at[z, d["y"], d["x"], d["c"]]
+        return self.line_of(z=z)
 
     def spec(self, slot):
-        z, a, b = self.digits["z"], self.first, self.second
+        z = self.digits["z"]
         if slot < 3:
             own = self.block_of(z)
             return own, own, self.device(z=(z + slot + 1) % 4)
-        flipped, towards = ((), (), (), (a,), (a,), (b,), (b, a))[slot - 3], (a, b, "c", b, "c", "c", "c")[slot - 3]
-        line = self.line_of(*flipped)
-        return line, line, self.device(**self.flip(towards))
+        held, towards = (
+            (self.line_of(), "x"),
+            (self.line_of(), "y"),
+            (self.line_of(), "c"),
+            (self.line_of("x", z=LOW), "y"),
+            (self.line_of("y", z=HIGH), "x"),
+            (self.line_of("x"), "c"),
+            (self.line_of("y"), "c"),
+            (self.line_of("x", "y"), "c"),
+        )[slot - 3]
+        return held, held, self.device(**self.flip(towards))
 
     def landing(self, slot):
-        a, b = self.first, self.second
         if slot < 3:
             return self.block_of((self.digits["z"] + 3 - slot) % 4)
-        return self.line_of(*((a,), (b,), ("c",), (b, a), ("c", a), ("c", b), ("c", b, a))[slot - 3])
+        return (
+            self.line_of("x"),
+            self.line_of("y"),
+            self.line_of("c"),
+            self.line_of("x", "y", z=LOW),
+            self.line_of("x", "y", z=HIGH),
+            self.line_of("c", "x"),
+            self.line_of("c", "y"),
+            self.line_of("c", "x", "y"),
+        )[slot - 3]
 
     def start(self):
         self.go(0, 1, 2)
@@ -192,22 +224,22 @@
 
     def across(self):
         self.arrived(3)
-        self.go(6, 7)
+        self.go(6, 8)
+        self.arrived(4)
+        self.go(7, 9)
 
     def along(self):
-        self.arrived(4)
-        self.go(8)
-        self.arrived(6)
-        self.go(9)
+        self.arrived(6, 7)
+        self.go(10)
 
     def finish(self):
-        self.arrived(5, 7, 8, 9)
+        self.arrived(5, 8, 9, 10)
         self.sent(self.SLOTS)
 
 
 class PlaneGather(Gather):
-    def __init__(self, full, send_sems, recv_sems, order, digits, device, plane):
-        super().__init__(full, send_sems, recv_sems, order, digits, device)
+    def __init__(self, full, send_sems, recv_sems, digits, device, plane):
+        super().__init__(full, send_sems, recv_sems, digits, device)
         self.plane = plane
 
     def spec(self, slot):
@@ -243,43 +275,48 @@
 
 
 class Reduce(Transfers):
-    SLOTS = 7
-
-    def __init__(self, parts, received, send_sems, recv_sems, order, digits, device, credits=None, grants=None):
+    SLOTS = 11
+
+    def __init__(self, parts, received, send_sems, recv_sems, digits, device, credits=None, grants=None):
         super().__init__(send_sems, recv_sems, digits, device)
         self.parts = parts
         self.from_core, self.from_first, self.from_second, self.from_line = received
-        self.first, self.second = order
         self.credits, self.grants = credits, grants
 
-    def half(self, first, c):
-        if self.first == "y":
-            return self.parts.at[:, first, :, c]
-        return self.parts.at[:, :, first, c]
-
-    def at(self, z, first, second):
-        d = {self.first: first, self.second: second}
-        return (z, d["y"], d["x"], self.digits["c"])
+    def side(self, high, far, c=None):
+        d = self.digits
+        c = d["c"] if c is None else c
+        if high:
+            return (HIGH, 1 - d["y"] if far else d["y"], slice(None), c)
+        return (LOW, slice(None), 1 - d["x"] if far else d["x"], c)
+
+    def pair(self, high, far):
+        d = self.digits
+        if high:
+            return (HIGH, d["y"], 1 - d["x"] if far else d["x"], d["c"])
+        return (LOW, 1 - d["y"] if far else d["y"], d["x"], d["c"])
 
     def spec(self, slot):
-        d, a, b = self.digits, self.first, self.second
-        if slot < 2:
-            side = (1 - d[a], d[a])[slot]
-            return self.half(side, 1 - d["c"]), self.from_core.at[slot], self.device(**self.flip("c"))
-        if slot == 2:
-            return self.half(1 - d[a], d["c"]), self.from_first, self.device(**self.flip(a))
-        if slot == 3:
-            q = {**d, **self.flip(b)}
-            return self.parts.at[:, q["y"], q["x"], d["c"]], self.from_second, self.device(**self.flip(b))
-        z = (d["z"] + slot - 3) % 4
-        return self.parts.at[z, d["y"], d["x"], d["c"]], self.from_line.at[slot - 4], self.device(z=z)
+        d = self.digits
+        if slot < 4:
+            high, near = slot % 2, slot // 2
+            source = self.parts.at[self.side(high, not near, 1 - d["c"])]
+            return source, self.from_core.at[near, high], self.device(**self.flip("c"))
+        if slot < 6:
+            high = slot - 4
+            return self.parts.at[self.side(high, True)], self.from_first.at[high], self.device(**self.flip("xy"[high]))
+        if slot < 8:
+            high = slot - 6
+            return self.parts.at[self.pair(high, True)], self.from_second.at[high], self.device(**self.flip("yx"[high]))
+        z = (d["z"] + slot - 7) % 4
+        return self.parts.at[z, d["y"], d["x"], d["c"]], self.from_line.at[slot - 8], self.device(z=z)
 
     def landing(self, slot):
-        if slot < 2:
-            return self.from_core.at[slot]
         if slot < 4:
-            return (self.from_first, self.from_second)[slot - 2]
-        return self.from_line.at[slot - 4]
+            return self.from_core.at[slot // 2, slot % 2]
+        if slot < 8:
+            return (self.from_first, self.from_second)[(slot - 4) // 2].at[slot % 2]
+        return self.from_line.at[slot - 8]
 
     def spend(self, *kinds):
         if self.credits is not None:
@@ -289,65 +326,66 @@
     def grant(self):
         d = self.digits
         if self.grants is not None:
-            others = [self.device(**self.flip(axis)) for axis in ("c", self.first, self.second)]
+            others = [self.device(**self.flip(axis)) for axis in "cxy"]
             others += [self.device(z=(d["z"] + 4 - step) % 4) for step in (1, 2, 3)]
             for kind, other in enumerate(others):
                 pl.semaphore_signal(self.grants.at[kind], inc=1, device_id=other, device_id_type=MESH_ID)
 
-    def add(self, first, second, received):
-        d = {self.first: first, self.second: slice(None) if second is None else second}
-        index = (slice(None), d["y"], d["x"], self.digits["c"])
+    def add(self, index, received):
         self.parts[index] = self.parts[index] + received
 
     def start(self):
         self.spend(0)
-        self.go(0, 1)
+        self.go(0, 1, 2, 3)
 
     def core(self):
-        d, a = self.digits, self.first
-        self.arrived(0)
-        self.add(1 - d[a], None, self.from_core[0])
-        self.spend(1)
-        self.go(2)
-        self.arrived(1)
-        self.add(d[a], None, self.from_core[1])
+        self.spend(1, 2)
+        for high in (0, 1):
+            self.arrived(high)
+            self.add(self.side(high, True), self.from_core[0, high])
+            self.go(4 + high)
+        for high in (0, 1):
+            self.arrived(2 + high)
+            self.add(self.side(high, False), self.from_core[1, high])
 
     def across(self):
-        d, a, b = self.digits, self.first, self.second
-        self.arrived(2)
-        self.add(d[a], 1 - d[b], self.from_first[:, 1 - d[b]])
-        self.spend(2)
-        self.go(3)
-        self.add(d[a], d[b], self.from_first[:, d[b]])
+        d = self.digits
+        for high, other in ((0, "y"), (1, "x")):
+            self.arrived(4 + high)
+            self.add(self.pair(high, True), self.from_first[high, :, 1 - d[other]])
+            self.go(6 + high)
+        for high, other in ((0, "y"), (1, "x")):
+            self.add(self.pair(high, False), self.from_first[high, :, d[other]])
+
+    def collect(self):
+        for high in (0, 1):
+            self.arrived(6 + high)
+            self.add(self.pair(high, False), self.from_second[high])
+        self.spend(3, 4, 5)
 
     def along(self):
-        d, a, b = self.digits, self.first, self.second
-        self.arrived(3)
-        self.add(d[a], d[b], self.from_second[...])
-        self.spend(3, 4, 5)
-        self.go(4, 5, 6)
+        self.collect()
+        self.go(8, 9, 10)
 
     def finish(self, store):
         d = self.digits
         total = self.parts[d["z"], d["y"], d["x"], d["c"]].astype(f32)
-        for slot in (4, 5, 6):
+        for slot in (8, 9, 10):
             self.arrived(slot)
-            total = total + self.from_line[slot - 4].astype(f32)
+            total = total + self.from_line[slot - 8].astype(f32)
         store(total)
         self.sent(self.SLOTS)
         self.grant()
 
 
 class PlaneReduce(Reduce):
-    def __init__(self, parts, received, plane_in, send_sems, recv_sems, order, digits, device, credits, grants, plane):
-        super().__init__(parts, received, send_sems, recv_sems, order, digits, device, credits, grants)
+    def __init__(self, parts, received, plane_in, send_sems, recv_sems, digits, device, credits, grants, plane):
+        super().__init__(parts, received, send_sems, recv_sems, digits, device, credits, grants)
         self.plane_in, self.plane = plane_in, plane
 
     def along(self):
-        d, a, b = self.digits, self.first, self.second
-        self.arrived(3)
-        self.add(d[a], d[b], self.from_second[...])
-        self.spend(3, 4, 5)
+        d = self.digits
+        self.collect()
         for step in (1, 2, 3):
 
             @pl.when(d["z"] == (self.plane + step) % 4)
@@ -359,8 +397,8 @@
         return pltpu.make_async_remote_copy(
             src_ref=self.parts.at[:, d["y"], d["x"], d["c"]],
             dst_ref=self.plane_in.at[step - 1],
-            send_sem=self.send_sems.at[3 + step],
-            recv_sem=self.recv_sems.at[3 + step],
+            send_sem=self.send_sems.at[7 + step],
+            recv_sem=self.recv_sems.at[7 + step],
             device_id=self.device(z=self.plane),
             device_id_type=MESH_ID,
         )
@@ -372,7 +410,7 @@
         def _():
             total = self.parts[:, d["y"], d["x"], d["c"]].astype(f32)
             for step in (1, 2, 3):
-                self.arrived_at(3 + step, self.plane_in.at[step - 1])
+                self.arrived_at(7 + step, self.plane_in.at[step - 1])
                 total = total + self.plane_in[step - 1].astype(f32)
             store(total)
 
@@ -382,7 +420,7 @@
             def _(step=step):
                 self.to_plane(step).wait_send()
 
-        for slot in range(4):
+        for slot in range(8):
             self.copy(slot).wait_send()
         self.grant()
 
@@ -676,18 +714,17 @@
     load_cot = pltpu.make_async_copy(cot_hbm, cot, local_sems.at[1])
     load_cot.start()
 
-    orders = ("xy", "yx")
-    gain_gather = Gather(gains, gain_send, gain_recv, "xy", digits, device)
+    gain_gather = Gather(gains, gain_send, gain_recv, digits, device)
     gathers = []
     for i in range(PIECES):
-        common = (pieces.at[i], gather_send.at[i], gather_recv.at[i], orders[i % 2], digits, device)
+        common = (pieces.at[i], gather_send.at[i], gather_recv.at[i], digits, device)
         gathers.append(PlaneGather(*common, FFN_PIECES.index(i)) if i in FFN_PIECES else Gather(*common))
     order = [i for t in range(TILES) for i in (IN_PIECES[t], FFN_PIECES[t])] + [OUT_PIECE, 0, 1, 2]
     reduces = []
     for n, i in enumerate(order):
         slot = n % LANDINGS
         received = (from_core.at[slot], from_first.at[slot], from_second.at[slot], from_line.at[slot])
-        sems = (reduce_send.at[n], reduce_recv.at[n], orders[n % 2], digits, device)
+        sems = (reduce_send.at[n], reduce_recv.at[n], digits, device)
         limits = (credits.at[slot] if n >= LANDINGS else None, credits.at[slot] if n + LANDINGS < PIECES else None)
         if i in FFN_PIECES:
             reduces.append(PlaneReduce(pieces.at[i], received, plane_in, *sems, *limits, FFN_PIECES.index(i)))
@@ -779,10 +816,11 @@
     lax.fori_loop(0, count // 256, norm_one, 0)
     run([stage(*entry) for entry in PLAN["S"]])
 
-    forward_plan = plan("F")
+    forward_plan, project_plan = plan("F"), plan("P")
 
     def forward_group(g, carry):
         qkv[g] = nn(normed[...], weights[GROUP_PIECE + g]).astype(bf16)
+        run_at(g, project_plan)
 
         def forward(pair, carry):
             attend(qkv.at[g], key_marks, query_marks, strips, mix, lse, g, pair)
@@ -893,7 +931,7 @@
     for z in range(4):
         pack_piece(pieces.at[OUT_PIECE], z, grad[192 * z : 192 * (z + 1)])
     run(before_plan.get(4, []))
-    back_plan = plan("K")
+    back_plan, group_plan = plan("K"), plan("G")
 
     def back_group(g, carry):
         def back(pair, carry):
@@ -906,6 +944,7 @@
         for z in range(4):
             pack_piece(pieces.at[GROUP_PIECE + g], z, grad[192 * z : 192 * (z + 1)])
         run_at(g, {k: [reduces[9 + k].start] for k in range(GROUPS)})
+        run_at(g, group_plan)
         return carry
 
     lax.fori_loop(0, GROUPS, back_group, 0)
@@ -933,8 +972,9 @@
     tail = [stage(*entry) for entry in PLAN["E"]]
     for slot in range(4):
         sums.start(slot)
-        if tail:
-            tail.pop(0)()
+        share = -(-len(tail) // (4 - slot))
+        run(tail[:share])
+        tail = tail[share:]
         sums.finish(slot)
     for target, row in ((grad_one, 0), (grad_two, 6)):
         line = jnp.concatenate([small[row + j : row + j + 1, :] for j in range(D // 128)], axis=1)
@@ -1023,9 +1063,9 @@
             pltpu.VMEM((count // SEQ, 16, SEQ), f32),
             pltpu.VMEM((H, 2, 8, 128), f32),
             pltpu.VMEM((32, 128), f32),
-            pltpu.VMEM((LANDINGS, 2, 4, 2, ROWS, COLS), bf16),
-            pltpu.VMEM((LANDINGS, 4, 2, ROWS, COLS), bf16),
-            pltpu.VMEM((LANDINGS, 4, ROWS, COLS), bf16),
+            pltpu.VMEM((LANDINGS, 2, 2, 2, 2, ROWS, COLS), bf16),
+            pltpu.VMEM((LANDINGS, 2, 2, 2, ROWS, COLS), bf16),
+            pltpu.VMEM((LANDINGS, 2, 2, ROWS, COLS), bf16),
             pltpu.VMEM((LANDINGS, 3, ROWS, COLS), bf16),
             pltpu.VMEM((3, 4, ROWS, COLS), bf16),
             pltpu.VMEM((10, 32, 128), f32),

time: 178 us -> 169 us (0.949)
  Pallas kernels: 177 us -> 168 us
    pallas_call x1, Pallas kernels: 173 us -> 163 us  [per_device(): pl.pallas_call(layer_kernel, out_shape=shapes, in_specs=[any_space] * 2 +...]
where the time goes in v6:
time: 169 us
  Pallas kernels  168 us (99%)
    pallas_call x1, Pallas kernels, per_device(): pl.pallas_call(layer_kernel, out_shape=shapes, in_specs=[any_space] * 2 +...  163 us
    pallas_call x1, Pallas kernels, per_device(): pl.pallas_call(deliver_kernel, out_shape=shapes, in_specs=[any_space] * l...  4.51 us

profile of v6, /device:TPU:0, one launch (start us, length us, event | category | flops | bytes accessed | tf_op | source)
XLA Modules:
  0.0 168.8 jit_solution(4071131597513225643)
XLA Ops:
  0.6 163.4 %shard_map.203 = (bf16[1024,768]{1,0:T(8,128)(2,1)}, f32[1024,768]{1,0:T(8,128)}, f32[1,24]{1,0:T(1,128)}, f32[1,24]{1,0:T(1,128)}, f32[12,32]{1,0:T(8,128)}, /*...) custom-call(bf16[1024,768]{1,0:T(8,128)(2,1)} %tokens_hbm.1, ...), custom_call_target="tpu_custom_call" | custom-call | tf_op jit(solution)/shard_map/pallas_call | solution.py:1038
  164.1 4.5 %shard_map.204 = (bf16[1024,768]{1,0:T(8,128)(2,1)}, f32[1024,768]{1,0:T(8,128)}, f32[1,24]{1,0:T(1,128)}, f32[1,24]{1,0:T(1,128)}, f32[12,32]{1,0:T(8,128)}, /*...) custom-call(bf16[1024,768]{1,0:T(8,128)(2,1)} %get-tuple-element.33., ...), custom_call_target="tpu_custom_call" | custom-call | tf_op jit(solution)/shard_map/pallas_call | solution.py:1098

commit v7 on v6

--- a/solution.py
+++ b/solution.py
@@ -75,7 +75,7 @@
     "K4": [("r", 9, "across"), ("r", 10, "core")],
     "G2": [("r", 8, "finish"), ("r", 9, "along")],
     "L0": [("r", 7, "finish"), ("r", 10, "across"), ("r", 11, "core")],
-    "E": [("r", 9, "finish"), ("r", 10, "along"), ("r", 11, "across"), ("r", 10, "finish"), ("r", 11, "along"), ("r", 11, "finish")],
+    "E": [("r", 11, "across"), ("r", 10, "along"), ("r", 9, "finish"), ("r", 11, "along"), ("r", 10, "finish"), ("r", 11, "finish")],
     "S0": [("g", 0, "line")],
     "S1": [("g", 1, "line"), ("g", 2, "line"), ("g", 0, "across")],
     "S2": [("g", 3, "line"), ("g", 1, "across"), ("g", 2, "across"), ("g", 0, "along")],

time: 169 us -> 170 us (level)
  no operation moved by 1% of the time
where the time goes in v7:
time: 170 us; the launch traced here: 169 us
  Pallas kernels  169 us (99%)
    pallas_call x1, Pallas kernels, per_device(): pl.pallas_call(layer_kernel, out_shape=shapes, in_specs=[any_space] * 2 +...  164 us
    pallas_call x1, Pallas kernels, per_device(): pl.pallas_call(deliver_kernel, out_shape=shapes, in_specs=[any_space] * l...  4.51 us

profile of v7, /device:TPU:0, one launch (start us, length us, event | category | flops | bytes accessed | tf_op | source)
XLA Modules:
  0.0 169.4 jit_solution(1406456403644550644)
XLA Ops:
  0.6 164.1 %shard_map.203 = (bf16[1024,768]{1,0:T(8,128)(2,1)}, f32[1024,768]{1,0:T(8,128)}, f32[1,24]{1,0:T(1,128)}, f32[1,24]{1,0:T(1,128)}, f32[12,32]{1,0:T(8,128)}, /*...) custom-call(bf16[1024,768]{1,0:T(8,128)(2,1)} %tokens_hbm.1, ...), custom_call_target="tpu_custom_call" | custom-call | tf_op jit(solution)/shard_map/pallas_call | solution.py:1038
  164.7 4.5 %shard_map.204 = (bf16[1024,768]{1,0:T(8,128)(2,1)}, f32[1024,768]{1,0:T(8,128)}, f32[1,24]{1,0:T(1,128)}, f32[1,24]{1,0:T(1,128)}, f32[12,32]{1,0:T(8,128)}, /*...) custom-call(bf16[1024,768]{1,0:T(8,128)(2,1)} %get-tuple-element.33., ...), custom_call_target="tpu_custom_call" | custom-call | tf_op jit(solution)/shard_map/pallas_call | solution.py:1098
